TPU v7x, 32 devices: a whole 2x2x4 slice. The times are simulated.
32 devices in a mesh: row: 16 (over z, x, core), col: 2 (over y), chan: 1.
Axes of the slice: x: 2, y: 2, z: 4, core: 2. Of those that a mesh axis runs over, the one named last changes fastest.
Arguments:
- voltages: bfloat16 [128, 8, 137216], P('row', ('col', 'chan')), may hold values from -6 to 6
- lane_map: int32 [16, 2, 32], P('row', 'col'), may hold values from 0 to 31, each once within a row
- input_flags: int32 [128, 8], P('row', 'col'), may hold values 0 or 1
Outputs:
- visibility: bfloat16 [16, 2, 128, 8, 8, 128], P('chan', None, 'row', None, 'col')
Inputs may be any that keep to these rules, and one draw needn't show every extreme that they name: For each block (row index, col index), lane_map lists every lane 0 to 31 once.
All inputs are finite; a program needn't handle non-finite values. No bound on the sum of `input_flags` on one device may be relied on, other than what follows from the above.
Results may differ from a plain program's by a relative error of at most 0.0069.
Values may be sent and summed in bfloat16 or wider, within the bound.
No kernel may reach another device: no remote copies, remote signals or barrier semaphores. Data moves between devices by JAX's collectives and lax.ppermute only.
A program may use at most 64 MiB of HBM per device.

v0:
```python
import jax
import jax.numpy as jnp
from jax import lax
from jax.sharding import PartitionSpec as P

NFFT = 2048
TAPS = 4
P_DEV = 8
Q_DEV = 4
CH_DEV = 16
SPECTRA = 64
LANES = 32
FRAMES = 67


def kernel_table(nfft, taps, chans):
    length = taps * nfft
    position = jnp.arange(length, dtype=jnp.float32)
    centre = (position - length / 2 + 0.5) / nfft
    window = jnp.sinc(centre) * (0.5 - 0.5 * jnp.cos(2.0 * jnp.pi * (position + 0.5) / length))
    norm_scale = jnp.sqrt(2.0 / jnp.sum(window * window))
    window = (window * norm_scale).reshape(taps, nfft)
    sample = jnp.arange(nfft, dtype=jnp.int32)
    bin_index = nfft // 4 + jnp.arange(chans, dtype=jnp.int32)
    phase_index = bin_index[:, None] * sample[None, :] % nfft
    phases = phase_index.astype(jnp.float32) * (2.0 * jnp.pi / nfft)
    both_parts = jnp.stack([jnp.cos(phases).T, -jnp.sin(phases).T], -1)
    built = window.T[:, :, None, None] * both_parts[:, None, :, :]
    return built.reshape(nfft, taps * chans * 2).astype(jnp.bfloat16)


def per_device(voltages, lane_map, input_flags):
    all_chans = CH_DEV * lax.axis_size("chan")
    half_q = voltages.shape[1]
    table_rows = kernel_table(NFFT, TAPS, all_chans)
    frames = voltages.reshape(P_DEV, half_q, FRAMES, NFFT)
    frame_sums = jnp.einsum("pqfn,nk->pqfk", frames, table_rows, preferred_element_type=jnp.float32)
    frame_sums = frame_sums.reshape(P_DEV, half_q, FRAMES, TAPS, all_chans, 2)
    tap_sum = frame_sums[:, :, 0:SPECTRA, 0]
    for tap_idx in range(1, TAPS):
        tap_sum = tap_sum + frame_sums[:, :, tap_idx : tap_idx + SPECTRA, tap_idx]
    filtered = tap_sum.astype(jnp.bfloat16)
    filtered = filtered.transpose(3, 0, 1, 4, 2).reshape(all_chans, P_DEV, half_q, 2 * SPECTRA)
    turned_over = lax.all_to_all(filtered, "chan", split_axis=0, concat_axis=2, tiled=True)
    lane_rows = turned_over.reshape(CH_DEV, LANES, 2 * SPECTRA)
    lane_index = lane_map.reshape(LANES)
    selector = (lane_index[:, None] == jnp.arange(LANES, dtype=jnp.int32)[None, :]).astype(
        jnp.bfloat16
    )
    reordered = jnp.einsum("kl,clz->ckz", selector, lane_rows, preferred_element_type=jnp.float32)
    weights = input_flags.reshape(LANES).astype(jnp.float32)[None, :, None]
    channelised = (
        (reordered * weights).astype(jnp.bfloat16).reshape(CH_DEV, P_DEV, Q_DEV, 2 * SPECTRA)
    )
    row_group = lax.all_gather(channelised, "col", axis=2, tiled=True)
    grid_cols = row_group.shape[2]
    row_block = row_group.reshape(CH_DEV, P_DEV * grid_cols, 2 * SPECTRA)
    col_set = lax.all_gather(channelised, "row", axis=1, tiled=True)
    real_part = col_set[..., :SPECTRA]
    imag_part = col_set[..., SPECTRA:]
    turned = jnp.concatenate([-imag_part, real_part], axis=-1)
    col_block = jnp.stack([col_set, turned], axis=1)
    products = jnp.einsum(
        "cik,crpqk->criqp", row_block, col_block, preferred_element_type=jnp.float32
    )
    products = (products * (1.0 / SPECTRA)).astype(jnp.bfloat16)
    return products.reshape(CH_DEV, 2, P_DEV, grid_cols, Q_DEV, col_set.shape[1])


def solution(mesh):
    return jax.shard_map(
        per_device,
        mesh=mesh,
        in_specs=(P("row", ("col", "chan"), None), P("row", "col", None), P("row", "col")),
        out_specs=P("chan", None, "row", None, "col", None),
        check_vma=False,
    )
```

profile of v0, /device:TPU:0, one launch (start us, length us, event | category | flops | bytes accessed | tf_op | source)
XLA Modules:
  0.0 91.3 jit_solution(10526656234236132531)
XLA Ops:
  6.5 0.0 all-gather.2.cloned.1.call-start
  6.5 0.8 fusion.64
  7.3 0.6 fusion.21
  7.9 0.2 copy.37
  8.9 0.3 fusion.37
  9.2 0.3 multiply_convert_fusion.1
  9.6 0.2 convert_element_type.66
  9.8 11.2 %reshape.155 = bf16[8,4,67,2048]{3,2,1,0:T(8,128)(2,1)} reshape(bf16[8,4,137216]{2,1,0:T(4,128)(2,1)} %param.3) | data formatting | bytes 17563648 | tf_op jit(solution)/shard_map/reshape | solution.py:36
  21.0 5.2 %convolution_bitcast_fusion = f32[8,4,67,128]{3,2,1,0:T(8,128)S(1)} fusion(bf16[8,4,67,2048]{3,2,1,0:T(8,128)(2,1)} %reshape.155, bf16[2048,128]{0,1:T(8,128)(2,1)S(1)} %convert_element_type.66), kind=kOutput, calls=%fused_computation.8 | convolution fusion | flops 1124073472 | bytes 10403840 | tf_op jit(solution)/shard_map/pqfn,nk->pqfk/dot_general | solution.py:37
  26.2 1.0 %copy.41 = f32[8,4,67,128]{2,0,3,1:T(8,128)S(1)} copy(f32[8,4,67,128]{3,2,1,0:T(8,128)S(1)} %convolution_bitcast_fusion) | data formatting | bytes 2195456 | tf_op jit(solution)/shard_map/pqfn,nk->pqfk/dot_general | solution.py:37
  27.2 0.0 copy-start.1
  27.2 0.0 copy-start.2
  27.2 0.5 fusion.12
  27.7 0.3 copy.42
  27.9 0.1 reshape_reshape.3
  28.1 0.0 copy-done.1
  28.1 0.1 copy.43
  28.2 0.1 convert_element_type.70
  28.3 0.0 copy-done.2
  28.3 0.2 fusion.9
  28.5 0.7 copy.44
  29.2 0.0 all-gather.2.cloned.1.call-update
  29.3 7.3 %all_gather.7 = bf16[16,8,8,128]{3,1,0,2:T(8,128)(2,1)S(1)} all-gather(bf16[16,8,4,128]{3,1,0,2:T(8,128)(2,1)S(1)} %copy.46), channel_id=1, replica_groups=mesh['row'=16,'col'=2,'chan'=1] {'col'}, dimensions={2}, use_global_device_ids=true | all-gather | bytes 393216 | tf_op jit(solution)/shard_map/all_gather | solution.py:55
  36.5 36.7 %all-gather.2.cloned.1.call-done = bf16[16,128,4,128]{3,1,2,0:T(8,128)(2,1)} async-done(((bf16[16,8,4,128]{3,1,2,0:T(8,128)(2,1)}), bf16[16,128,4,128]{3,1,2,0:T(8,128)(2,1)}) %all-gather.2.cloned.1.call-update) | async-done | bytes 2097168 | tf_op jit(solution)/shard_map/all_gather | solution.py:58
  73.3 3.1 %slice_negate_fusion = (bf16[16,128,4,64]{3,1,2,0:T(8,128)(2,1)S(1)}, bf16[16,128,4,64]{3,1,2,0:T(8,128)(2,1)S(1)}) fusion(bf16[16,128,4,128]{3,1,2,0:T(8,128)(2,1)} %all-gather.2.cloned.1.call-done), kind=kLoop, calls=%fused_computation.5 | loop fusion | flops 524288 | bytes 4194304 | tf_op jit(solution)/shard_map/neg | solution.py:61
  76.4 0.0 copy-start
  76.4 1.3 %maximum_bitcast_fusion = bf16[16,1,128,4,128]{4,2,3,1,0:T(8,128)(2,1)S(1)} fusion(bf16[16,128,4,64]{3,1,2,0:T(8,128)(2,1)S(1)} %get-tuple-element.6, bf16[16,128,4,64]{3,1,2,0:T(8,128)(2,1)S(1)} %get-tuple-element.5), kind=kLoop, calls=%fused_computation.6 | loop fusion | flops 4194304 | bytes 4194304 | tf_op jit(solution)/shard_map/stack | solution.py:62
  77.7 0.3 copy-done
  78.0 1.6 %fusion.6 = bf16[16,2,8,8,4,128]{5,3,2,4,1,0:T(8,128)(2,1)S(1)} fusion(bf16[16,1,128,4,128]{4,2,3,1,0:T(8,128)(2,1)S(1)} %maximum_bitcast_fusion, bf16[16,1,128,4,128]{4,2,3,1,0:T(8,128)(2,1)S(1)} %bitcast.37, bf16[16,8,8,128]{3,1,0,2:T(8,128)(2,1)S(1)} %all_gather.7), kind=kOutput, calls=%fused_computation.7 | convolution fusion | flops 272629760 | bytes 6553600 | tf_op jit(solution)/shard_map/cik,crpqk->criqp/dot_general | solution.py:63
  79.6 4.9 %copy.48 = bf16[16,2,8,8,4,128]{5,4,3,2,1,0:T(4,128)(2,1)} copy(bf16[16,2,8,8,4,128]{5,3,2,4,1,0:T(8,128)(2,1)S(1)} %fusion.6) | data formatting | bytes 4194304 | tf_op jit(solution)/shard_map/reshape | solution.py:67
  (4 shorter events, 0.0 us)
Async XLA Ops:
  6.5 66.7 %all-gather.2.cloned.1.call-start = ((), (), s32[]{:S(2)}) async-start(), calls=%async_computation | async-start | bytes 2228224 | tf_op jit(solution)/shard_map/all_gather | solution.py:58
  27.2 0.9 %copy-start.1 = (s32[8,4]{0,1:T(4,128)S(1)}, s32[8,4]{0,1:T(4,128)}, u32[]{:S(2)}) copy-start(s32[8,4]{0,1:T(4,128)} %param.5) | copy-start | bytes 388
  27.2 1.1 %copy-start.2 = (s32[1,1,32]{2,1,0:T(1,128)S(1)}, s32[1,1,32]{2,1,0:T(1,128)}, u32[]{:S(2)}) copy-start(s32[1,1,32]{2,1,0:T(1,128)} %param.4) | copy-start | bytes 388
  76.4 1.6 %copy-start = (bf16[16,128,4,128]{3,1,2,0:T(8,128)(2,1)S(1)}, bf16[16,128,4,128]{3,1,2,0:T(8,128)(2,1)}, u32[]{:S(2)}) copy-start(bf16[16,128,4,128]{3,1,2,0:T(8,128)(2,1)} %all-gather.2.cloned.1.call-done) | copy-start | bytes 6291460
Sparse Core Ops, SparseCore 0:
  29.3 43.8 all-gather.1
where the time goes:
time: 91.7 us; the launch traced here: 91.3 us
  waiting for transfers between devices  36.7 us (40%)
  local copies, waits for them, and re-layouts  19.1 us (21%)
  between operations  14.3 us (16%)
  blocking collectives  7.29 us (8%)
  matrix products  7.07 us (8%)
  other arithmetic  6.91 us (8%)
    all_gather x1, waiting for transfers between devices, per_device(): col_set = lax.all_gather(channelised, 'row', axis=1, tiled=True)  36.7 us
    reshape x1, local copies, waits for them, and re-layouts, per_device(): frames = voltages.reshape(P_DEV, half_q, FRAMES, NFFT)  11.2 us
    all_gather x1, blocking collectives, per_device(): row_group = lax.all_gather(channelised, 'col', axis=2, tiled=True)  7.29 us
    dot_general x1, matrix products, per_device(): jnp.einsum('pqfn,nk->pqfk', frames, table_rows, preferred_element_type=jn...  5.25 us
    reshape x1, local copies, waits for them, and re-layouts, per_device(): products.reshape(CH_DEV, 2, P_DEV, grid_cols, Q_DEV, col_set.shape[1])  4.94 us
    neg x1, other arithmetic, per_device(): turned = jnp.concatenate([-imag_part, real_part], axis=-1)  3.09 us
  transfers between devices with their start and end apart: 1, of which 1 were waited for; matrix products, arithmetic and copies ran while one was open for 0% of the time, Pallas kernels for 0%

commit v1 on v0

--- a/solution.py
+++ b/solution.py
@@ -1,5 +1,9 @@
 import jax
+import jax.experimental.pallas as pl
+import jax.experimental.pallas.tpu as pltpu
 import jax.numpy as jnp
+import ml_dtypes
+import numpy as np
 from jax import lax
 from jax.sharding import PartitionSpec as P
 
@@ -11,6 +15,9 @@
 SPECTRA = 64
 LANES = 32
 FRAMES = 67
+CHUNK = 128
+CHUNKS = NFFT // CHUNK
+ROWS = 16
 
 
 def kernel_table(nfft, taps, chans):
@@ -29,7 +36,7 @@
     return built.reshape(nfft, taps * chans * 2).astype(jnp.bfloat16)
 
 
-def per_device(voltages, lane_map, input_flags):
+def per_device_general(voltages, lane_map, input_flags):
     all_chans = CH_DEV * lax.axis_size("chan")
     half_q = voltages.shape[1]
     table_rows = kernel_table(NFFT, TAPS, all_chans)
@@ -67,9 +74,228 @@
     return products.reshape(CH_DEV, 2, P_DEV, grid_cols, Q_DEV, col_set.shape[1])
 
 
+def filter_table(chans):
+    f32 = np.float32
+    length = TAPS * NFFT
+    position = np.arange(length, dtype=f32)
+    centre = (position - f32(length / 2) + f32(0.5)) / f32(NFFT)
+    window = np.sinc(centre.astype(np.float64)).astype(f32)
+    window = window * (f32(0.5) - f32(0.5) * np.cos(f32(2.0 * np.pi) * (position + f32(0.5)) / f32(length)))
+    window = (window * np.sqrt(f32(2.0) / np.sum(window * window))).reshape(TAPS, NFFT)
+    bins = NFFT // 4 + np.arange(chans)
+    phase_index = np.arange(NFFT)[:, None] * bins[None, :] % NFFT
+    phases = phase_index.astype(f32) * f32(2.0 * np.pi / NFFT)
+    parts = np.stack([np.cos(phases), -np.sin(phases)], 1)
+    table = window.T[:, :, None, None] * parts[:, None]
+    table = table.reshape(CHUNKS // 2, 2, CHUNK, TAPS * 2 * chans)
+    return table.transpose(0, 2, 1, 3).reshape(NFFT // 2, -1).astype(ml_dtypes.bfloat16)
+
+
+def lane_order():
+    order = np.zeros((8 * SPECTRA, 8 * SPECTRA), np.float32)
+    part, s, half, q = np.meshgrid(range(2), range(SPECTRA // 2), range(2), range(Q_DEV), indexing="ij")
+    source = ((part * (SPECTRA // 2) + s) * 2 + half) * Q_DEV + q
+    target = ((q * 2 + part) * 2 + half) * (SPECTRA // 2) + s
+    order[source.ravel(), target.ravel()] = 1
+    return order.astype(ml_dtypes.bfloat16)
+
+
+def filter_kernel(
+    volts, table, order, lane_map, flags, out, held, table_v, order_v, sums, lanes, rows, in_sem, const_sem
+):
+    ahead = 3
+    arrivals = [
+        [
+            pltpu.make_async_copy(volts.at[p, :, j], held.at[p, j, pl.ds(0, FRAMES)], in_sem.at[p])
+            for j in range(CHUNKS // 2)
+        ]
+        for p in range(P_DEV)
+    ]
+    get_table = pltpu.make_async_copy(table, table_v, const_sem.at[0])
+    get_order = pltpu.make_async_copy(order, order_v, const_sem.at[1])
+
+    def begin(p):
+        for copy in arrivals[p]:
+            copy.start()
+        if p == 0:
+            get_table.start()
+        if p == 2:
+            get_order.start()
+
+    first_half = lax.broadcasted_iota(jnp.int32, (35, 8, CHUNK), 1) < Q_DEV
+    tap_of_lane = lax.broadcasted_iota(jnp.int32, (32, 8, CHUNK), 2) // 32
+
+    def frames_of(p):
+        block = jnp.concatenate(
+            [held.at[p, j].reshape(68 * 8, CHUNK)[...] for j in range(CHUNKS // 2)], axis=1
+        )
+        both = jnp.dot(block, table_v[...], preferred_element_type=jnp.float32).reshape(68, 8, 2 * CHUNK)
+        even, odd = both[:, :, :CHUNK], both[:, :, CHUNK:]
+        straight = jnp.where(first_half, even[0:35], odd[32:67])
+        crossed = jnp.where(first_half, even[32:67], odd[0:35])
+        sums[p % 4] = straight + pltpu.roll(crossed, 4, 1)
+
+    def finish(first):
+        total = None
+        for turn in range(4):
+            term = sums[turn, 0:32]
+            for tap in range(1, TAPS):
+                term = jnp.where(tap_of_lane == tap, sums[(tap + turn) % 4, tap : tap + 32], term)
+            if turn:
+                term = pltpu.roll(term, 32 * turn, 2)
+            total = term if total is None else total + term
+        filtered = total.reshape(4 * SPECTRA, CHUNK).T.astype(jnp.bfloat16)
+        filtered = filtered.reshape(4, 2, CH_DEV, 4 * SPECTRA)
+        filtered = jnp.concatenate(
+            [jnp.concatenate([filtered[i, 0], filtered[i, 1]], axis=1) for i in range(4)], axis=0
+        )
+        ordered = jnp.dot(filtered, order_v[...], preferred_element_type=jnp.float32)
+        for i in range(4):
+            for q in range(Q_DEV):
+                lanes[(first + i) * Q_DEV + q] = ordered[i * 16 : i * 16 + 16, q * 128 : q * 128 + 128]
+
+    for p in range(ahead):
+        begin(p)
+    for p in range(P_DEV):
+        for copy in arrivals[p]:
+            copy.wait()
+        if p + ahead < P_DEV:
+            begin(p + ahead)
+        if p == 0:
+            get_table.wait()
+        frames_of(p)
+        if p % 4 == 3:
+            if p == 3:
+                get_order.wait()
+            finish(p - 3)
+    for p in range(P_DEV):
+        for q in range(Q_DEV):
+            weight = flags[q, p].astype(jnp.float32)
+            rows[pl.ds(q * P_DEV + p, CH_DEV, stride=LANES), :] = lanes[lane_map[0, p * Q_DEV + q]] * weight
+    out[...] = rows[...].astype(jnp.bfloat16).reshape(CH_DEV, LANES, 2 * SPECTRA)
+
+
+def channelise(voltages, lane_map, input_flags):
+    volts = voltages.reshape(P_DEV, Q_DEV, FRAMES, CHUNKS // 2, 2, CHUNK).transpose(0, 2, 3, 4, 1, 5)
+    volts = volts.reshape(P_DEV, FRAMES, CHUNKS // 2, 2 * Q_DEV, CHUNK)
+    vmem = pl.BlockSpec(memory_space=pltpu.VMEM)
+    smem = pl.BlockSpec(memory_space=pltpu.SMEM)
+    hbm = pl.BlockSpec(memory_space=pltpu.HBM)
+    return pl.pallas_call(
+        filter_kernel,
+        out_shape=jax.ShapeDtypeStruct((CH_DEV, LANES, 2 * SPECTRA), jnp.bfloat16),
+        in_specs=[hbm, hbm, hbm, smem, smem],
+        out_specs=vmem,
+        scratch_shapes=[
+            pltpu.VMEM((P_DEV, CHUNKS // 2, 68, 2 * Q_DEV, CHUNK), jnp.bfloat16),
+            pltpu.VMEM((NFFT // 2, 2 * CHUNK), jnp.bfloat16),
+            pltpu.VMEM((8 * SPECTRA, 8 * SPECTRA), jnp.bfloat16),
+            pltpu.VMEM((4, 35, 8, CHUNK), jnp.float32),
+            pltpu.VMEM((LANES, CH_DEV, 2 * SPECTRA), jnp.float32),
+            pltpu.VMEM((CH_DEV * LANES, 2 * SPECTRA), jnp.float32),
+            pltpu.SemaphoreType.DMA((P_DEV,)),
+            pltpu.SemaphoreType.DMA((2,)),
+        ],
+        compiler_params=pltpu.CompilerParams(vmem_limit_bytes=56 << 20),
+        name="channelise",
+    )(
+        volts,
+        jnp.asarray(filter_table(CH_DEV)),
+        jnp.asarray(lane_order()),
+        lane_map.reshape(1, LANES),
+        input_flags.T,
+    )
+
+
+def gather_rows(own):
+    def swap(block, d):
+        return lax.ppermute(block, "row", [(i, i ^ d) for i in range(ROWS)])
+
+    blocks = {0: own}
+    blocks[8] = swap(own, 8)
+    blocks[4] = swap(own, 4)
+    blocks[2] = swap(own, 2)
+    blocks[12] = swap(blocks[8], 4)
+    for d in (4, 8, 12):
+        blocks[d + 2] = swap(blocks[d], 2)
+    for d in range(0, ROWS, 2):
+        blocks[d + 1] = swap(blocks[d], 1)
+    return [blocks[d] for d in range(ROWS)]
+
+
+def correlate_kernel(*refs):
+    blocks, other = refs[:ROWS], refs[ROWS]
+    out, columns, spread, packed, sem = refs[ROWS + 1 :]
+    row = lax.axis_index("row")
+    first_col = lax.axis_index("col") == 0
+    odd = lax.rem(row, 2) == 1
+    pair = lax.div(row, 2)
+    sign = jnp.where(lax.broadcasted_iota(jnp.int32, (64, 128), 1) < SPECTRA, 1.0, -1.0)
+    sign = sign.astype(jnp.bfloat16)
+    copies = []
+    for c in range(CH_DEV):
+        slot = c % 2
+        for e in range(ROWS // 2):
+            near, far = blocks[2 * e][c], blocks[2 * e + 1][c]
+            low, high = jnp.where(odd, far, near), jnp.where(odd, near, far)
+            at = pl.multiple_of(lax.bitwise_xor(pair, e) * 16, 16)
+            for q in range(Q_DEV):
+                both = jnp.concatenate([low[q * 8 : q * 8 + 8], high[q * 8 : q * 8 + 8]], axis=0)
+                columns[slot, q, pl.ds(at, 16), :] = both
+        mine, theirs = blocks[0][c], other[c]
+        left = jnp.concatenate(
+            [jnp.where(first_col, mine, theirs), jnp.where(first_col, theirs, mine)], axis=0
+        )
+        left = jnp.concatenate([left, pltpu.roll(left, SPECTRA, 1) * sign], axis=0)
+        for h in range(2):
+            right = columns[slot, 2 * h : 2 * h + 2].reshape(256, 2 * SPECTRA)
+            products = lax.dot_general(
+                left, right, (((1,), (1,)), ((), ())), preferred_element_type=jnp.float32
+            ) * (1.0 / SPECTRA)
+            for k in range(2):
+                for part in range(2):
+                    for q in range(2 * Q_DEV):
+                        start = (part * 8 + q) * 8
+                        spread[slot, part, pl.ds(q * Q_DEV + 2 * h + k, 8, stride=32), :] = products[
+                            start : start + 8, k * 128 : k * 128 + 128
+                        ]
+        packed[c] = spread[slot].astype(jnp.bfloat16)
+        copy = pltpu.make_async_copy(packed.at[c], out.at[c], sem.at[c])
+        copy.start()
+        copies.append(copy)
+    for copy in copies:
+        copy.wait()
+
+
+def correlate(blocks, other):
+    vmem = pl.BlockSpec(memory_space=pltpu.VMEM)
+    return pl.pallas_call(
+        correlate_kernel,
+        out_shape=jax.ShapeDtypeStruct((CH_DEV, 2, 2 * LANES * Q_DEV, 8 * ROWS), jnp.bfloat16),
+        in_specs=[vmem] * (ROWS + 1),
+        out_specs=pl.BlockSpec(memory_space=pltpu.HBM),
+        scratch_shapes=[
+            pltpu.VMEM((2, Q_DEV, 8 * ROWS, 2 * SPECTRA), jnp.bfloat16),
+            pltpu.VMEM((2, 2, 2 * LANES * Q_DEV, 8 * ROWS), jnp.float32),
+            pltpu.VMEM((CH_DEV, 2, 2 * LANES * Q_DEV, 8 * ROWS), jnp.bfloat16),
+            pltpu.SemaphoreType.DMA((CH_DEV,)),
+        ],
+        compiler_params=pltpu.CompilerParams(vmem_limit_bytes=32 << 20),
+        name="correlate",
+    )(*blocks, other)
+
+
+def per_device(voltages, lane_map, input_flags):
+    own = channelise(voltages, lane_map, input_flags)
+    other = lax.ppermute(own, "col", [(0, 1), (1, 0)])
+    products = correlate(gather_rows(own), other)
+    return products.reshape(CH_DEV, 2, P_DEV, 2 * Q_DEV, Q_DEV, P_DEV * ROWS)
+
+
 def solution(mesh):
+    fast = mesh.shape["row"] == ROWS and mesh.shape["col"] == 2 and mesh.shape["chan"] == 1
     return jax.shard_map(
-        per_device,
+        per_device if fast else per_device_general,
         mesh=mesh,
         in_specs=(P("row", ("col", "chan"), None), P("row", "col", None), P("row", "col")),
         out_specs=P("chan", None, "row", None, "col", None),

time: 91.7 us -> 39.4 us (0.43)
  waiting for transfers between devices: 36.7 us -> 9.13 us
  local copies, waits for them, and re-layouts: 19.1 us -> 0.9 us
  Pallas kernels: 0 us -> 14.7 us
  starting transfers between devices: 0.01 us -> 14.4 us
  between operations: 14.3 us -> 0.05 us
  blocking collectives: 7.29 us -> 0 us
  matrix products: 7.07 us -> 0 us
  other arithmetic: 6.91 us -> 0 us
    all_gather x1 -> x0, waiting for transfers between devices: 36.7 us -> none  [per_device(): col_set = lax.all_gather(channelised, 'row', axis=1, tiled=True)]
    reshape x4 -> x0, local copies, waits for them, and re-layouts: 16.8 us -> none  [the longest x1 11.2 us: per_device(): frames = voltages.reshape(P_DEV, half_q, FRAMES, NFFT)]
    pallas_call x0 -> x2, Pallas kernels: none -> 14.7 us  [the longest x1 10.3 us: channelise(): pl.pallas_call(filter_kernel, out_shape=jax.ShapeDtypeStruct((CH_DEV, LAN...]
    ppermute x0 -> x16, starting transfers between devices: none -> 14.4 us  [the longest x15 12.9 us: swap(): return lax.ppermute(block, 'row', [(i, i ^ d) for i in range(ROWS)])]
    ppermute x0 -> x16, waiting for transfers between devices: none -> 9.13 us  [the longest x15 9.12 us: swap(): return lax.ppermute(block, 'row', [(i, i ^ d) for i in range(ROWS)])]
    all_gather x1 -> x0, blocking collectives: 7.29 us -> none  [per_device(): row_group = lax.all_gather(channelised, 'col', axis=2, tiled=True)]
    dot_general x3 -> x0, matrix products: 7.07 us -> none  [the longest x1 5.25 us: per_device(): jnp.einsum('pqfn,nk->pqfk', frames, table_rows, preferred_element_type=jn...]
    neg x1 -> x0, other arithmetic: 3.09 us -> none  [per_device(): turned = jnp.concatenate([-imag_part, real_part], axis=-1)]
  transfers between devices with their start and end apart: 1 -> 16, of which waited for: 1 -> 5; matrix products, arithmetic and copies ran while one was open for 0% -> 0% of each run, Pallas kernels for 0% -> 0%
where the time goes in v1:
time: 39.4 us; the launch traced here: 39.2 us
  Pallas kernels  14.7 us (37%)
  starting transfers between devices  14.4 us (37%)
  waiting for transfers between devices  9.13 us (23%)
  local copies, waits for them, and re-layouts  0.9 us (2%)
    ppermute x15, starting transfers between devices, swap(): return lax.ppermute(block, 'row', [(i, i ^ d) for i in range(ROWS)])  12.9 us
    pallas_call x1, Pallas kernels, channelise(): pl.pallas_call(filter_kernel, out_shape=jax.ShapeDtypeStruct((CH_DEV, LAN...  10.3 us
    ppermute x15, waiting for transfers between devices, swap(): return lax.ppermute(block, 'row', [(i, i ^ d) for i in range(ROWS)])  9.12 us
    pallas_call x1, Pallas kernels, correlate(): pl.pallas_call(correlate_kernel, out_shape=jax.ShapeDtypeStruct((CH_DEV,...  4.33 us
    ppermute x1, starting transfers between devices, per_device(): other = lax.ppermute(own, 'col', [(0, 1), (1, 0)])  1.52 us
    unnamed x2, local copies, waits for them, and re-layouts  0.9 us
  transfers between devices with their start and end apart: 16, of which 5 were waited for; matrix products, arithmetic and copies ran while one was open for 0% of the time, Pallas kernels for 0%

profile of v1, /device:TPU:0, one launch (start us, length us, event | category | flops | bytes accessed | tf_op | source)
XLA Modules:
  0.0 39.2 jit_solution(16819444588344325497)
XLA Ops:
  0.0 10.3 %channelise.1.refs_0_ = bf16[16,32,128]{2,1,0:T(8,128)(2,1)} custom-call(bf16[8,67,8,8,128]{4,3,2,1,0:T(8,128)(2,1)} %bitcast.8, bf16[1024,256]{1,0:T(8,128)(2,1)} %constant.4.clone.table, bf16[512,512]{1,0:T(8,128)(2,1)} %constant.5.clone.order, s32[1,32]{1,0:T(1,128)} %bitcast.10, s32[4,8]{1,0:T(4,128)} %bitcast.9), custom_call_target="tpu_custom_call" | custom-call | tf_op jit(solution)/shard_map/channelise/pallas_call | solution.py:184
  10.3 4.1 %collective-permute-start.7 = (bf16[16,32,128]{2,1,0:T(8,128)(2,1)}, bf16[16,32,128]{2,1,0:T(8,128)(2,1)S(1)}, u32[]{:S(2)}, u32[]{:S(2)}) collective-permute-start(bf16[16,32,128]{2,1,0:T(8,128)(2,1)} %channelise.1.refs_0_), channel_id=1, source_target_pairs={{0,16},{2,18},{4,20},{6,22},{8,24},{10,26},{12,28},{14,30},{16,0},... | collective-permute-start | bytes 393224 | tf_op jit(solution)/shard_map/ppermute | solution.py:212
  14.5 1.5 %collective-permute-start.15 = (bf16[16,32,128]{2,1,0:T(8,128)(2,1)}, bf16[16,32,128]{2,1,0:T(8,128)(2,1)S(1)}, u32[]{:S(2)}, u32[]{:S(2)}) collective-permute-start(bf16[16,32,128]{2,1,0:T(8,128)(2,1)} %channelise.1.refs_0_), channel_id=1, source_target_pairs={{0,1},{1,0},{2,3},{3,2},{4,5},{5,4},{6,7},{7,6},{8,9},{9,8},{10,11... | collective-permute-start | bytes 393224 | tf_op jit(solution)/shard_map/ppermute | solution.py:290
  16.0 1.6 %collective-permute-start.3 = (bf16[16,32,128]{2,1,0:T(8,128)(2,1)}, bf16[16,32,128]{2,1,0:T(8,128)(2,1)S(1)}, u32[]{:S(2)}, u32[]{:S(2)}) collective-permute-start(bf16[16,32,128]{2,1,0:T(8,128)(2,1)} %channelise.1.refs_0_), channel_id=1, source_target_pairs={{0,8},{2,10},{4,12},{6,14},{8,0},{10,2},{12,4},{14,6},{16,24},{18,... | collective-permute-start | bytes 393224 | tf_op jit(solution)/shard_map/ppermute | solution.py:212
  17.6 1.5 %collective-permute-start.1 = (bf16[16,32,128]{2,1,0:T(8,128)(2,1)}, bf16[16,32,128]{2,1,0:T(8,128)(2,1)S(1)}, u32[]{:S(2)}, u32[]{:S(2)}) collective-permute-start(bf16[16,32,128]{2,1,0:T(8,128)(2,1)} %channelise.1.refs_0_), channel_id=1, source_target_pairs={{0,4},{2,6},{4,0},{6,2},{8,12},{10,14},{12,8},{14,10},{16,20},{18,... | collective-permute-start | bytes 393224 | tf_op jit(solution)/shard_map/ppermute | solution.py:212
  19.0 0.0 collective-permute-start
  19.0 2.0 %collective-permute-done.7.refs_8_ = bf16[16,32,128]{2,1,0:T(8,128)(2,1)S(1)} collective-permute-done((bf16[16,32,128]{2,1,0:T(8,128)(2,1)}, bf16[16,32,128]{2,1,0:T(8,128)(2,1)S(1)}, u32[]{:S(2)}, u32[]{:S(2)}) %collective-permute-start.7) | collective-permute-done | bytes 131104 | tf_op jit(solution)/shard_map/ppermute | solution.py:212
  21.1 0.8 %collective-permute-start.11 = (bf16[16,32,128]{2,1,0:T(8,128)(2,1)S(1)}, bf16[16,32,128]{2,1,0:T(8,128)(2,1)S(1)}, u32[]{:S(2)}, u32[]{:S(2)}) collective-permute-start(bf16[16,32,128]{2,1,0:T(8,128)(2,1)S(1)} %collective-permute-done.7.refs_8_), channel_id=1, source_target_pairs={{0,8},{2,10},{4,12},{6,14},{8,0},{10,2},{12,4},{14,6},{16,24},{18,... | collective-permute-start | bytes 393224 | tf_op jit(solution)/shard_map/ppermute | solution.py:212
  21.8 0.0 collective-permute-done.15.refs_16_
  21.8 1.5 %collective-permute-start.9 = (bf16[16,32,128]{2,1,0:T(8,128)(2,1)S(1)}, bf16[16,32,128]{2,1,0:T(8,128)(2,1)S(1)}, u32[]{:S(2)}, u32[]{:S(2)}) collective-permute-start(bf16[16,32,128]{2,1,0:T(8,128)(2,1)S(1)} %collective-permute-done.7.refs_8_), channel_id=1, source_target_pairs={{0,4},{2,6},{4,0},{6,2},{8,12},{10,14},{12,8},{14,10},{16,20},{18,... | collective-permute-start | bytes 393224 | tf_op jit(solution)/shard_map/ppermute | solution.py:212
  23.3 0.0 collective-permute-done.3.refs_4_
  23.3 0.0 collective-permute-start.8
  23.3 0.0 collective-permute-done.1.refs_2_
  23.4 0.9 %collective-permute-start.5 = (bf16[16,32,128]{2,1,0:T(8,128)(2,1)S(1)}, bf16[16,32,128]{2,1,0:T(8,128)(2,1)S(1)}, u32[]{:S(2)}, u32[]{:S(2)}) collective-permute-start(bf16[16,32,128]{2,1,0:T(8,128)(2,1)S(1)} %collective-permute-done.3.refs_4_), channel_id=1, source_target_pairs={{0,4},{2,6},{4,0},{6,2},{8,12},{10,14},{12,8},{14,10},{16,20},{18,... | collective-permute-start | bytes 393224 | tf_op jit(solution)/shard_map/ppermute | solution.py:212
  24.2 0.0 collective-permute-done.refs_1_
  24.2 0.1 collective-permute-start.4
  24.3 1.8 %collective-permute-done.11.refs_12_ = bf16[16,32,128]{2,1,0:T(8,128)(2,1)S(1)} collective-permute-done((bf16[16,32,128]{2,1,0:T(8,128)(2,1)S(1)}, bf16[16,32,128]{2,1,0:T(8,128)(2,1)S(1)}, u32[]{:S(2)}, u32[]{:S(2)}) %collective-permute-start.11) | collective-permute-done | bytes 131104 | tf_op jit(solution)/shard_map/ppermute | solution.py:212
  26.0 1.5 %collective-permute-start.13 = (bf16[16,32,128]{2,1,0:T(8,128)(2,1)S(1)}, bf16[16,32,128]{2,1,0:T(8,128)(2,1)S(1)}, u32[]{:S(2)}, u32[]{:S(2)}) collective-permute-start(bf16[16,32,128]{2,1,0:T(8,128)(2,1)S(1)} %collective-permute-done.11.refs_12_), channel_id=1, source_target_pairs={{0,4},{2,6},{4,0},{6,2},{8,12},{10,14},{12,8},{14,10},{16,20},{18,... | collective-permute-start | bytes 393224 | tf_op jit(solution)/shard_map/ppermute | solution.py:212
  27.6 0.0 collective-permute-done.9.refs_10_
  27.6 0.0 collective-permute-start.2
  27.6 0.0 collective-permute-done.8.refs_9_
  27.6 0.5 %collective-permute-start.12 = (bf16[16,32,128]{2,1,0:T(8,128)(2,1)S(1)}, bf16[16,32,128]{2,1,0:T(8,128)(2,1)S(1)}, u32[]{:S(2)}, u32[]{:S(2)}) collective-permute-start(bf16[16,32,128]{2,1,0:T(8,128)(2,1)S(1)} %collective-permute-done.11.refs_12_), channel_id=1, source_target_pairs={{0,2},{2,0},{4,6},{6,4},{8,10},{10,8},{12,14},{14,12},{16,18},{18,... | collective-permute-start | bytes 393224 | tf_op jit(solution)/shard_map/ppermute | solution.py:212
  28.1 2.2 %collective-permute-done.5.refs_6_ = bf16[16,32,128]{2,1,0:T(8,128)(2,1)S(1)} collective-permute-done((bf16[16,32,128]{2,1,0:T(8,128)(2,1)S(1)}, bf16[16,32,128]{2,1,0:T(8,128)(2,1)S(1)}, u32[]{:S(2)}, u32[]{:S(2)}) %collective-permute-start.5) | collective-permute-done | bytes 131104 | tf_op jit(solution)/shard_map/ppermute | solution.py:212
  30.3 0.0 collective-permute-start.10
  30.3 0.0 collective-permute-done.4.refs_5_
  30.3 0.5 %collective-permute-start.6 = (bf16[16,32,128]{2,1,0:T(8,128)(2,1)S(1)}, bf16[16,32,128]{2,1,0:T(8,128)(2,1)S(1)}, u32[]{:S(2)}, u32[]{:S(2)}) collective-permute-start(bf16[16,32,128]{2,1,0:T(8,128)(2,1)S(1)} %collective-permute-done.5.refs_6_), channel_id=1, source_target_pairs={{0,2},{2,0},{4,6},{6,4},{8,10},{10,8},{12,14},{14,12},{16,18},{18,... | collective-permute-start | bytes 393224 | tf_op jit(solution)/shard_map/ppermute | solution.py:212
  30.8 1.8 %collective-permute-done.13.refs_14_ = bf16[16,32,128]{2,1,0:T(8,128)(2,1)S(1)} collective-permute-done((bf16[16,32,128]{2,1,0:T(8,128)(2,1)S(1)}, bf16[16,32,128]{2,1,0:T(8,128)(2,1)S(1)}, u32[]{:S(2)}, u32[]{:S(2)}) %collective-permute-start.13) | collective-permute-done | bytes 131104 | tf_op jit(solution)/shard_map/ppermute | solution.py:212
  32.6 0.0 collective-permute-start.14
  32.6 0.0 collective-permute-done.2.refs_3_
  32.6 0.0 collective-permute-done.12.refs_13_
  32.6 0.0 collective-permute-done.10.refs_11_
  32.6 0.0 collective-permute-done.6.refs_7_
  32.6 1.3 %collective-permute-done.14.refs_15_ = bf16[16,32,128]{2,1,0:T(8,128)(2,1)S(1)} collective-permute-done((bf16[16,32,128]{2,1,0:T(8,128)(2,1)S(1)}, bf16[16,32,128]{2,1,0:T(8,128)(2,1)S(1)}, u32[]{:S(2)}, u32[]{:S(2)}) %collective-permute-start.14) | collective-permute-done | bytes 131104 | tf_op jit(solution)/shard_map/ppermute | solution.py:212
  33.9 0.0 copy-start
  34.0 0.9 %copy-done = bf16[16,32,128]{2,1,0:T(8,128)(2,1)S(1)} copy-done((bf16[16,32,128]{2,1,0:T(8,128)(2,1)S(1)}, bf16[16,32,128]{2,1,0:T(8,128)(2,1)}, u32[]{:S(2)}) %copy-start) | copy-done | bytes 131096
  34.9 4.3 %correlate.1 = bf16[16,2,256,128]{3,2,1,0:T(8,128)(2,1)} custom-call(bf16[16,32,128]{2,1,0:T(8,128)(2,1)S(1)} %copy-done, bf16[16,32,128]{2,1,0:T(8,128)(2,1)S(1)} %collective-permute-done.refs_1_, bf16[16,32,128]{2,1,0:T(8,128)(2,1)S(1)} %collective-permute-done.1.refs_2_, bf16[16,32,128]{2,1,0:T(8,128)(2,1)S(1)} %collective-permute-done.2.refs_3_, ...), custom_call_target="tpu_custom_call" | custom-call | tf_op jit(solution)/shard_map/correlate/pallas_call | solution.py:272
Async XLA Ops:
  10.3 10.7 %collective-permute-start.7 = (bf16[16,32,128]{2,1,0:T(8,128)(2,1)}, bf16[16,32,128]{2,1,0:T(8,128)(2,1)S(1)}, u32[]{:S(2)}, u32[]{:S(2)}) collective-permute-start(bf16[16,32,128]{2,1,0:T(8,128)(2,1)} %channelise.1.refs_0_), channel_id=1, source_target_pairs={{0,16},{2,18},{4,20},{6,22},{8,24},{10,26},{12,28},{14,30},{16,0},... | collective-permute-start | bytes 393224 | tf_op jit(solution)/shard_map/ppermute | solution.py:212
  14.5 7.4 %collective-permute-start.15 = (bf16[16,32,128]{2,1,0:T(8,128)(2,1)}, bf16[16,32,128]{2,1,0:T(8,128)(2,1)S(1)}, u32[]{:S(2)}, u32[]{:S(2)}) collective-permute-start(bf16[16,32,128]{2,1,0:T(8,128)(2,1)} %channelise.1.refs_0_), channel_id=1, source_target_pairs={{0,1},{1,0},{2,3},{3,2},{4,5},{5,4},{6,7},{7,6},{8,9},{9,8},{10,11... | collective-permute-start | bytes 393224 | tf_op jit(solution)/shard_map/ppermute | solution.py:290
  16.0 7.4 %collective-permute-start.3 = (bf16[16,32,128]{2,1,0:T(8,128)(2,1)}, bf16[16,32,128]{2,1,0:T(8,128)(2,1)S(1)}, u32[]{:S(2)}, u32[]{:S(2)}) collective-permute-start(bf16[16,32,128]{2,1,0:T(8,128)(2,1)} %channelise.1.refs_0_), channel_id=1, source_target_pairs={{0,8},{2,10},{4,12},{6,14},{8,0},{10,2},{12,4},{14,6},{16,24},{18,... | collective-permute-start | bytes 393224 | tf_op jit(solution)/shard_map/ppermute | solution.py:212
  17.6 5.8 %collective-permute-start.1 = (bf16[16,32,128]{2,1,0:T(8,128)(2,1)}, bf16[16,32,128]{2,1,0:T(8,128)(2,1)S(1)}, u32[]{:S(2)}, u32[]{:S(2)}) collective-permute-start(bf16[16,32,128]{2,1,0:T(8,128)(2,1)} %channelise.1.refs_0_), channel_id=1, source_target_pairs={{0,4},{2,6},{4,0},{6,2},{8,12},{10,14},{12,8},{14,10},{16,20},{18,... | collective-permute-start | bytes 393224 | tf_op jit(solution)/shard_map/ppermute | solution.py:212
  19.0 5.2 %collective-permute-start = (bf16[16,32,128]{2,1,0:T(8,128)(2,1)}, bf16[16,32,128]{2,1,0:T(8,128)(2,1)S(1)}, u32[]{:S(2)}, u32[]{:S(2)}) collective-permute-start(bf16[16,32,128]{2,1,0:T(8,128)(2,1)} %channelise.1.refs_0_), channel_id=1, source_target_pairs={{0,2},{2,0},{4,6},{6,4},{8,10},{10,8},{12,14},{14,12},{16,18},{18,... | collective-permute-start | bytes 393224 | tf_op jit(solution)/shard_map/ppermute | solution.py:212
  21.1 5.0 %collective-permute-start.11 = (bf16[16,32,128]{2,1,0:T(8,128)(2,1)S(1)}, bf16[16,32,128]{2,1,0:T(8,128)(2,1)S(1)}, u32[]{:S(2)}, u32[]{:S(2)}) collective-permute-start(bf16[16,32,128]{2,1,0:T(8,128)(2,1)S(1)} %collective-permute-done.7.refs_8_), channel_id=1, source_target_pairs={{0,8},{2,10},{4,12},{6,14},{8,0},{10,2},{12,4},{14,6},{16,24},{18,... | collective-permute-start | bytes 393224 | tf_op jit(solution)/shard_map/ppermute | solution.py:212
  21.8 5.7 %collective-permute-start.9 = (bf16[16,32,128]{2,1,0:T(8,128)(2,1)S(1)}, bf16[16,32,128]{2,1,0:T(8,128)(2,1)S(1)}, u32[]{:S(2)}, u32[]{:S(2)}) collective-permute-start(bf16[16,32,128]{2,1,0:T(8,128)(2,1)S(1)} %collective-permute-done.7.refs_8_), channel_id=1, source_target_pairs={{0,4},{2,6},{4,0},{6,2},{8,12},{10,14},{12,8},{14,10},{16,20},{18,... | collective-permute-start | bytes 393224 | tf_op jit(solution)/shard_map/ppermute | solution.py:212
  23.3 4.2 %collective-permute-start.8 = (bf16[16,32,128]{2,1,0:T(8,128)(2,1)S(1)}, bf16[16,32,128]{2,1,0:T(8,128)(2,1)S(1)}, u32[]{:S(2)}, u32[]{:S(2)}) collective-permute-start(bf16[16,32,128]{2,1,0:T(8,128)(2,1)S(1)} %collective-permute-done.7.refs_8_), channel_id=1, source_target_pairs={{0,2},{2,0},{4,6},{6,4},{8,10},{10,8},{12,14},{14,12},{16,18},{18,... | collective-permute-start | bytes 393224 | tf_op jit(solution)/shard_map/ppermute | solution.py:212
  23.4 7.0 %collective-permute-start.5 = (bf16[16,32,128]{2,1,0:T(8,128)(2,1)S(1)}, bf16[16,32,128]{2,1,0:T(8,128)(2,1)S(1)}, u32[]{:S(2)}, u32[]{:S(2)}) collective-permute-start(bf16[16,32,128]{2,1,0:T(8,128)(2,1)S(1)} %collective-permute-done.3.refs_4_), channel_id=1, source_target_pairs={{0,4},{2,6},{4,0},{6,2},{8,12},{10,14},{12,8},{14,10},{16,20},{18,... | collective-permute-start | bytes 393224 | tf_op jit(solution)/shard_map/ppermute | solution.py:212
  24.2 6.1 %collective-permute-start.4 = (bf16[16,32,128]{2,1,0:T(8,128)(2,1)S(1)}, bf16[16,32,128]{2,1,0:T(8,128)(2,1)S(1)}, u32[]{:S(2)}, u32[]{:S(2)}) collective-permute-start(bf16[16,32,128]{2,1,0:T(8,128)(2,1)S(1)} %collective-permute-done.3.refs_4_), channel_id=1, source_target_pairs={{0,2},{2,0},{4,6},{6,4},{8,10},{10,8},{12,14},{14,12},{16,18},{18,... | collective-permute-start | bytes 393224 | tf_op jit(solution)/shard_map/ppermute | solution.py:212
  26.0 6.6 %collective-permute-start.13 = (bf16[16,32,128]{2,1,0:T(8,128)(2,1)S(1)}, bf16[16,32,128]{2,1,0:T(8,128)(2,1)S(1)}, u32[]{:S(2)}, u32[]{:S(2)}) collective-permute-start(bf16[16,32,128]{2,1,0:T(8,128)(2,1)S(1)} %collective-permute-done.11.refs_12_), channel_id=1, source_target_pairs={{0,4},{2,6},{4,0},{6,2},{8,12},{10,14},{12,8},{14,10},{16,20},{18,... | collective-permute-start | bytes 393224 | tf_op jit(solution)/shard_map/ppermute | solution.py:212
  27.6 5.0 %collective-permute-start.2 = (bf16[16,32,128]{2,1,0:T(8,128)(2,1)S(1)}, bf16[16,32,128]{2,1,0:T(8,128)(2,1)S(1)}, u32[]{:S(2)}, u32[]{:S(2)}) collective-permute-start(bf16[16,32,128]{2,1,0:T(8,128)(2,1)S(1)} %collective-permute-done.1.refs_2_), channel_id=1, source_target_pairs={{0,2},{2,0},{4,6},{6,4},{8,10},{10,8},{12,14},{14,12},{16,18},{18,... | collective-permute-start | bytes 393224 | tf_op jit(solution)/shard_map/ppermute | solution.py:212
  27.6 5.0 %collective-permute-start.12 = (bf16[16,32,128]{2,1,0:T(8,128)(2,1)S(1)}, bf16[16,32,128]{2,1,0:T(8,128)(2,1)S(1)}, u32[]{:S(2)}, u32[]{:S(2)}) collective-permute-start(bf16[16,32,128]{2,1,0:T(8,128)(2,1)S(1)} %collective-permute-done.11.refs_12_), channel_id=1, source_target_pairs={{0,2},{2,0},{4,6},{6,4},{8,10},{10,8},{12,14},{14,12},{16,18},{18,... | collective-permute-start | bytes 393224 | tf_op jit(solution)/shard_map/ppermute | solution.py:212
  30.3 2.3 %collective-permute-start.10 = (bf16[16,32,128]{2,1,0:T(8,128)(2,1)S(1)}, bf16[16,32,128]{2,1,0:T(8,128)(2,1)S(1)}, u32[]{:S(2)}, u32[]{:S(2)}) collective-permute-start(bf16[16,32,128]{2,1,0:T(8,128)(2,1)S(1)} %collective-permute-done.9.refs_10_), channel_id=1, source_target_pairs={{0,2},{2,0},{4,6},{6,4},{8,10},{10,8},{12,14},{14,12},{16,18},{18,... | collective-permute-start | bytes 393224 | tf_op jit(solution)/shard_map/ppermute | solution.py:212
  30.3 2.3 %collective-permute-start.6 = (bf16[16,32,128]{2,1,0:T(8,128)(2,1)S(1)}, bf16[16,32,128]{2,1,0:T(8,128)(2,1)S(1)}, u32[]{:S(2)}, u32[]{:S(2)}) collective-permute-start(bf16[16,32,128]{2,1,0:T(8,128)(2,1)S(1)} %collective-permute-done.5.refs_6_), channel_id=1, source_target_pairs={{0,2},{2,0},{4,6},{6,4},{8,10},{10,8},{12,14},{14,12},{16,18},{18,... | collective-permute-start | bytes 393224 | tf_op jit(solution)/shard_map/ppermute | solution.py:212
  32.6 1.3 %collective-permute-start.14 = (bf16[16,32,128]{2,1,0:T(8,128)(2,1)S(1)}, bf16[16,32,128]{2,1,0:T(8,128)(2,1)S(1)}, u32[]{:S(2)}, u32[]{:S(2)}) collective-permute-start(bf16[16,32,128]{2,1,0:T(8,128)(2,1)S(1)} %collective-permute-done.13.refs_14_), channel_id=1, source_target_pairs={{0,2},{2,0},{4,6},{6,4},{8,10},{10,8},{12,14},{14,12},{16,18},{18,... | collective-permute-start | bytes 393224 | tf_op jit(solution)/shard_map/ppermute | solution.py:212
  33.9 0.9 %copy-start = (bf16[16,32,128]{2,1,0:T(8,128)(2,1)S(1)}, bf16[16,32,128]{2,1,0:T(8,128)(2,1)}, u32[]{:S(2)}) copy-start(bf16[16,32,128]{2,1,0:T(8,128)(2,1)} %channelise.1.refs_0_) | copy-start | bytes 393220

commit v2 on v1

--- a/solution.py
+++ b/solution.py
@@ -91,17 +91,8 @@
     return table.transpose(0, 2, 1, 3).reshape(NFFT // 2, -1).astype(ml_dtypes.bfloat16)
 
 
-def lane_order():
-    order = np.zeros((8 * SPECTRA, 8 * SPECTRA), np.float32)
-    part, s, half, q = np.meshgrid(range(2), range(SPECTRA // 2), range(2), range(Q_DEV), indexing="ij")
-    source = ((part * (SPECTRA // 2) + s) * 2 + half) * Q_DEV + q
-    target = ((q * 2 + part) * 2 + half) * (SPECTRA // 2) + s
-    order[source.ravel(), target.ravel()] = 1
-    return order.astype(ml_dtypes.bfloat16)
-
-
 def filter_kernel(
-    volts, table, order, lane_map, flags, out, held, table_v, order_v, sums, lanes, rows, in_sem, const_sem
+    volts, table, lane_map, flags, out, held, table_v, map_s, flags_s, frames, sums, lanes, rows, in_sem, const_sem
 ):
     ahead = 3
     arrivals = [
@@ -112,7 +103,8 @@
         for p in range(P_DEV)
     ]
     get_table = pltpu.make_async_copy(table, table_v, const_sem.at[0])
-    get_order = pltpu.make_async_copy(order, order_v, const_sem.at[1])
+    get_map = pltpu.make_async_copy(lane_map, map_s, const_sem.at[1])
+    get_flags = pltpu.make_async_copy(flags, flags_s, const_sem.at[2])
 
     def begin(p):
         for copy in arrivals[p]:
@@ -120,39 +112,64 @@
         if p == 0:
             get_table.start()
         if p == 2:
-            get_order.start()
-
-    first_half = lax.broadcasted_iota(jnp.int32, (35, 8, CHUNK), 1) < Q_DEV
-    tap_of_lane = lax.broadcasted_iota(jnp.int32, (32, 8, CHUNK), 2) // 32
-
-    def frames_of(p):
+            get_map.start()
+            get_flags.start()
+
+    first_half = lax.broadcasted_iota(jnp.int32, (8, 8, CHUNK), 1) < Q_DEV
+    real_lanes = lax.broadcasted_iota(jnp.int32, (CH_DEV, 2 * SPECTRA), 1) < SPECTRA
+    lane_group = lax.broadcasted_iota(jnp.int32, (64, CHUNK), 1) // 32
+
+    def pair(low, high):
+        upper = first_half[: low.shape[0]]
+        straight = jnp.where(upper, low[:, :, :CHUNK], high[:, :, CHUNK:])
+        crossed = jnp.where(upper, high[:, :, :CHUNK], low[:, :, CHUNK:])
+        return straight + pltpu.roll(crossed, 4, 1)
+
+    def frames_of(p, i, kept):
+        spans = [(64 * i, 64), (256 + 64 * i, 64 if i < 3 else 96)]
         block = jnp.concatenate(
-            [held.at[p, j].reshape(68 * 8, CHUNK)[...] for j in range(CHUNKS // 2)], axis=1
+            [
+                jnp.concatenate([held.at[p, j].reshape(68 * 8, CHUNK)[at : at + size] for at, size in spans], axis=0)
+                for j in range(CHUNKS // 2)
+            ],
+            axis=1,
         )
-        both = jnp.dot(block, table_v[...], preferred_element_type=jnp.float32).reshape(68, 8, 2 * CHUNK)
-        even, odd = both[:, :, :CHUNK], both[:, :, CHUNK:]
-        straight = jnp.where(first_half, even[0:35], odd[32:67])
-        crossed = jnp.where(first_half, even[32:67], odd[0:35])
-        sums[p % 4] = straight + pltpu.roll(crossed, 4, 1)
+        both = jnp.dot(block, table_v[...], preferred_element_type=jnp.float32)
+        both = both.reshape(-1, 8, 2 * CHUNK)
+        frames[p % 2, 8 * i : 8 * i + 8] = pair(both[:8], both[8:16])
+        if i == 0:
+            return both[8:11]
+        if i == 3:
+            frames[p % 2, 32:35] = pair(kept, both[16:19])
+        return kept
+
+    def taps_of(p, i):
+        total = None
+        for tap in range(TAPS):
+            term = frames[p % 2, 8 * i + tap : 8 * i + tap + 8]
+            turn = 32 * (p % 4 - tap) % CHUNK
+            if turn:
+                term = pltpu.roll(term, turn, 2)
+            total = term if total is None else total + term
+        total = total.reshape(64, CHUNK)
+        at = slice(64 * i, 64 * i + 64)
+        sums[p // 4, at] = total if p % 4 == 0 else jnp.where(lane_group == p % 4, total, sums[p // 4, at])
 
     def finish(first):
-        total = None
-        for turn in range(4):
-            term = sums[turn, 0:32]
-            for tap in range(1, TAPS):
-                term = jnp.where(tap_of_lane == tap, sums[(tap + turn) % 4, tap : tap + 32], term)
-            if turn:
-                term = pltpu.roll(term, 32 * turn, 2)
-            total = term if total is None else total + term
-        filtered = total.reshape(4 * SPECTRA, CHUNK).T.astype(jnp.bfloat16)
-        filtered = filtered.reshape(4, 2, CH_DEV, 4 * SPECTRA)
-        filtered = jnp.concatenate(
-            [jnp.concatenate([filtered[i, 0], filtered[i, 1]], axis=1) for i in range(4)], axis=0
-        )
-        ordered = jnp.dot(filtered, order_v[...], preferred_element_type=jnp.float32)
+        by_q = [
+            sums[first // 4, pl.ds(half * Q_DEV + q, SPECTRA // 2, stride=8), :]
+            for q in range(Q_DEV)
+            for half in range(2)
+        ]
+        turned = jnp.concatenate(by_q, axis=0).T.reshape(4, 2, CH_DEV, Q_DEV * SPECTRA)
         for i in range(4):
             for q in range(Q_DEV):
-                lanes[(first + i) * Q_DEV + q] = ordered[i * 16 : i * 16 + 16, q * 128 : q * 128 + 128]
+                real, imag = (turned[i, part, :, q // 2 * CHUNK : q // 2 * CHUNK + CHUNK] for part in range(2))
+                if q % 2:
+                    real = pltpu.roll(real, SPECTRA, 1)
+                else:
+                    imag = pltpu.roll(imag, SPECTRA, 1)
+                lanes[(first + i) * Q_DEV + q] = jnp.where(real_lanes, real, imag)
 
     for p in range(ahead):
         begin(p)
@@ -163,15 +180,23 @@
             begin(p + ahead)
         if p == 0:
             get_table.wait()
-        frames_of(p)
-        if p % 4 == 3:
-            if p == 3:
-                get_order.wait()
-            finish(p - 3)
+        if p == 5:
+            get_map.wait()
+            get_flags.wait()
+        kept = None
+        for i in range(4):
+            kept = frames_of(p, i, kept)
+            if p > 0:
+                taps_of(p - 1, i)
+        if p == 5:
+            finish(0)
+    for i in range(4):
+        taps_of(P_DEV - 1, i)
+    finish(4)
     for p in range(P_DEV):
         for q in range(Q_DEV):
-            weight = flags[q, p].astype(jnp.float32)
-            rows[pl.ds(q * P_DEV + p, CH_DEV, stride=LANES), :] = lanes[lane_map[0, p * Q_DEV + q]] * weight
+            weight = flags_s[q, p].astype(jnp.float32)
+            rows[pl.ds(q * P_DEV + p, CH_DEV, stride=LANES), :] = lanes[map_s[0, p * Q_DEV + q]] * weight
     out[...] = rows[...].astype(jnp.bfloat16).reshape(CH_DEV, LANES, 2 * SPECTRA)
 
 
@@ -179,29 +204,29 @@
     volts = voltages.reshape(P_DEV, Q_DEV, FRAMES, CHUNKS // 2, 2, CHUNK).transpose(0, 2, 3, 4, 1, 5)
     volts = volts.reshape(P_DEV, FRAMES, CHUNKS // 2, 2 * Q_DEV, CHUNK)
     vmem = pl.BlockSpec(memory_space=pltpu.VMEM)
-    smem = pl.BlockSpec(memory_space=pltpu.SMEM)
     hbm = pl.BlockSpec(memory_space=pltpu.HBM)
     return pl.pallas_call(
         filter_kernel,
         out_shape=jax.ShapeDtypeStruct((CH_DEV, LANES, 2 * SPECTRA), jnp.bfloat16),
-        in_specs=[hbm, hbm, hbm, smem, smem],
+        in_specs=[hbm] * 4,
         out_specs=vmem,
         scratch_shapes=[
             pltpu.VMEM((P_DEV, CHUNKS // 2, 68, 2 * Q_DEV, CHUNK), jnp.bfloat16),
             pltpu.VMEM((NFFT // 2, 2 * CHUNK), jnp.bfloat16),
-            pltpu.VMEM((8 * SPECTRA, 8 * SPECTRA), jnp.bfloat16),
-            pltpu.VMEM((4, 35, 8, CHUNK), jnp.float32),
+            pltpu.SMEM((1, LANES), jnp.int32),
+            pltpu.SMEM((Q_DEV, P_DEV), jnp.int32),
+            pltpu.VMEM((2, 35, 8, CHUNK), jnp.float32),
+            pltpu.VMEM((2, 4 * SPECTRA, CHUNK), jnp.float32),
             pltpu.VMEM((LANES, CH_DEV, 2 * SPECTRA), jnp.float32),
             pltpu.VMEM((CH_DEV * LANES, 2 * SPECTRA), jnp.float32),
             pltpu.SemaphoreType.DMA((P_DEV,)),
-            pltpu.SemaphoreType.DMA((2,)),
+            pltpu.SemaphoreType.DMA((3,)),
         ],
         compiler_params=pltpu.CompilerParams(vmem_limit_bytes=56 << 20),
         name="channelise",
     )(
         volts,
         jnp.asarray(filter_table(CH_DEV)),
-        jnp.asarray(lane_order()),
         lane_map.reshape(1, LANES),
         input_flags.T,
     )

time: 39.4 us -> 36.7 us (0.931)
  Pallas kernels: 14.7 us -> 12 us
    pallas_call x1, Pallas kernels: 10.3 us -> 7.68 us  [channelise(): pl.pallas_call(filter_kernel, out_shape=jax.ShapeDtypeStruct((CH_DEV, LAN...]
where the time goes in v2:
time: 36.7 us; the launch traced here: 36.5 us
  starting transfers between devices  14.4 us (39%)
  Pallas kernels  12 us (33%)
  waiting for transfers between devices  9.11 us (25%)
  local copies, waits for them, and re-layouts  0.9 us (2%)
    ppermute x15, starting transfers between devices, swap(): return lax.ppermute(block, 'row', [(i, i ^ d) for i in range(ROWS)])  12.9 us
    ppermute x15, waiting for transfers between devices, swap(): return lax.ppermute(block, 'row', [(i, i ^ d) for i in range(ROWS)])  9.1 us
    pallas_call x1, Pallas kernels, channelise(): pl.pallas_call(filter_kernel, out_shape=jax.ShapeDtypeStruct((CH_DEV, LAN...  7.68 us
    pallas_call x1, Pallas kernels, correlate(): pl.pallas_call(correlate_kernel, out_shape=jax.ShapeDtypeStruct((CH_DEV,...  4.33 us
    ppermute x1, starting transfers between devices, per_device(): other = lax.ppermute(own, 'col', [(0, 1), (1, 0)])  1.55 us
    unnamed x2, local copies, waits for them, and re-layouts  0.9 us
  transfers between devices with their start and end apart: 16, of which 5 were waited for; matrix products, arithmetic and copies ran while one was open for 0% of the time, Pallas kernels for 0%

profile of v2, /device:TPU:0, one launch (start us, length us, event | category | flops | bytes accessed | tf_op | source)
XLA Modules:
  0.0 36.5 jit_solution(12136327716428253954)
XLA Ops:
  0.0 7.7 %channelise.1.refs_0_ = bf16[16,32,128]{2,1,0:T(8,128)(2,1)} custom-call(bf16[8,67,8,8,128]{4,3,2,1,0:T(8,128)(2,1)} %bitcast.8, bf16[1024,256]{1,0:T(8,128)(2,1)} %constant.2.clone.table, s32[1,32]{1,0:T(1,128)} %bitcast.10, s32[4,8]{1,0:T(4,128)} %bitcast.9), custom_call_target="tpu_custom_call" | custom-call | tf_op jit(solution)/shard_map/channelise/pallas_call | solution.py:208
  7.7 4.1 %collective-permute-start.7 = (bf16[16,32,128]{2,1,0:T(8,128)(2,1)}, bf16[16,32,128]{2,1,0:T(8,128)(2,1)S(1)}, u32[]{:S(2)}, u32[]{:S(2)}) collective-permute-start(bf16[16,32,128]{2,1,0:T(8,128)(2,1)} %channelise.1.refs_0_), channel_id=1, source_target_pairs={{0,16},{2,18},{4,20},{6,22},{8,24},{10,26},{12,28},{14,30},{16,0},... | collective-permute-start | bytes 393224 | tf_op jit(solution)/shard_map/ppermute | solution.py:237
  11.8 1.5 %collective-permute-start.15 = (bf16[16,32,128]{2,1,0:T(8,128)(2,1)}, bf16[16,32,128]{2,1,0:T(8,128)(2,1)S(1)}, u32[]{:S(2)}, u32[]{:S(2)}) collective-permute-start(bf16[16,32,128]{2,1,0:T(8,128)(2,1)} %channelise.1.refs_0_), channel_id=1, source_target_pairs={{0,1},{1,0},{2,3},{3,2},{4,5},{5,4},{6,7},{7,6},{8,9},{9,8},{10,11... | collective-permute-start | bytes 393224 | tf_op jit(solution)/shard_map/ppermute | solution.py:315
  13.3 1.5 %collective-permute-start.3 = (bf16[16,32,128]{2,1,0:T(8,128)(2,1)}, bf16[16,32,128]{2,1,0:T(8,128)(2,1)S(1)}, u32[]{:S(2)}, u32[]{:S(2)}) collective-permute-start(bf16[16,32,128]{2,1,0:T(8,128)(2,1)} %channelise.1.refs_0_), channel_id=1, source_target_pairs={{0,8},{2,10},{4,12},{6,14},{8,0},{10,2},{12,4},{14,6},{16,24},{18,... | collective-permute-start | bytes 393224 | tf_op jit(solution)/shard_map/ppermute | solution.py:237
  14.9 1.5 %collective-permute-start.1 = (bf16[16,32,128]{2,1,0:T(8,128)(2,1)}, bf16[16,32,128]{2,1,0:T(8,128)(2,1)S(1)}, u32[]{:S(2)}, u32[]{:S(2)}) collective-permute-start(bf16[16,32,128]{2,1,0:T(8,128)(2,1)} %channelise.1.refs_0_), channel_id=1, source_target_pairs={{0,4},{2,6},{4,0},{6,2},{8,12},{10,14},{12,8},{14,10},{16,20},{18,... | collective-permute-start | bytes 393224 | tf_op jit(solution)/shard_map/ppermute | solution.py:237
  16.4 0.0 collective-permute-start
  16.4 2.0 %collective-permute-done.7.refs_8_ = bf16[16,32,128]{2,1,0:T(8,128)(2,1)S(1)} collective-permute-done((bf16[16,32,128]{2,1,0:T(8,128)(2,1)}, bf16[16,32,128]{2,1,0:T(8,128)(2,1)S(1)}, u32[]{:S(2)}, u32[]{:S(2)}) %collective-permute-start.7) | collective-permute-done | bytes 131104 | tf_op jit(solution)/shard_map/ppermute | solution.py:237
  18.4 0.8 %collective-permute-start.11 = (bf16[16,32,128]{2,1,0:T(8,128)(2,1)S(1)}, bf16[16,32,128]{2,1,0:T(8,128)(2,1)S(1)}, u32[]{:S(2)}, u32[]{:S(2)}) collective-permute-start(bf16[16,32,128]{2,1,0:T(8,128)(2,1)S(1)} %collective-permute-done.7.refs_8_), channel_id=1, source_target_pairs={{0,8},{2,10},{4,12},{6,14},{8,0},{10,2},{12,4},{14,6},{16,24},{18,... | collective-permute-start | bytes 393224 | tf_op jit(solution)/shard_map/ppermute | solution.py:237
  19.2 0.0 collective-permute-done.15.refs_16_
  19.2 1.5 %collective-permute-start.9 = (bf16[16,32,128]{2,1,0:T(8,128)(2,1)S(1)}, bf16[16,32,128]{2,1,0:T(8,128)(2,1)S(1)}, u32[]{:S(2)}, u32[]{:S(2)}) collective-permute-start(bf16[16,32,128]{2,1,0:T(8,128)(2,1)S(1)} %collective-permute-done.7.refs_8_), channel_id=1, source_target_pairs={{0,4},{2,6},{4,0},{6,2},{8,12},{10,14},{12,8},{14,10},{16,20},{18,... | collective-permute-start | bytes 393224 | tf_op jit(solution)/shard_map/ppermute | solution.py:237
  20.7 0.0 collective-permute-done.3.refs_4_
  20.7 0.0 collective-permute-start.8
  20.7 0.0 collective-permute-done.1.refs_2_
  20.7 0.9 %collective-permute-start.5 = (bf16[16,32,128]{2,1,0:T(8,128)(2,1)S(1)}, bf16[16,32,128]{2,1,0:T(8,128)(2,1)S(1)}, u32[]{:S(2)}, u32[]{:S(2)}) collective-permute-start(bf16[16,32,128]{2,1,0:T(8,128)(2,1)S(1)} %collective-permute-done.3.refs_4_), channel_id=1, source_target_pairs={{0,4},{2,6},{4,0},{6,2},{8,12},{10,14},{12,8},{14,10},{16,20},{18,... | collective-permute-start | bytes 393224 | tf_op jit(solution)/shard_map/ppermute | solution.py:237
  21.6 0.0 collective-permute-done.refs_1_
  21.6 0.1 collective-permute-start.4
  21.6 1.8 %collective-permute-done.11.refs_12_ = bf16[16,32,128]{2,1,0:T(8,128)(2,1)S(1)} collective-permute-done((bf16[16,32,128]{2,1,0:T(8,128)(2,1)S(1)}, bf16[16,32,128]{2,1,0:T(8,128)(2,1)S(1)}, u32[]{:S(2)}, u32[]{:S(2)}) %collective-permute-start.11) | collective-permute-done | bytes 131104 | tf_op jit(solution)/shard_map/ppermute | solution.py:237
  23.4 1.5 %collective-permute-start.13 = (bf16[16,32,128]{2,1,0:T(8,128)(2,1)S(1)}, bf16[16,32,128]{2,1,0:T(8,128)(2,1)S(1)}, u32[]{:S(2)}, u32[]{:S(2)}) collective-permute-start(bf16[16,32,128]{2,1,0:T(8,128)(2,1)S(1)} %collective-permute-done.11.refs_12_), channel_id=1, source_target_pairs={{0,4},{2,6},{4,0},{6,2},{8,12},{10,14},{12,8},{14,10},{16,20},{18,... | collective-permute-start | bytes 393224 | tf_op jit(solution)/shard_map/ppermute | solution.py:237
  24.9 0.0 collective-permute-done.9.refs_10_
  24.9 0.0 collective-permute-start.2
  24.9 0.0 collective-permute-done.8.refs_9_
  24.9 0.5 %collective-permute-start.12 = (bf16[16,32,128]{2,1,0:T(8,128)(2,1)S(1)}, bf16[16,32,128]{2,1,0:T(8,128)(2,1)S(1)}, u32[]{:S(2)}, u32[]{:S(2)}) collective-permute-start(bf16[16,32,128]{2,1,0:T(8,128)(2,1)S(1)} %collective-permute-done.11.refs_12_), channel_id=1, source_target_pairs={{0,2},{2,0},{4,6},{6,4},{8,10},{10,8},{12,14},{14,12},{16,18},{18,... | collective-permute-start | bytes 393224 | tf_op jit(solution)/shard_map/ppermute | solution.py:237
  25.4 2.2 %collective-permute-done.5.refs_6_ = bf16[16,32,128]{2,1,0:T(8,128)(2,1)S(1)} collective-permute-done((bf16[16,32,128]{2,1,0:T(8,128)(2,1)S(1)}, bf16[16,32,128]{2,1,0:T(8,128)(2,1)S(1)}, u32[]{:S(2)}, u32[]{:S(2)}) %collective-permute-start.5) | collective-permute-done | bytes 131104 | tf_op jit(solution)/shard_map/ppermute | solution.py:237
  27.7 0.0 collective-permute-start.10
  27.7 0.0 collective-permute-done.4.refs_5_
  27.7 0.5 %collective-permute-start.6 = (bf16[16,32,128]{2,1,0:T(8,128)(2,1)S(1)}, bf16[16,32,128]{2,1,0:T(8,128)(2,1)S(1)}, u32[]{:S(2)}, u32[]{:S(2)}) collective-permute-start(bf16[16,32,128]{2,1,0:T(8,128)(2,1)S(1)} %collective-permute-done.5.refs_6_), channel_id=1, source_target_pairs={{0,2},{2,0},{4,6},{6,4},{8,10},{10,8},{12,14},{14,12},{16,18},{18,... | collective-permute-start | bytes 393224 | tf_op jit(solution)/shard_map/ppermute | solution.py:237
  28.2 1.8 %collective-permute-done.13.refs_14_ = bf16[16,32,128]{2,1,0:T(8,128)(2,1)S(1)} collective-permute-done((bf16[16,32,128]{2,1,0:T(8,128)(2,1)S(1)}, bf16[16,32,128]{2,1,0:T(8,128)(2,1)S(1)}, u32[]{:S(2)}, u32[]{:S(2)}) %collective-permute-start.13) | collective-permute-done | bytes 131104 | tf_op jit(solution)/shard_map/ppermute | solution.py:237
  29.9 0.0 collective-permute-start.14
  29.9 0.0 collective-permute-done.2.refs_3_
  29.9 0.0 collective-permute-done.12.refs_13_
  29.9 0.0 collective-permute-done.10.refs_11_
  30.0 0.0 collective-permute-done.6.refs_7_
  30.0 1.3 %collective-permute-done.14.refs_15_ = bf16[16,32,128]{2,1,0:T(8,128)(2,1)S(1)} collective-permute-done((bf16[16,32,128]{2,1,0:T(8,128)(2,1)S(1)}, bf16[16,32,128]{2,1,0:T(8,128)(2,1)S(1)}, u32[]{:S(2)}, u32[]{:S(2)}) %collective-permute-start.14) | collective-permute-done | bytes 131104 | tf_op jit(solution)/shard_map/ppermute | solution.py:237
  31.3 0.0 copy-start
  31.3 0.9 %copy-done = bf16[16,32,128]{2,1,0:T(8,128)(2,1)S(1)} copy-done((bf16[16,32,128]{2,1,0:T(8,128)(2,1)S(1)}, bf16[16,32,128]{2,1,0:T(8,128)(2,1)}, u32[]{:S(2)}) %copy-start) | copy-done | bytes 131096
  32.2 4.3 %correlate.1 = bf16[16,2,256,128]{3,2,1,0:T(8,128)(2,1)} custom-call(bf16[16,32,128]{2,1,0:T(8,128)(2,1)S(1)} %copy-done, bf16[16,32,128]{2,1,0:T(8,128)(2,1)S(1)} %collective-permute-done.refs_1_, bf16[16,32,128]{2,1,0:T(8,128)(2,1)S(1)} %collective-permute-done.1.refs_2_, bf16[16,32,128]{2,1,0:T(8,128)(2,1)S(1)} %collective-permute-done.2.refs_3_, ...), custom_call_target="tpu_custom_call" | custom-call | tf_op jit(solution)/shard_map/correlate/pallas_call | solution.py:297
Async XLA Ops:
  7.7 10.7 %collective-permute-start.7 = (bf16[16,32,128]{2,1,0:T(8,128)(2,1)}, bf16[16,32,128]{2,1,0:T(8,128)(2,1)S(1)}, u32[]{:S(2)}, u32[]{:S(2)}) collective-permute-start(bf16[16,32,128]{2,1,0:T(8,128)(2,1)} %channelise.1.refs_0_), channel_id=1, source_target_pairs={{0,16},{2,18},{4,20},{6,22},{8,24},{10,26},{12,28},{14,30},{16,0},... | collective-permute-start | bytes 393224 | tf_op jit(solution)/shard_map/ppermute | solution.py:237
  11.8 7.4 %collective-permute-start.15 = (bf16[16,32,128]{2,1,0:T(8,128)(2,1)}, bf16[16,32,128]{2,1,0:T(8,128)(2,1)S(1)}, u32[]{:S(2)}, u32[]{:S(2)}) collective-permute-start(bf16[16,32,128]{2,1,0:T(8,128)(2,1)} %channelise.1.refs_0_), channel_id=1, source_target_pairs={{0,1},{1,0},{2,3},{3,2},{4,5},{5,4},{6,7},{7,6},{8,9},{9,8},{10,11... | collective-permute-start | bytes 393224 | tf_op jit(solution)/shard_map/ppermute | solution.py:315
  13.3 7.3 %collective-permute-start.3 = (bf16[16,32,128]{2,1,0:T(8,128)(2,1)}, bf16[16,32,128]{2,1,0:T(8,128)(2,1)S(1)}, u32[]{:S(2)}, u32[]{:S(2)}) collective-permute-start(bf16[16,32,128]{2,1,0:T(8,128)(2,1)} %channelise.1.refs_0_), channel_id=1, source_target_pairs={{0,8},{2,10},{4,12},{6,14},{8,0},{10,2},{12,4},{14,6},{16,24},{18,... | collective-permute-start | bytes 393224 | tf_op jit(solution)/shard_map/ppermute | solution.py:237
  14.9 5.8 %collective-permute-start.1 = (bf16[16,32,128]{2,1,0:T(8,128)(2,1)}, bf16[16,32,128]{2,1,0:T(8,128)(2,1)S(1)}, u32[]{:S(2)}, u32[]{:S(2)}) collective-permute-start(bf16[16,32,128]{2,1,0:T(8,128)(2,1)} %channelise.1.refs_0_), channel_id=1, source_target_pairs={{0,4},{2,6},{4,0},{6,2},{8,12},{10,14},{12,8},{14,10},{16,20},{18,... | collective-permute-start | bytes 393224 | tf_op jit(solution)/shard_map/ppermute | solution.py:237
  16.4 5.2 %collective-permute-start = (bf16[16,32,128]{2,1,0:T(8,128)(2,1)}, bf16[16,32,128]{2,1,0:T(8,128)(2,1)S(1)}, u32[]{:S(2)}, u32[]{:S(2)}) collective-permute-start(bf16[16,32,128]{2,1,0:T(8,128)(2,1)} %channelise.1.refs_0_), channel_id=1, source_target_pairs={{0,2},{2,0},{4,6},{6,4},{8,10},{10,8},{12,14},{14,12},{16,18},{18,... | collective-permute-start | bytes 393224 | tf_op jit(solution)/shard_map/ppermute | solution.py:237
  18.4 5.0 %collective-permute-start.11 = (bf16[16,32,128]{2,1,0:T(8,128)(2,1)S(1)}, bf16[16,32,128]{2,1,0:T(8,128)(2,1)S(1)}, u32[]{:S(2)}, u32[]{:S(2)}) collective-permute-start(bf16[16,32,128]{2,1,0:T(8,128)(2,1)S(1)} %collective-permute-done.7.refs_8_), channel_id=1, source_target_pairs={{0,8},{2,10},{4,12},{6,14},{8,0},{10,2},{12,4},{14,6},{16,24},{18,... | collective-permute-start | bytes 393224 | tf_op jit(solution)/shard_map/ppermute | solution.py:237
  19.2 5.7 %collective-permute-start.9 = (bf16[16,32,128]{2,1,0:T(8,128)(2,1)S(1)}, bf16[16,32,128]{2,1,0:T(8,128)(2,1)S(1)}, u32[]{:S(2)}, u32[]{:S(2)}) collective-permute-start(bf16[16,32,128]{2,1,0:T(8,128)(2,1)S(1)} %collective-permute-done.7.refs_8_), channel_id=1, source_target_pairs={{0,4},{2,6},{4,0},{6,2},{8,12},{10,14},{12,8},{14,10},{16,20},{18,... | collective-permute-start | bytes 393224 | tf_op jit(solution)/shard_map/ppermute | solution.py:237
  20.7 4.3 %collective-permute-start.8 = (bf16[16,32,128]{2,1,0:T(8,128)(2,1)S(1)}, bf16[16,32,128]{2,1,0:T(8,128)(2,1)S(1)}, u32[]{:S(2)}, u32[]{:S(2)}) collective-permute-start(bf16[16,32,128]{2,1,0:T(8,128)(2,1)S(1)} %collective-permute-done.7.refs_8_), channel_id=1, source_target_pairs={{0,2},{2,0},{4,6},{6,4},{8,10},{10,8},{12,14},{14,12},{16,18},{18,... | collective-permute-start | bytes 393224 | tf_op jit(solution)/shard_map/ppermute | solution.py:237
  20.7 7.0 %collective-permute-start.5 = (bf16[16,32,128]{2,1,0:T(8,128)(2,1)S(1)}, bf16[16,32,128]{2,1,0:T(8,128)(2,1)S(1)}, u32[]{:S(2)}, u32[]{:S(2)}) collective-permute-start(bf16[16,32,128]{2,1,0:T(8,128)(2,1)S(1)} %collective-permute-done.3.refs_4_), channel_id=1, source_target_pairs={{0,4},{2,6},{4,0},{6,2},{8,12},{10,14},{12,8},{14,10},{16,20},{18,... | collective-permute-start | bytes 393224 | tf_op jit(solution)/shard_map/ppermute | solution.py:237
  21.6 6.1 %collective-permute-start.4 = (bf16[16,32,128]{2,1,0:T(8,128)(2,1)S(1)}, bf16[16,32,128]{2,1,0:T(8,128)(2,1)S(1)}, u32[]{:S(2)}, u32[]{:S(2)}) collective-permute-start(bf16[16,32,128]{2,1,0:T(8,128)(2,1)S(1)} %collective-permute-done.3.refs_4_), channel_id=1, source_target_pairs={{0,2},{2,0},{4,6},{6,4},{8,10},{10,8},{12,14},{14,12},{16,18},{18,... | collective-permute-start | bytes 393224 | tf_op jit(solution)/shard_map/ppermute | solution.py:237
  23.4 6.6 %collective-permute-start.13 = (bf16[16,32,128]{2,1,0:T(8,128)(2,1)S(1)}, bf16[16,32,128]{2,1,0:T(8,128)(2,1)S(1)}, u32[]{:S(2)}, u32[]{:S(2)}) collective-permute-start(bf16[16,32,128]{2,1,0:T(8,128)(2,1)S(1)} %collective-permute-done.11.refs_12_), channel_id=1, source_target_pairs={{0,4},{2,6},{4,0},{6,2},{8,12},{10,14},{12,8},{14,10},{16,20},{18,... | collective-permute-start | bytes 393224 | tf_op jit(solution)/shard_map/ppermute | solution.py:237
  24.9 5.0 %collective-permute-start.2 = (bf16[16,32,128]{2,1,0:T(8,128)(2,1)S(1)}, bf16[16,32,128]{2,1,0:T(8,128)(2,1)S(1)}, u32[]{:S(2)}, u32[]{:S(2)}) collective-permute-start(bf16[16,32,128]{2,1,0:T(8,128)(2,1)S(1)} %collective-permute-done.1.refs_2_), channel_id=1, source_target_pairs={{0,2},{2,0},{4,6},{6,4},{8,10},{10,8},{12,14},{14,12},{16,18},{18,... | collective-permute-start | bytes 393224 | tf_op jit(solution)/shard_map/ppermute | solution.py:237
  24.9 5.0 %collective-permute-start.12 = (bf16[16,32,128]{2,1,0:T(8,128)(2,1)S(1)}, bf16[16,32,128]{2,1,0:T(8,128)(2,1)S(1)}, u32[]{:S(2)}, u32[]{:S(2)}) collective-permute-start(bf16[16,32,128]{2,1,0:T(8,128)(2,1)S(1)} %collective-permute-done.11.refs_12_), channel_id=1, source_target_pairs={{0,2},{2,0},{4,6},{6,4},{8,10},{10,8},{12,14},{14,12},{16,18},{18,... | collective-permute-start | bytes 393224 | tf_op jit(solution)/shard_map/ppermute | solution.py:237
  27.7 2.3 %collective-permute-start.10 = (bf16[16,32,128]{2,1,0:T(8,128)(2,1)S(1)}, bf16[16,32,128]{2,1,0:T(8,128)(2,1)S(1)}, u32[]{:S(2)}, u32[]{:S(2)}) collective-permute-start(bf16[16,32,128]{2,1,0:T(8,128)(2,1)S(1)} %collective-permute-done.9.refs_10_), channel_id=1, source_target_pairs={{0,2},{2,0},{4,6},{6,4},{8,10},{10,8},{12,14},{14,12},{16,18},{18,... | collective-permute-start | bytes 393224 | tf_op jit(solution)/shard_map/ppermute | solution.py:237
  27.7 2.3 %collective-permute-start.6 = (bf16[16,32,128]{2,1,0:T(8,128)(2,1)S(1)}, bf16[16,32,128]{2,1,0:T(8,128)(2,1)S(1)}, u32[]{:S(2)}, u32[]{:S(2)}) collective-permute-start(bf16[16,32,128]{2,1,0:T(8,128)(2,1)S(1)} %collective-permute-done.5.refs_6_), channel_id=1, source_target_pairs={{0,2},{2,0},{4,6},{6,4},{8,10},{10,8},{12,14},{14,12},{16,18},{18,... | collective-permute-start | bytes 393224 | tf_op jit(solution)/shard_map/ppermute | solution.py:237
  29.9 1.3 %collective-permute-start.14 = (bf16[16,32,128]{2,1,0:T(8,128)(2,1)S(1)}, bf16[16,32,128]{2,1,0:T(8,128)(2,1)S(1)}, u32[]{:S(2)}, u32[]{:S(2)}) collective-permute-start(bf16[16,32,128]{2,1,0:T(8,128)(2,1)S(1)} %collective-permute-done.13.refs_14_), channel_id=1, source_target_pairs={{0,2},{2,0},{4,6},{6,4},{8,10},{10,8},{12,14},{14,12},{16,18},{18,... | collective-permute-start | bytes 393224 | tf_op jit(solution)/shard_map/ppermute | solution.py:237
  31.3 0.9 %copy-start = (bf16[16,32,128]{2,1,0:T(8,128)(2,1)S(1)}, bf16[16,32,128]{2,1,0:T(8,128)(2,1)}, u32[]{:S(2)}) copy-start(bf16[16,32,128]{2,1,0:T(8,128)(2,1)} %channelise.1.refs_0_) | copy-start | bytes 393220

commit v3 on v2

--- a/solution.py
+++ b/solution.py
@@ -72,6 +72,9 @@
     )
     products = (products * (1.0 / SPECTRA)).astype(jnp.bfloat16)
     return products.reshape(CH_DEV, 2, P_DEV, grid_cols, Q_DEV, col_set.shape[1])
+
+
+PITCH = 36
 
 
 def filter_table(chans):
@@ -196,8 +199,9 @@
     for p in range(P_DEV):
         for q in range(Q_DEV):
             weight = flags_s[q, p].astype(jnp.float32)
-            rows[pl.ds(q * P_DEV + p, CH_DEV, stride=LANES), :] = lanes[map_s[0, p * Q_DEV + q]] * weight
-    out[...] = rows[...].astype(jnp.bfloat16).reshape(CH_DEV, LANES, 2 * SPECTRA)
+            rows[pl.ds(q * P_DEV + p, CH_DEV, stride=PITCH), :] = lanes[map_s[0, p * Q_DEV + q]] * weight
+    for c in range(CH_DEV):
+        out[c] = rows[PITCH * c : PITCH * c + LANES].astype(jnp.bfloat16)
 
 
 def channelise(voltages, lane_map, input_flags):
@@ -218,11 +222,11 @@
             pltpu.VMEM((2, 35, 8, CHUNK), jnp.float32),
             pltpu.VMEM((2, 4 * SPECTRA, CHUNK), jnp.float32),
             pltpu.VMEM((LANES, CH_DEV, 2 * SPECTRA), jnp.float32),
-            pltpu.VMEM((CH_DEV * LANES, 2 * SPECTRA), jnp.float32),
+            pltpu.VMEM((CH_DEV * PITCH, 2 * SPECTRA), jnp.float32),
             pltpu.SemaphoreType.DMA((P_DEV,)),
             pltpu.SemaphoreType.DMA((3,)),
         ],
-        compiler_params=pltpu.CompilerParams(vmem_limit_bytes=56 << 20),
+        compiler_params=pltpu.CompilerParams(vmem_limit_bytes=50 << 20),
         name="channelise",
     )(
         volts,
@@ -232,20 +236,20 @@
     )
 
 
-def gather_rows(own):
+def gather(own):
     def swap(block, d):
         return lax.ppermute(block, "row", [(i, i ^ d) for i in range(ROWS)])
 
     blocks = {0: own}
-    blocks[8] = swap(own, 8)
-    blocks[4] = swap(own, 4)
-    blocks[2] = swap(own, 2)
-    blocks[12] = swap(blocks[8], 4)
-    for d in (4, 8, 12):
-        blocks[d + 2] = swap(blocks[d], 2)
+    for d in (8, 4, 2, 6):
+        blocks[d] = swap(own, d)
+    for d in (14, 12, 10):
+        blocks[d] = swap(blocks[8], d ^ 8)
     for d in range(0, ROWS, 2):
         blocks[d + 1] = swap(blocks[d], 1)
-    return [blocks[d] for d in range(ROWS)]
+    late, _ = lax.optimization_barrier((own, blocks[8]))
+    other = lax.ppermute(late, "col", [(0, 1), (1, 0)])
+    return [blocks[d] for d in range(ROWS)], other
 
 
 def correlate_kernel(*refs):
@@ -281,10 +285,11 @@
                 for part in range(2):
                     for q in range(2 * Q_DEV):
                         start = (part * 8 + q) * 8
-                        spread[slot, part, pl.ds(q * Q_DEV + 2 * h + k, 8, stride=32), :] = products[
+                        spread[slot, part, pl.ds(q * Q_DEV + 2 * h + k, 8, stride=PITCH), :] = products[
                             start : start + 8, k * 128 : k * 128 + 128
                         ]
-        packed[c] = spread[slot].astype(jnp.bfloat16)
+        for p in range(P_DEV):
+            packed[c, :, 32 * p : 32 * p + 32] = spread[slot, :, PITCH * p : PITCH * p + 32].astype(jnp.bfloat16)
         copy = pltpu.make_async_copy(packed.at[c], out.at[c], sem.at[c])
         copy.start()
         copies.append(copy)
@@ -301,7 +306,7 @@
         out_specs=pl.BlockSpec(memory_space=pltpu.HBM),
         scratch_shapes=[
             pltpu.VMEM((2, Q_DEV, 8 * ROWS, 2 * SPECTRA), jnp.bfloat16),
-            pltpu.VMEM((2, 2, 2 * LANES * Q_DEV, 8 * ROWS), jnp.float32),
+            pltpu.VMEM((2, 2, P_DEV * PITCH, 8 * ROWS), jnp.float32),
             pltpu.VMEM((CH_DEV, 2, 2 * LANES * Q_DEV, 8 * ROWS), jnp.bfloat16),
             pltpu.SemaphoreType.DMA((CH_DEV,)),
         ],
@@ -312,8 +317,7 @@
 
 def per_device(voltages, lane_map, input_flags):
     own = channelise(voltages, lane_map, input_flags)
-    other = lax.ppermute(own, "col", [(0, 1), (1, 0)])
-    products = correlate(gather_rows(own), other)
+    products = correlate(*gather(own))
     return products.reshape(CH_DEV, 2, P_DEV, 2 * Q_DEV, Q_DEV, P_DEV * ROWS)
 
 

time: 36.7 us -> 33.4 us (0.910)
  Pallas kernels: 12 us -> 8.06 us
  local copies, waits for them, and re-layouts: 0.9 us -> 2.38 us
  starting transfers between devices: 14.4 us -> 13.1 us
  waiting for transfers between devices: 9.11 us -> 9.57 us
    pallas_call x1, Pallas kernels: 4.33 us -> 2.02 us  [correlate(): pl.pallas_call(correlate_kernel, out_shape=jax.ShapeDtypeStruct((CH_DEV,...]
    pallas_call x1, Pallas kernels: 7.68 us -> 6.04 us  [channelise(): pl.pallas_call(filter_kernel, out_shape=jax.ShapeDtypeStruct((CH_DEV, LAN...]
    unnamed x2 -> x6, local copies, waits for them, and re-layouts: 0.9 us -> 2.38 us
    ppermute x15, starting transfers between devices: 12.9 us -> 11.5 us  [swap(): return lax.ppermute(block, 'row', [(i, i ^ d) for i in range(ROWS)])]
    ppermute x15, waiting for transfers between devices: 9.1 us -> 9.57 us  [swap(): return lax.ppermute(block, 'row', [(i, i ^ d) for i in range(ROWS)])]
  transfers between devices with their start and end apart: 16 -> 16, of which waited for: 5 -> 10; matrix products, arithmetic and copies ran while one was open for 0% -> 0% of each run, Pallas kernels for 0% -> 0%
where the time goes in v3:
time: 33.4 us; the launch traced here: 33.2 us
  starting transfers between devices  13.1 us (39%)
  waiting for transfers between devices  9.57 us (29%)
  Pallas kernels  8.06 us (24%)
  local copies, waits for them, and re-layouts  2.38 us (7%)
    ppermute x15, starting transfers between devices, swap(): return lax.ppermute(block, 'row', [(i, i ^ d) for i in range(ROWS)])  11.5 us
    ppermute x15, waiting for transfers between devices, swap(): return lax.ppermute(block, 'row', [(i, i ^ d) for i in range(ROWS)])  9.57 us
    pallas_call x1, Pallas kernels, channelise(): pl.pallas_call(filter_kernel, out_shape=jax.ShapeDtypeStruct((CH_DEV, LAN...  6.04 us
    unnamed x6, local copies, waits for them, and re-layouts  2.38 us
    pallas_call x1, Pallas kernels, correlate(): pl.pallas_call(correlate_kernel, out_shape=jax.ShapeDtypeStruct((CH_DEV,...  2.02 us
    ppermute x1, starting transfers between devices, gather(): other = lax.ppermute(late, 'col', [(0, 1), (1, 0)])  1.6 us
  transfers between devices with their start and end apart: 16, of which 10 were waited for; matrix products, arithmetic and copies ran while one was open for 0% of the time, Pallas kernels for 0%

profile of v3, /device:TPU:0, one launch (start us, length us, event | category | flops | bytes accessed | tf_op | source)
XLA Modules:
  0.0 33.2 jit_solution(5232860004689449665)
XLA Ops:
  0.0 0.0 copy-start
  0.0 1.0 %copy-done = bf16[1024,256]{1,0:T(8,128)(2,1)S(1)} copy-done((bf16[1024,256]{1,0:T(8,128)(2,1)S(1)}, bf16[1024,256]{1,0:T(8,128)(2,1)}, u32[]{:S(2)}) %copy-start) | copy-done | bytes 524312
  1.0 0.0 copy-start.1
  1.0 0.7 %copy-done.1 = s32[8,4]{0,1:T(4,128)S(1)} copy-done((s32[8,4]{0,1:T(4,128)S(1)}, s32[8,4]{0,1:T(4,128)}, u32[]{:S(2)}) %copy-start.1) | copy-done | bytes 152
  1.7 0.0 copy-start.2
  1.7 0.7 %copy-done.2 = s32[1,1,32]{2,1,0:T(1,128)S(1)} copy-done((s32[1,1,32]{2,1,0:T(1,128)S(1)}, s32[1,1,32]{2,1,0:T(1,128)}, u32[]{:S(2)}) %copy-start.2) | copy-done | bytes 152
  2.4 6.0 %channelise.1.refs_0_ = bf16[16,32,128]{2,1,0:T(8,128)(2,1)S(1)} custom-call(bf16[8,67,8,8,128]{4,3,2,1,0:T(8,128)(2,1)} %bitcast.10, bf16[1024,256]{1,0:T(8,128)(2,1)S(1)} %copy-done, s32[1,32]{1,0:T(1,128)S(1)} %bitcast.9, s32[4,8]{1,0:T(4,128)S(1)} %bitcast.8), custom_call_target="tpu_custom_call" | custom-call | tf_op jit(solution)/shard_map/channelise/pallas_call | solution.py:212
  8.4 4.1 %collective-permute-start.7 = (bf16[16,32,128]{2,1,0:T(8,128)(2,1)S(1)}, bf16[16,32,128]{2,1,0:T(8,128)(2,1)S(1)}, u32[]{:S(2)}, u32[]{:S(2)}) collective-permute-start(bf16[16,32,128]{2,1,0:T(8,128)(2,1)S(1)} %channelise.1.refs_0_), channel_id=1, source_target_pairs={{0,16},{2,18},{4,20},{6,22},{8,24},{10,26},{12,28},{14,30},{16,0},... | collective-permute-start | bytes 393224 | tf_op jit(solution)/shard_map/ppermute | solution.py:241
  12.5 2.5 %collective-permute-start.5 = (bf16[16,32,128]{2,1,0:T(8,128)(2,1)S(1)}, bf16[16,32,128]{2,1,0:T(8,128)(2,1)S(1)}, u32[]{:S(2)}, u32[]{:S(2)}) collective-permute-start(bf16[16,32,128]{2,1,0:T(8,128)(2,1)S(1)} %channelise.1.refs_0_), channel_id=1, source_target_pairs={{0,12},{2,14},{4,8},{6,10},{8,4},{10,6},{12,0},{14,2},{16,28},{18,... | collective-permute-start | bytes 393224 | tf_op jit(solution)/shard_map/ppermute | solution.py:241
  15.0 0.5 %collective-permute-start.3 = (bf16[16,32,128]{2,1,0:T(8,128)(2,1)S(1)}, bf16[16,32,128]{2,1,0:T(8,128)(2,1)S(1)}, u32[]{:S(2)}, u32[]{:S(2)}) collective-permute-start(bf16[16,32,128]{2,1,0:T(8,128)(2,1)S(1)} %channelise.1.refs_0_), channel_id=1, source_target_pairs={{0,8},{2,10},{4,12},{6,14},{8,0},{10,2},{12,4},{14,6},{16,24},{18,... | collective-permute-start | bytes 393224 | tf_op jit(solution)/shard_map/ppermute | solution.py:241
  15.5 0.5 %collective-permute-start.1 = (bf16[16,32,128]{2,1,0:T(8,128)(2,1)S(1)}, bf16[16,32,128]{2,1,0:T(8,128)(2,1)S(1)}, u32[]{:S(2)}, u32[]{:S(2)}) collective-permute-start(bf16[16,32,128]{2,1,0:T(8,128)(2,1)S(1)} %channelise.1.refs_0_), channel_id=1, source_target_pairs={{0,4},{2,6},{4,0},{6,2},{8,12},{10,14},{12,8},{14,10},{16,20},{18,... | collective-permute-start | bytes 393224 | tf_op jit(solution)/shard_map/ppermute | solution.py:241
  16.0 0.0 collective-permute-start
  16.0 2.9 %collective-permute-done.7.refs_8_ = bf16[16,32,128]{2,1,0:T(8,128)(2,1)S(1)} collective-permute-done((bf16[16,32,128]{2,1,0:T(8,128)(2,1)S(1)}, bf16[16,32,128]{2,1,0:T(8,128)(2,1)S(1)}, u32[]{:S(2)}, u32[]{:S(2)}) %collective-permute-start.7) | collective-permute-done | bytes 131104 | tf_op jit(solution)/shard_map/ppermute | solution.py:241
  18.9 1.6 %collective-permute-start.15 = (bf16[16,32,128]{2,1,0:T(8,128)(2,1)S(1)}, bf16[16,32,128]{2,1,0:T(8,128)(2,1)S(1)}, u32[]{:S(2)}, u32[]{:S(2)}) collective-permute-start(bf16[16,32,128]{2,1,0:T(8,128)(2,1)S(1)} %channelise.1.refs_0_), channel_id=1, source_target_pairs={{0,1},{1,0},{2,3},{3,2},{4,5},{5,4},{6,7},{7,6},{8,9},{9,8},{10,11... | collective-permute-start | bytes 393224 | tf_op jit(solution)/shard_map/ppermute | solution.py:251
  20.5 0.9 %collective-permute-done.5.refs_6_ = bf16[16,32,128]{2,1,0:T(8,128)(2,1)S(1)} collective-permute-done((bf16[16,32,128]{2,1,0:T(8,128)(2,1)S(1)}, bf16[16,32,128]{2,1,0:T(8,128)(2,1)S(1)}, u32[]{:S(2)}, u32[]{:S(2)}) %collective-permute-start.5) | collective-permute-done | bytes 131104 | tf_op jit(solution)/shard_map/ppermute | solution.py:241
  21.5 0.9 %collective-permute-start.13 = (bf16[16,32,128]{2,1,0:T(8,128)(2,1)S(1)}, bf16[16,32,128]{2,1,0:T(8,128)(2,1)S(1)}, u32[]{:S(2)}, u32[]{:S(2)}) collective-permute-start(bf16[16,32,128]{2,1,0:T(8,128)(2,1)S(1)} %collective-permute-done.7.refs_8_), channel_id=1, source_target_pairs={{0,12},{2,14},{4,8},{6,10},{8,4},{10,6},{12,0},{14,2},{16,28},{18,... | collective-permute-start | bytes 393224 | tf_op jit(solution)/shard_map/ppermute | solution.py:241
  22.4 0.6 %collective-permute-done.3.refs_4_ = bf16[16,32,128]{2,1,0:T(8,128)(2,1)S(1)} collective-permute-done((bf16[16,32,128]{2,1,0:T(8,128)(2,1)S(1)}, bf16[16,32,128]{2,1,0:T(8,128)(2,1)S(1)}, u32[]{:S(2)}, u32[]{:S(2)}) %collective-permute-start.3) | collective-permute-done | bytes 131104 | tf_op jit(solution)/shard_map/ppermute | solution.py:241
  23.0 1.0 %collective-permute-start.11 = (bf16[16,32,128]{2,1,0:T(8,128)(2,1)S(1)}, bf16[16,32,128]{2,1,0:T(8,128)(2,1)S(1)}, u32[]{:S(2)}, u32[]{:S(2)}) collective-permute-start(bf16[16,32,128]{2,1,0:T(8,128)(2,1)S(1)} %collective-permute-done.7.refs_8_), channel_id=1, source_target_pairs={{0,8},{2,10},{4,12},{6,14},{8,0},{10,2},{12,4},{14,6},{16,24},{18,... | collective-permute-start | bytes 393224 | tf_op jit(solution)/shard_map/ppermute | solution.py:241
  24.0 0.0 collective-permute-done.1.refs_2_
  24.0 0.9 %collective-permute-start.9 = (bf16[16,32,128]{2,1,0:T(8,128)(2,1)S(1)}, bf16[16,32,128]{2,1,0:T(8,128)(2,1)S(1)}, u32[]{:S(2)}, u32[]{:S(2)}) collective-permute-start(bf16[16,32,128]{2,1,0:T(8,128)(2,1)S(1)} %collective-permute-done.7.refs_8_), channel_id=1, source_target_pairs={{0,4},{2,6},{4,0},{6,2},{8,12},{10,14},{12,8},{14,10},{16,20},{18,... | collective-permute-start | bytes 393224 | tf_op jit(solution)/shard_map/ppermute | solution.py:241
  25.0 0.0 collective-permute-done.refs_1_
  25.0 0.0 collective-permute-start.8
  25.0 0.0 collective-permute-done.15.refs_16_
  25.0 0.5 %collective-permute-start.6 = (bf16[16,32,128]{2,1,0:T(8,128)(2,1)S(1)}, bf16[16,32,128]{2,1,0:T(8,128)(2,1)S(1)}, u32[]{:S(2)}, u32[]{:S(2)}) collective-permute-start(bf16[16,32,128]{2,1,0:T(8,128)(2,1)S(1)} %collective-permute-done.5.refs_6_), channel_id=1, source_target_pairs={{0,2},{2,0},{4,6},{6,4},{8,10},{10,8},{12,14},{14,12},{16,18},{18,... | collective-permute-start | bytes 393224 | tf_op jit(solution)/shard_map/ppermute | solution.py:241
  25.5 2.0 %collective-permute-done.13.refs_14_ = bf16[16,32,128]{2,1,0:T(8,128)(2,1)S(1)} collective-permute-done((bf16[16,32,128]{2,1,0:T(8,128)(2,1)S(1)}, bf16[16,32,128]{2,1,0:T(8,128)(2,1)S(1)}, u32[]{:S(2)}, u32[]{:S(2)}) %collective-permute-start.13) | collective-permute-done | bytes 131104 | tf_op jit(solution)/shard_map/ppermute | solution.py:241
  27.4 0.0 collective-permute-start.4
  27.4 1.3 %collective-permute-done.11.refs_12_ = bf16[16,32,128]{2,1,0:T(8,128)(2,1)S(1)} collective-permute-done((bf16[16,32,128]{2,1,0:T(8,128)(2,1)S(1)}, bf16[16,32,128]{2,1,0:T(8,128)(2,1)S(1)}, u32[]{:S(2)}, u32[]{:S(2)}) %collective-permute-start.11) | collective-permute-done | bytes 131104 | tf_op jit(solution)/shard_map/ppermute | solution.py:241
  28.8 0.0 collective-permute-start.2
  28.8 0.5 %collective-permute-done.9.refs_10_ = bf16[16,32,128]{2,1,0:T(8,128)(2,1)S(1)} collective-permute-done((bf16[16,32,128]{2,1,0:T(8,128)(2,1)S(1)}, bf16[16,32,128]{2,1,0:T(8,128)(2,1)S(1)}, u32[]{:S(2)}, u32[]{:S(2)}) %collective-permute-start.9) | collective-permute-done | bytes 131104 | tf_op jit(solution)/shard_map/ppermute | solution.py:241
  29.3 0.0 collective-permute-start.14
  29.3 0.0 collective-permute-done.8.refs_9_
  29.3 0.5 %collective-permute-start.12 = (bf16[16,32,128]{2,1,0:T(8,128)(2,1)S(1)}, bf16[16,32,128]{2,1,0:T(8,128)(2,1)S(1)}, u32[]{:S(2)}, u32[]{:S(2)}) collective-permute-start(bf16[16,32,128]{2,1,0:T(8,128)(2,1)S(1)} %collective-permute-done.11.refs_12_), channel_id=1, source_target_pairs={{0,2},{2,0},{4,6},{6,4},{8,10},{10,8},{12,14},{14,12},{16,18},{18,... | collective-permute-start | bytes 393224 | tf_op jit(solution)/shard_map/ppermute | solution.py:241
  29.8 0.0 collective-permute-done.6.refs_7_
  29.8 0.1 collective-permute-start.10
  29.9 0.0 collective-permute-done.4.refs_5_
  29.9 0.3 collective-permute-done.2.refs_3_
  30.1 0.5 %collective-permute-done.14.refs_15_ = bf16[16,32,128]{2,1,0:T(8,128)(2,1)S(1)} collective-permute-done((bf16[16,32,128]{2,1,0:T(8,128)(2,1)S(1)}, bf16[16,32,128]{2,1,0:T(8,128)(2,1)S(1)}, u32[]{:S(2)}, u32[]{:S(2)}) %collective-permute-start.14) | collective-permute-done | bytes 131104 | tf_op jit(solution)/shard_map/ppermute | solution.py:241
  30.6 0.2 collective-permute-done.12.refs_13_
  30.8 0.3 collective-permute-done.10.refs_11_
  31.1 2.0 %correlate.1 = bf16[16,2,256,128]{3,2,1,0:T(8,128)(2,1)} custom-call(bf16[16,32,128]{2,1,0:T(8,128)(2,1)S(1)} %channelise.1.refs_0_, bf16[16,32,128]{2,1,0:T(8,128)(2,1)S(1)} %collective-permute-done.refs_1_, bf16[16,32,128]{2,1,0:T(8,128)(2,1)S(1)} %collective-permute-done.1.refs_2_, bf16[16,32,128]{2,1,0:T(8,128)(2,1)S(1)} %collective-permute-done.2.refs_3_, ...), custom_call_target="tpu_custom_call" | custom-call | tf_op jit(solution)/shard_map/correlate/pallas_call | solution.py:302
Async XLA Ops:
  0.0 1.0 %copy-start = (bf16[1024,256]{1,0:T(8,128)(2,1)S(1)}, bf16[1024,256]{1,0:T(8,128)(2,1)}, u32[]{:S(2)}) copy-start(bf16[1024,256]{1,0:T(8,128)(2,1)} %constant.2.clone.table) | copy-start | bytes 1572868
  1.0 0.7 %copy-start.1 = (s32[8,4]{0,1:T(4,128)S(1)}, s32[8,4]{0,1:T(4,128)}, u32[]{:S(2)}) copy-start(s32[8,4]{0,1:T(4,128)} %param.6) | copy-start | bytes 388
  1.7 0.7 %copy-start.2 = (s32[1,1,32]{2,1,0:T(1,128)S(1)}, s32[1,1,32]{2,1,0:T(1,128)}, u32[]{:S(2)}) copy-start(s32[1,1,32]{2,1,0:T(1,128)} %param.5) | copy-start | bytes 388
  8.4 10.5 %collective-permute-start.7 = (bf16[16,32,128]{2,1,0:T(8,128)(2,1)S(1)}, bf16[16,32,128]{2,1,0:T(8,128)(2,1)S(1)}, u32[]{:S(2)}, u32[]{:S(2)}) collective-permute-start(bf16[16,32,128]{2,1,0:T(8,128)(2,1)S(1)} %channelise.1.refs_0_), channel_id=1, source_target_pairs={{0,16},{2,18},{4,20},{6,22},{8,24},{10,26},{12,28},{14,30},{16,0},... | collective-permute-start | bytes 393224 | tf_op jit(solution)/shard_map/ppermute | solution.py:241
  12.5 8.9 %collective-permute-start.5 = (bf16[16,32,128]{2,1,0:T(8,128)(2,1)S(1)}, bf16[16,32,128]{2,1,0:T(8,128)(2,1)S(1)}, u32[]{:S(2)}, u32[]{:S(2)}) collective-permute-start(bf16[16,32,128]{2,1,0:T(8,128)(2,1)S(1)} %channelise.1.refs_0_), channel_id=1, source_target_pairs={{0,12},{2,14},{4,8},{6,10},{8,4},{10,6},{12,0},{14,2},{16,28},{18,... | collective-permute-start | bytes 393224 | tf_op jit(solution)/shard_map/ppermute | solution.py:241
  15.0 8.0 %collective-permute-start.3 = (bf16[16,32,128]{2,1,0:T(8,128)(2,1)S(1)}, bf16[16,32,128]{2,1,0:T(8,128)(2,1)S(1)}, u32[]{:S(2)}, u32[]{:S(2)}) collective-permute-start(bf16[16,32,128]{2,1,0:T(8,128)(2,1)S(1)} %channelise.1.refs_0_), channel_id=1, source_target_pairs={{0,8},{2,10},{4,12},{6,14},{8,0},{10,2},{12,4},{14,6},{16,24},{18,... | collective-permute-start | bytes 393224 | tf_op jit(solution)/shard_map/ppermute | solution.py:241
  15.5 8.5 %collective-permute-start.1 = (bf16[16,32,128]{2,1,0:T(8,128)(2,1)S(1)}, bf16[16,32,128]{2,1,0:T(8,128)(2,1)S(1)}, u32[]{:S(2)}, u32[]{:S(2)}) collective-permute-start(bf16[16,32,128]{2,1,0:T(8,128)(2,1)S(1)} %channelise.1.refs_0_), channel_id=1, source_target_pairs={{0,4},{2,6},{4,0},{6,2},{8,12},{10,14},{12,8},{14,10},{16,20},{18,... | collective-permute-start | bytes 393224 | tf_op jit(solution)/shard_map/ppermute | solution.py:241
  16.0 9.0 %collective-permute-start = (bf16[16,32,128]{2,1,0:T(8,128)(2,1)S(1)}, bf16[16,32,128]{2,1,0:T(8,128)(2,1)S(1)}, u32[]{:S(2)}, u32[]{:S(2)}) collective-permute-start(bf16[16,32,128]{2,1,0:T(8,128)(2,1)S(1)} %channelise.1.refs_0_), channel_id=1, source_target_pairs={{0,2},{2,0},{4,6},{6,4},{8,10},{10,8},{12,14},{14,12},{16,18},{18,... | collective-permute-start | bytes 393224 | tf_op jit(solution)/shard_map/ppermute | solution.py:241
  18.9 6.0 %collective-permute-start.15 = (bf16[16,32,128]{2,1,0:T(8,128)(2,1)S(1)}, bf16[16,32,128]{2,1,0:T(8,128)(2,1)S(1)}, u32[]{:S(2)}, u32[]{:S(2)}) collective-permute-start(bf16[16,32,128]{2,1,0:T(8,128)(2,1)S(1)} %channelise.1.refs_0_), channel_id=1, source_target_pairs={{0,1},{1,0},{2,3},{3,2},{4,5},{5,4},{6,7},{7,6},{8,9},{9,8},{10,11... | collective-permute-start | bytes 393224 | tf_op jit(solution)/shard_map/ppermute | solution.py:251
  21.5 6.0 %collective-permute-start.13 = (bf16[16,32,128]{2,1,0:T(8,128)(2,1)S(1)}, bf16[16,32,128]{2,1,0:T(8,128)(2,1)S(1)}, u32[]{:S(2)}, u32[]{:S(2)}) collective-permute-start(bf16[16,32,128]{2,1,0:T(8,128)(2,1)S(1)} %collective-permute-done.7.refs_8_), channel_id=1, source_target_pairs={{0,12},{2,14},{4,8},{6,10},{8,4},{10,6},{12,0},{14,2},{16,28},{18,... | collective-permute-start | bytes 393224 | tf_op jit(solution)/shard_map/ppermute | solution.py:241
  23.0 5.7 %collective-permute-start.11 = (bf16[16,32,128]{2,1,0:T(8,128)(2,1)S(1)}, bf16[16,32,128]{2,1,0:T(8,128)(2,1)S(1)}, u32[]{:S(2)}, u32[]{:S(2)}) collective-permute-start(bf16[16,32,128]{2,1,0:T(8,128)(2,1)S(1)} %collective-permute-done.7.refs_8_), channel_id=1, source_target_pairs={{0,8},{2,10},{4,12},{6,14},{8,0},{10,2},{12,4},{14,6},{16,24},{18,... | collective-permute-start | bytes 393224 | tf_op jit(solution)/shard_map/ppermute | solution.py:241
  24.0 5.2 %collective-permute-start.9 = (bf16[16,32,128]{2,1,0:T(8,128)(2,1)S(1)}, bf16[16,32,128]{2,1,0:T(8,128)(2,1)S(1)}, u32[]{:S(2)}, u32[]{:S(2)}) collective-permute-start(bf16[16,32,128]{2,1,0:T(8,128)(2,1)S(1)} %collective-permute-done.7.refs_8_), channel_id=1, source_target_pairs={{0,4},{2,6},{4,0},{6,2},{8,12},{10,14},{12,8},{14,10},{16,20},{18,... | collective-permute-start | bytes 393224 | tf_op jit(solution)/shard_map/ppermute | solution.py:241
  25.0 4.3 %collective-permute-start.8 = (bf16[16,32,128]{2,1,0:T(8,128)(2,1)S(1)}, bf16[16,32,128]{2,1,0:T(8,128)(2,1)S(1)}, u32[]{:S(2)}, u32[]{:S(2)}) collective-permute-start(bf16[16,32,128]{2,1,0:T(8,128)(2,1)S(1)} %collective-permute-done.7.refs_8_), channel_id=1, source_target_pairs={{0,2},{2,0},{4,6},{6,4},{8,10},{10,8},{12,14},{14,12},{16,18},{18,... | collective-permute-start | bytes 393224 | tf_op jit(solution)/shard_map/ppermute | solution.py:241
  25.0 4.8 %collective-permute-start.6 = (bf16[16,32,128]{2,1,0:T(8,128)(2,1)S(1)}, bf16[16,32,128]{2,1,0:T(8,128)(2,1)S(1)}, u32[]{:S(2)}, u32[]{:S(2)}) collective-permute-start(bf16[16,32,128]{2,1,0:T(8,128)(2,1)S(1)} %collective-permute-done.5.refs_6_), channel_id=1, source_target_pairs={{0,2},{2,0},{4,6},{6,4},{8,10},{10,8},{12,14},{14,12},{16,18},{18,... | collective-permute-start | bytes 393224 | tf_op jit(solution)/shard_map/ppermute | solution.py:241
  27.4 2.4 %collective-permute-start.4 = (bf16[16,32,128]{2,1,0:T(8,128)(2,1)S(1)}, bf16[16,32,128]{2,1,0:T(8,128)(2,1)S(1)}, u32[]{:S(2)}, u32[]{:S(2)}) collective-permute-start(bf16[16,32,128]{2,1,0:T(8,128)(2,1)S(1)} %collective-permute-done.3.refs_4_), channel_id=1, source_target_pairs={{0,2},{2,0},{4,6},{6,4},{8,10},{10,8},{12,14},{14,12},{16,18},{18,... | collective-permute-start | bytes 393224 | tf_op jit(solution)/shard_map/ppermute | solution.py:241
  28.8 1.3 %collective-permute-start.2 = (bf16[16,32,128]{2,1,0:T(8,128)(2,1)S(1)}, bf16[16,32,128]{2,1,0:T(8,128)(2,1)S(1)}, u32[]{:S(2)}, u32[]{:S(2)}) collective-permute-start(bf16[16,32,128]{2,1,0:T(8,128)(2,1)S(1)} %collective-permute-done.1.refs_2_), channel_id=1, source_target_pairs={{0,2},{2,0},{4,6},{6,4},{8,10},{10,8},{12,14},{14,12},{16,18},{18,... | collective-permute-start | bytes 393224 | tf_op jit(solution)/shard_map/ppermute | solution.py:241
  29.3 1.3 %collective-permute-start.14 = (bf16[16,32,128]{2,1,0:T(8,128)(2,1)S(1)}, bf16[16,32,128]{2,1,0:T(8,128)(2,1)S(1)}, u32[]{:S(2)}, u32[]{:S(2)}) collective-permute-start(bf16[16,32,128]{2,1,0:T(8,128)(2,1)S(1)} %collective-permute-done.13.refs_14_), channel_id=1, source_target_pairs={{0,2},{2,0},{4,6},{6,4},{8,10},{10,8},{12,14},{14,12},{16,18},{18,... | collective-permute-start | bytes 393224 | tf_op jit(solution)/shard_map/ppermute | solution.py:241
  29.3 1.5 %collective-permute-start.12 = (bf16[16,32,128]{2,1,0:T(8,128)(2,1)S(1)}, bf16[16,32,128]{2,1,0:T(8,128)(2,1)S(1)}, u32[]{:S(2)}, u32[]{:S(2)}) collective-permute-start(bf16[16,32,128]{2,1,0:T(8,128)(2,1)S(1)} %collective-permute-done.11.refs_12_), channel_id=1, source_target_pairs={{0,2},{2,0},{4,6},{6,4},{8,10},{10,8},{12,14},{14,12},{16,18},{18,... | collective-permute-start | bytes 393224 | tf_op jit(solution)/shard_map/ppermute | solution.py:241
  29.8 1.3 %collective-permute-start.10 = (bf16[16,32,128]{2,1,0:T(8,128)(2,1)S(1)}, bf16[16,32,128]{2,1,0:T(8,128)(2,1)S(1)}, u32[]{:S(2)}, u32[]{:S(2)}) collective-permute-start(bf16[16,32,128]{2,1,0:T(8,128)(2,1)S(1)} %collective-permute-done.9.refs_10_), channel_id=1, source_target_pairs={{0,2},{2,0},{4,6},{6,4},{8,10},{10,8},{12,14},{14,12},{16,18},{18,... | collective-permute-start | bytes 393224 | tf_op jit(solution)/shard_map/ppermute | solution.py:241

commit v4 on v3

--- a/solution.py
+++ b/solution.py
@@ -226,7 +226,7 @@
             pltpu.SemaphoreType.DMA((P_DEV,)),
             pltpu.SemaphoreType.DMA((3,)),
         ],
-        compiler_params=pltpu.CompilerParams(vmem_limit_bytes=50 << 20),
+        compiler_params=pltpu.CompilerParams(vmem_limit_bytes=56 << 20),
         name="channelise",
     )(
         volts,
@@ -249,6 +249,7 @@
         blocks[d + 1] = swap(blocks[d], 1)
     late, _ = lax.optimization_barrier((own, blocks[8]))
     other = lax.ppermute(late, "col", [(0, 1), (1, 0)])
+    blocks[0] = swap(blocks[1], 1)
     return [blocks[d] for d in range(ROWS)], other
 
 

time: 33.4 us -> 32.7 us (0.979)
  local copies, waits for them, and re-layouts: 2.38 us -> 0 us
  Pallas kernels: 8.06 us -> 9.5 us
  starting transfers between devices: 13.1 us -> 13.6 us
    unnamed x6 -> x0, local copies, waits for them, and re-layouts: 2.38 us -> none
    pallas_call x1, Pallas kernels: 6.04 us -> 7.48 us  [channelise(): pl.pallas_call(filter_kernel, out_shape=jax.ShapeDtypeStruct((CH_DEV, LAN...]
    ppermute x15 -> x16, starting transfers between devices: 11.5 us -> 12 us  [swap(): return lax.ppermute(block, 'row', [(i, i ^ d) for i in range(ROWS)])]
    ppermute x15 -> x16, waiting for transfers between devices: 9.57 us -> 9.45 us  [swap(): return lax.ppermute(block, 'row', [(i, i ^ d) for i in range(ROWS)])]
  transfers between devices with their start and end apart: 16 -> 17, of which waited for: 10 -> 10; matrix products, arithmetic and copies ran while one was open for 0% -> 0% of each run, Pallas kernels for 0% -> 0%
where the time goes in v4:
time: 32.7 us; the launch traced here: 32.6 us
  starting transfers between devices  13.6 us (42%)
  Pallas kernels  9.5 us (29%)
  waiting for transfers between devices  9.45 us (29%)
    ppermute x16, starting transfers between devices, swap(): return lax.ppermute(block, 'row', [(i, i ^ d) for i in range(ROWS)])  12 us
    ppermute x16, waiting for transfers between devices, swap(): return lax.ppermute(block, 'row', [(i, i ^ d) for i in range(ROWS)])  9.45 us
    pallas_call x1, Pallas kernels, channelise(): pl.pallas_call(filter_kernel, out_shape=jax.ShapeDtypeStruct((CH_DEV, LAN...  7.48 us
    pallas_call x1, Pallas kernels, correlate(): pl.pallas_call(correlate_kernel, out_shape=jax.ShapeDtypeStruct((CH_DEV,...  2.01 us
    ppermute x1, starting transfers between devices, gather(): other = lax.ppermute(late, 'col', [(0, 1), (1, 0)])  1.58 us
  transfers between devices with their start and end apart: 17, of which 10 were waited for; matrix products, arithmetic and copies ran while one was open for 0% of the time, Pallas kernels for 0%

profile of v4, /device:TPU:0, one launch (start us, length us, event | category | flops | bytes accessed | tf_op | source)
XLA Modules:
  0.0 32.6 jit_solution(13787685139493549143)
XLA Ops:
  0.0 7.5 %channelise.1 = bf16[16,32,128]{2,1,0:T(8,128)(2,1)} custom-call(bf16[8,67,8,8,128]{4,3,2,1,0:T(8,128)(2,1)} %bitcast.8, bf16[1024,256]{1,0:T(8,128)(2,1)} %constant.2.clone.table, s32[1,32]{1,0:T(1,128)} %bitcast.10, s32[4,8]{1,0:T(4,128)} %bitcast.9), custom_call_target="tpu_custom_call" | custom-call | tf_op jit(solution)/shard_map/channelise/pallas_call | solution.py:212
  7.5 4.1 %collective-permute-start.8 = (bf16[16,32,128]{2,1,0:T(8,128)(2,1)}, bf16[16,32,128]{2,1,0:T(8,128)(2,1)S(1)}, u32[]{:S(2)}, u32[]{:S(2)}) collective-permute-start(bf16[16,32,128]{2,1,0:T(8,128)(2,1)} %channelise.1), channel_id=1, source_target_pairs={{0,16},{2,18},{4,20},{6,22},{8,24},{10,26},{12,28},{14,30},{16,0},... | collective-permute-start | bytes 393224 | tf_op jit(solution)/shard_map/ppermute | solution.py:241
  11.6 2.5 %collective-permute-start.6 = (bf16[16,32,128]{2,1,0:T(8,128)(2,1)}, bf16[16,32,128]{2,1,0:T(8,128)(2,1)S(1)}, u32[]{:S(2)}, u32[]{:S(2)}) collective-permute-start(bf16[16,32,128]{2,1,0:T(8,128)(2,1)} %channelise.1), channel_id=1, source_target_pairs={{0,12},{2,14},{4,8},{6,10},{8,4},{10,6},{12,0},{14,2},{16,28},{18,... | collective-permute-start | bytes 393224 | tf_op jit(solution)/shard_map/ppermute | solution.py:241
  14.1 0.4 %collective-permute-start.4 = (bf16[16,32,128]{2,1,0:T(8,128)(2,1)}, bf16[16,32,128]{2,1,0:T(8,128)(2,1)S(1)}, u32[]{:S(2)}, u32[]{:S(2)}) collective-permute-start(bf16[16,32,128]{2,1,0:T(8,128)(2,1)} %channelise.1), channel_id=1, source_target_pairs={{0,8},{2,10},{4,12},{6,14},{8,0},{10,2},{12,4},{14,6},{16,24},{18,... | collective-permute-start | bytes 393224 | tf_op jit(solution)/shard_map/ppermute | solution.py:241
  14.5 0.5 %collective-permute-start.2 = (bf16[16,32,128]{2,1,0:T(8,128)(2,1)}, bf16[16,32,128]{2,1,0:T(8,128)(2,1)S(1)}, u32[]{:S(2)}, u32[]{:S(2)}) collective-permute-start(bf16[16,32,128]{2,1,0:T(8,128)(2,1)} %channelise.1), channel_id=1, source_target_pairs={{0,4},{2,6},{4,0},{6,2},{8,12},{10,14},{12,8},{14,10},{16,20},{18,... | collective-permute-start | bytes 393224 | tf_op jit(solution)/shard_map/ppermute | solution.py:241
  15.1 0.0 collective-permute-start
  15.1 3.1 %collective-permute-done.8.refs_8_ = bf16[16,32,128]{2,1,0:T(8,128)(2,1)S(1)} collective-permute-done((bf16[16,32,128]{2,1,0:T(8,128)(2,1)}, bf16[16,32,128]{2,1,0:T(8,128)(2,1)S(1)}, u32[]{:S(2)}, u32[]{:S(2)}) %collective-permute-start.8) | collective-permute-done | bytes 131104 | tf_op jit(solution)/shard_map/ppermute | solution.py:241
  18.2 1.6 %collective-permute-start.16 = (bf16[16,32,128]{2,1,0:T(8,128)(2,1)}, bf16[16,32,128]{2,1,0:T(8,128)(2,1)S(1)}, u32[]{:S(2)}, u32[]{:S(2)}) collective-permute-start(bf16[16,32,128]{2,1,0:T(8,128)(2,1)} %channelise.1), channel_id=1, source_target_pairs={{0,1},{1,0},{2,3},{3,2},{4,5},{5,4},{6,7},{7,6},{8,9},{9,8},{10,11... | collective-permute-start | bytes 393224 | tf_op jit(solution)/shard_map/ppermute | solution.py:251
  19.8 1.0 %collective-permute-done.6.refs_6_ = bf16[16,32,128]{2,1,0:T(8,128)(2,1)S(1)} collective-permute-done((bf16[16,32,128]{2,1,0:T(8,128)(2,1)}, bf16[16,32,128]{2,1,0:T(8,128)(2,1)S(1)}, u32[]{:S(2)}, u32[]{:S(2)}) %collective-permute-start.6) | collective-permute-done | bytes 131104 | tf_op jit(solution)/shard_map/ppermute | solution.py:241
  20.7 1.0 %collective-permute-start.14 = (bf16[16,32,128]{2,1,0:T(8,128)(2,1)S(1)}, bf16[16,32,128]{2,1,0:T(8,128)(2,1)S(1)}, u32[]{:S(2)}, u32[]{:S(2)}) collective-permute-start(bf16[16,32,128]{2,1,0:T(8,128)(2,1)S(1)} %collective-permute-done.8.refs_8_), channel_id=1, source_target_pairs={{0,12},{2,14},{4,8},{6,10},{8,4},{10,6},{12,0},{14,2},{16,28},{18,... | collective-permute-start | bytes 393224 | tf_op jit(solution)/shard_map/ppermute | solution.py:241
  21.7 0.6 %collective-permute-done.4.refs_4_ = bf16[16,32,128]{2,1,0:T(8,128)(2,1)S(1)} collective-permute-done((bf16[16,32,128]{2,1,0:T(8,128)(2,1)}, bf16[16,32,128]{2,1,0:T(8,128)(2,1)S(1)}, u32[]{:S(2)}, u32[]{:S(2)}) %collective-permute-start.4) | collective-permute-done | bytes 131104 | tf_op jit(solution)/shard_map/ppermute | solution.py:241
  22.3 1.0 %collective-permute-start.12 = (bf16[16,32,128]{2,1,0:T(8,128)(2,1)S(1)}, bf16[16,32,128]{2,1,0:T(8,128)(2,1)S(1)}, u32[]{:S(2)}, u32[]{:S(2)}) collective-permute-start(bf16[16,32,128]{2,1,0:T(8,128)(2,1)S(1)} %collective-permute-done.8.refs_8_), channel_id=1, source_target_pairs={{0,8},{2,10},{4,12},{6,14},{8,0},{10,2},{12,4},{14,6},{16,24},{18,... | collective-permute-start | bytes 393224 | tf_op jit(solution)/shard_map/ppermute | solution.py:241
  23.3 0.0 collective-permute-done.2.refs_2_
  23.3 1.0 %collective-permute-start.10 = (bf16[16,32,128]{2,1,0:T(8,128)(2,1)S(1)}, bf16[16,32,128]{2,1,0:T(8,128)(2,1)S(1)}, u32[]{:S(2)}, u32[]{:S(2)}) collective-permute-start(bf16[16,32,128]{2,1,0:T(8,128)(2,1)S(1)} %collective-permute-done.8.refs_8_), channel_id=1, source_target_pairs={{0,4},{2,6},{4,0},{6,2},{8,12},{10,14},{12,8},{14,10},{16,20},{18,... | collective-permute-start | bytes 393224 | tf_op jit(solution)/shard_map/ppermute | solution.py:241
  24.2 0.0 collective-permute-done.refs_1_
  24.2 0.0 collective-permute-start.9
  24.2 0.0 collective-permute-done.16.refs_16_
  24.2 0.5 %collective-permute-start.7 = (bf16[16,32,128]{2,1,0:T(8,128)(2,1)S(1)}, bf16[16,32,128]{2,1,0:T(8,128)(2,1)S(1)}, u32[]{:S(2)}, u32[]{:S(2)}) collective-permute-start(bf16[16,32,128]{2,1,0:T(8,128)(2,1)S(1)} %collective-permute-done.6.refs_6_), channel_id=1, source_target_pairs={{0,2},{2,0},{4,6},{6,4},{8,10},{10,8},{12,14},{14,12},{16,18},{18,... | collective-permute-start | bytes 393224 | tf_op jit(solution)/shard_map/ppermute | solution.py:241
  24.8 2.0 %collective-permute-done.14.refs_14_ = bf16[16,32,128]{2,1,0:T(8,128)(2,1)S(1)} collective-permute-done((bf16[16,32,128]{2,1,0:T(8,128)(2,1)S(1)}, bf16[16,32,128]{2,1,0:T(8,128)(2,1)S(1)}, u32[]{:S(2)}, u32[]{:S(2)}) %collective-permute-start.14) | collective-permute-done | bytes 131104 | tf_op jit(solution)/shard_map/ppermute | solution.py:241
  26.7 0.0 collective-permute-start.5
  26.7 1.3 %collective-permute-done.12.refs_12_ = bf16[16,32,128]{2,1,0:T(8,128)(2,1)S(1)} collective-permute-done((bf16[16,32,128]{2,1,0:T(8,128)(2,1)S(1)}, bf16[16,32,128]{2,1,0:T(8,128)(2,1)S(1)}, u32[]{:S(2)}, u32[]{:S(2)}) %collective-permute-start.12) | collective-permute-done | bytes 131104 | tf_op jit(solution)/shard_map/ppermute | solution.py:241
  28.0 0.0 collective-permute-start.3
  28.0 0.5 %collective-permute-done.10.refs_10_ = bf16[16,32,128]{2,1,0:T(8,128)(2,1)S(1)} collective-permute-done((bf16[16,32,128]{2,1,0:T(8,128)(2,1)S(1)}, bf16[16,32,128]{2,1,0:T(8,128)(2,1)S(1)}, u32[]{:S(2)}, u32[]{:S(2)}) %collective-permute-start.10) | collective-permute-done | bytes 131104 | tf_op jit(solution)/shard_map/ppermute | solution.py:241
  28.5 0.0 collective-permute-start.1
  28.5 0.0 collective-permute-done.9.refs_9_
  28.5 0.5 %collective-permute-start.15 = (bf16[16,32,128]{2,1,0:T(8,128)(2,1)S(1)}, bf16[16,32,128]{2,1,0:T(8,128)(2,1)S(1)}, u32[]{:S(2)}, u32[]{:S(2)}) collective-permute-start(bf16[16,32,128]{2,1,0:T(8,128)(2,1)S(1)} %collective-permute-done.14.refs_14_), channel_id=1, source_target_pairs={{0,2},{2,0},{4,6},{6,4},{8,10},{10,8},{12,14},{14,12},{16,18},{18,... | collective-permute-start | bytes 393224 | tf_op jit(solution)/shard_map/ppermute | solution.py:241
  29.0 0.0 collective-permute-done.7.refs_7_
  29.0 0.1 collective-permute-start.13
  29.1 0.0 collective-permute-done.5.refs_5_
  29.1 0.4 %collective-permute-start.11 = (bf16[16,32,128]{2,1,0:T(8,128)(2,1)S(1)}, bf16[16,32,128]{2,1,0:T(8,128)(2,1)S(1)}, u32[]{:S(2)}, u32[]{:S(2)}) collective-permute-start(bf16[16,32,128]{2,1,0:T(8,128)(2,1)S(1)} %collective-permute-done.10.refs_10_), channel_id=1, source_target_pairs={{0,2},{2,0},{4,6},{6,4},{8,10},{10,8},{12,14},{14,12},{16,18},{18,... | collective-permute-start | bytes 393224 | tf_op jit(solution)/shard_map/ppermute | solution.py:241
  29.5 0.0 collective-permute-done.3.refs_3_
  29.5 0.3 collective-permute-done.1.refs_0_
  29.9 0.2 collective-permute-done.15.refs_15_
  30.0 0.3 %collective-permute-done.13.refs_13_ = bf16[16,32,128]{2,1,0:T(8,128)(2,1)S(1)} collective-permute-done((bf16[16,32,128]{2,1,0:T(8,128)(2,1)S(1)}, bf16[16,32,128]{2,1,0:T(8,128)(2,1)S(1)}, u32[]{:S(2)}, u32[]{:S(2)}) %collective-permute-start.13) | collective-permute-done | bytes 131104 | tf_op jit(solution)/shard_map/ppermute | solution.py:241
  30.4 0.2 collective-permute-done.11.refs_11_
  30.6 2.0 %correlate.1 = bf16[16,2,256,128]{3,2,1,0:T(8,128)(2,1)} custom-call(bf16[16,32,128]{2,1,0:T(8,128)(2,1)S(1)} %collective-permute-done.1.refs_0_, bf16[16,32,128]{2,1,0:T(8,128)(2,1)S(1)} %collective-permute-done.refs_1_, bf16[16,32,128]{2,1,0:T(8,128)(2,1)S(1)} %collective-permute-done.2.refs_2_, bf16[16,32,128]{2,1,0:T(8,128)(2,1)S(1)} %collective-permute-done.3.refs_3_, ...), custom_call_target="tpu_custom_call" | custom-call | tf_op jit(solution)/shard_map/correlate/pallas_call | solution.py:303
Async XLA Ops:
  7.5 10.7 %collective-permute-start.8 = (bf16[16,32,128]{2,1,0:T(8,128)(2,1)}, bf16[16,32,128]{2,1,0:T(8,128)(2,1)S(1)}, u32[]{:S(2)}, u32[]{:S(2)}) collective-permute-start(bf16[16,32,128]{2,1,0:T(8,128)(2,1)} %channelise.1), channel_id=1, source_target_pairs={{0,16},{2,18},{4,20},{6,22},{8,24},{10,26},{12,28},{14,30},{16,0},... | collective-permute-start | bytes 393224 | tf_op jit(solution)/shard_map/ppermute | solution.py:241
  11.6 9.2 %collective-permute-start.6 = (bf16[16,32,128]{2,1,0:T(8,128)(2,1)}, bf16[16,32,128]{2,1,0:T(8,128)(2,1)S(1)}, u32[]{:S(2)}, u32[]{:S(2)}) collective-permute-start(bf16[16,32,128]{2,1,0:T(8,128)(2,1)} %channelise.1), channel_id=1, source_target_pairs={{0,12},{2,14},{4,8},{6,10},{8,4},{10,6},{12,0},{14,2},{16,28},{18,... | collective-permute-start | bytes 393224 | tf_op jit(solution)/shard_map/ppermute | solution.py:241
  14.1 8.2 %collective-permute-start.4 = (bf16[16,32,128]{2,1,0:T(8,128)(2,1)}, bf16[16,32,128]{2,1,0:T(8,128)(2,1)S(1)}, u32[]{:S(2)}, u32[]{:S(2)}) collective-permute-start(bf16[16,32,128]{2,1,0:T(8,128)(2,1)} %channelise.1), channel_id=1, source_target_pairs={{0,8},{2,10},{4,12},{6,14},{8,0},{10,2},{12,4},{14,6},{16,24},{18,... | collective-permute-start | bytes 393224 | tf_op jit(solution)/shard_map/ppermute | solution.py:241
  14.5 8.7 %collective-permute-start.2 = (bf16[16,32,128]{2,1,0:T(8,128)(2,1)}, bf16[16,32,128]{2,1,0:T(8,128)(2,1)S(1)}, u32[]{:S(2)}, u32[]{:S(2)}) collective-permute-start(bf16[16,32,128]{2,1,0:T(8,128)(2,1)} %channelise.1), channel_id=1, source_target_pairs={{0,4},{2,6},{4,0},{6,2},{8,12},{10,14},{12,8},{14,10},{16,20},{18,... | collective-permute-start | bytes 393224 | tf_op jit(solution)/shard_map/ppermute | solution.py:241
  15.1 9.2 %collective-permute-start = (bf16[16,32,128]{2,1,0:T(8,128)(2,1)}, bf16[16,32,128]{2,1,0:T(8,128)(2,1)S(1)}, u32[]{:S(2)}, u32[]{:S(2)}) collective-permute-start(bf16[16,32,128]{2,1,0:T(8,128)(2,1)} %channelise.1), channel_id=1, source_target_pairs={{0,2},{2,0},{4,6},{6,4},{8,10},{10,8},{12,14},{14,12},{16,18},{18,... | collective-permute-start | bytes 393224 | tf_op jit(solution)/shard_map/ppermute | solution.py:241
  18.2 6.0 %collective-permute-start.16 = (bf16[16,32,128]{2,1,0:T(8,128)(2,1)}, bf16[16,32,128]{2,1,0:T(8,128)(2,1)S(1)}, u32[]{:S(2)}, u32[]{:S(2)}) collective-permute-start(bf16[16,32,128]{2,1,0:T(8,128)(2,1)} %channelise.1), channel_id=1, source_target_pairs={{0,1},{1,0},{2,3},{3,2},{4,5},{5,4},{6,7},{7,6},{8,9},{9,8},{10,11... | collective-permute-start | bytes 393224 | tf_op jit(solution)/shard_map/ppermute | solution.py:251
  20.7 6.0 %collective-permute-start.14 = (bf16[16,32,128]{2,1,0:T(8,128)(2,1)S(1)}, bf16[16,32,128]{2,1,0:T(8,128)(2,1)S(1)}, u32[]{:S(2)}, u32[]{:S(2)}) collective-permute-start(bf16[16,32,128]{2,1,0:T(8,128)(2,1)S(1)} %collective-permute-done.8.refs_8_), channel_id=1, source_target_pairs={{0,12},{2,14},{4,8},{6,10},{8,4},{10,6},{12,0},{14,2},{16,28},{18,... | collective-permute-start | bytes 393224 | tf_op jit(solution)/shard_map/ppermute | solution.py:241
  22.3 5.7 %collective-permute-start.12 = (bf16[16,32,128]{2,1,0:T(8,128)(2,1)S(1)}, bf16[16,32,128]{2,1,0:T(8,128)(2,1)S(1)}, u32[]{:S(2)}, u32[]{:S(2)}) collective-permute-start(bf16[16,32,128]{2,1,0:T(8,128)(2,1)S(1)} %collective-permute-done.8.refs_8_), channel_id=1, source_target_pairs={{0,8},{2,10},{4,12},{6,14},{8,0},{10,2},{12,4},{14,6},{16,24},{18,... | collective-permute-start | bytes 393224 | tf_op jit(solution)/shard_map/ppermute | solution.py:241
  23.3 5.2 %collective-permute-start.10 = (bf16[16,32,128]{2,1,0:T(8,128)(2,1)S(1)}, bf16[16,32,128]{2,1,0:T(8,128)(2,1)S(1)}, u32[]{:S(2)}, u32[]{:S(2)}) collective-permute-start(bf16[16,32,128]{2,1,0:T(8,128)(2,1)S(1)} %collective-permute-done.8.refs_8_), channel_id=1, source_target_pairs={{0,4},{2,6},{4,0},{6,2},{8,12},{10,14},{12,8},{14,10},{16,20},{18,... | collective-permute-start | bytes 393224 | tf_op jit(solution)/shard_map/ppermute | solution.py:241
  24.2 4.3 %collective-permute-start.9 = (bf16[16,32,128]{2,1,0:T(8,128)(2,1)S(1)}, bf16[16,32,128]{2,1,0:T(8,128)(2,1)S(1)}, u32[]{:S(2)}, u32[]{:S(2)}) collective-permute-start(bf16[16,32,128]{2,1,0:T(8,128)(2,1)S(1)} %collective-permute-done.8.refs_8_), channel_id=1, source_target_pairs={{0,2},{2,0},{4,6},{6,4},{8,10},{10,8},{12,14},{14,12},{16,18},{18,... | collective-permute-start | bytes 393224 | tf_op jit(solution)/shard_map/ppermute | solution.py:241
  24.2 4.8 %collective-permute-start.7 = (bf16[16,32,128]{2,1,0:T(8,128)(2,1)S(1)}, bf16[16,32,128]{2,1,0:T(8,128)(2,1)S(1)}, u32[]{:S(2)}, u32[]{:S(2)}) collective-permute-start(bf16[16,32,128]{2,1,0:T(8,128)(2,1)S(1)} %collective-permute-done.6.refs_6_), channel_id=1, source_target_pairs={{0,2},{2,0},{4,6},{6,4},{8,10},{10,8},{12,14},{14,12},{16,18},{18,... | collective-permute-start | bytes 393224 | tf_op jit(solution)/shard_map/ppermute | solution.py:241
  26.7 2.4 %collective-permute-start.5 = (bf16[16,32,128]{2,1,0:T(8,128)(2,1)S(1)}, bf16[16,32,128]{2,1,0:T(8,128)(2,1)S(1)}, u32[]{:S(2)}, u32[]{:S(2)}) collective-permute-start(bf16[16,32,128]{2,1,0:T(8,128)(2,1)S(1)} %collective-permute-done.4.refs_4_), channel_id=1, source_target_pairs={{0,2},{2,0},{4,6},{6,4},{8,10},{10,8},{12,14},{14,12},{16,18},{18,... | collective-permute-start | bytes 393224 | tf_op jit(solution)/shard_map/ppermute | solution.py:241
  28.0 1.5 %collective-permute-start.3 = (bf16[16,32,128]{2,1,0:T(8,128)(2,1)S(1)}, bf16[16,32,128]{2,1,0:T(8,128)(2,1)S(1)}, u32[]{:S(2)}, u32[]{:S(2)}) collective-permute-start(bf16[16,32,128]{2,1,0:T(8,128)(2,1)S(1)} %collective-permute-done.2.refs_2_), channel_id=1, source_target_pairs={{0,2},{2,0},{4,6},{6,4},{8,10},{10,8},{12,14},{14,12},{16,18},{18,... | collective-permute-start | bytes 393224 | tf_op jit(solution)/shard_map/ppermute | solution.py:241
  28.5 1.3 %collective-permute-start.1 = (bf16[16,32,128]{2,1,0:T(8,128)(2,1)S(1)}, bf16[16,32,128]{2,1,0:T(8,128)(2,1)S(1)}, u32[]{:S(2)}, u32[]{:S(2)}) collective-permute-start(bf16[16,32,128]{2,1,0:T(8,128)(2,1)S(1)} %collective-permute-done.refs_1_), channel_id=1, source_target_pairs={{0,2},{2,0},{4,6},{6,4},{8,10},{10,8},{12,14},{14,12},{16,18},{18,... | collective-permute-start | bytes 393224 | tf_op jit(solution)/shard_map/ppermute | solution.py:241
  28.5 1.5 %collective-permute-start.15 = (bf16[16,32,128]{2,1,0:T(8,128)(2,1)S(1)}, bf16[16,32,128]{2,1,0:T(8,128)(2,1)S(1)}, u32[]{:S(2)}, u32[]{:S(2)}) collective-permute-start(bf16[16,32,128]{2,1,0:T(8,128)(2,1)S(1)} %collective-permute-done.14.refs_14_), channel_id=1, source_target_pairs={{0,2},{2,0},{4,6},{6,4},{8,10},{10,8},{12,14},{14,12},{16,18},{18,... | collective-permute-start | bytes 393224 | tf_op jit(solution)/shard_map/ppermute | solution.py:241
  29.0 1.3 %collective-permute-start.13 = (bf16[16,32,128]{2,1,0:T(8,128)(2,1)S(1)}, bf16[16,32,128]{2,1,0:T(8,128)(2,1)S(1)}, u32[]{:S(2)}, u32[]{:S(2)}) collective-permute-start(bf16[16,32,128]{2,1,0:T(8,128)(2,1)S(1)} %collective-permute-done.12.refs_12_), channel_id=1, source_target_pairs={{0,2},{2,0},{4,6},{6,4},{8,10},{10,8},{12,14},{14,12},{16,18},{18,... | collective-permute-start | bytes 393224 | tf_op jit(solution)/shard_map/ppermute | solution.py:241
  29.1 1.5 %collective-permute-start.11 = (bf16[16,32,128]{2,1,0:T(8,128)(2,1)S(1)}, bf16[16,32,128]{2,1,0:T(8,128)(2,1)S(1)}, u32[]{:S(2)}, u32[]{:S(2)}) collective-permute-start(bf16[16,32,128]{2,1,0:T(8,128)(2,1)S(1)} %collective-permute-done.10.refs_10_), channel_id=1, source_target_pairs={{0,2},{2,0},{4,6},{6,4},{8,10},{10,8},{12,14},{14,12},{16,18},{18,... | collective-permute-start | bytes 393224 | tf_op jit(solution)/shard_map/ppermute | solution.py:241

commit v5 on v4

--- a/solution.py
+++ b/solution.py
@@ -97,24 +97,28 @@
 def filter_kernel(
     volts, table, lane_map, flags, out, held, table_v, map_s, flags_s, frames, sums, lanes, rows, in_sem, const_sem
 ):
-    ahead = 3
+    spans = ((0, 2), (2, 5), (5, 8))
     arrivals = [
         [
-            pltpu.make_async_copy(volts.at[p, :, j], held.at[p, j, pl.ds(0, FRAMES)], in_sem.at[p])
+            pltpu.make_async_copy(
+                volts.at[pl.ds(low, high - low), :, j],
+                held.at[pl.ds(low, high - low), j, pl.ds(0, FRAMES)],
+                in_sem.at[k],
+            )
             for j in range(CHUNKS // 2)
         ]
-        for p in range(P_DEV)
+        for k, (low, high) in enumerate(spans)
     ]
     get_table = pltpu.make_async_copy(table, table_v, const_sem.at[0])
     get_map = pltpu.make_async_copy(lane_map, map_s, const_sem.at[1])
     get_flags = pltpu.make_async_copy(flags, flags_s, const_sem.at[2])
 
-    def begin(p):
-        for copy in arrivals[p]:
+    def begin(k):
+        for copy in arrivals[k]:
             copy.start()
-        if p == 0:
+        if k == 0:
             get_table.start()
-        if p == 2:
+        if k == 1:
             get_map.start()
             get_flags.start()
 
@@ -174,13 +178,13 @@
                     imag = pltpu.roll(imag, SPECTRA, 1)
                 lanes[(first + i) * Q_DEV + q] = jnp.where(real_lanes, real, imag)
 
-    for p in range(ahead):
-        begin(p)
+    for k in range(len(spans)):
+        begin(k)
     for p in range(P_DEV):
-        for copy in arrivals[p]:
-            copy.wait()
-        if p + ahead < P_DEV:
-            begin(p + ahead)
+        for k, (low, _) in enumerate(spans):
+            if p == low:
+                for copy in arrivals[k]:
+                    copy.wait()
         if p == 0:
             get_table.wait()
         if p == 5:
@@ -223,7 +227,7 @@
             pltpu.VMEM((2, 4 * SPECTRA, CHUNK), jnp.float32),
             pltpu.VMEM((LANES, CH_DEV, 2 * SPECTRA), jnp.float32),
             pltpu.VMEM((CH_DEV * PITCH, 2 * SPECTRA), jnp.float32),
-            pltpu.SemaphoreType.DMA((P_DEV,)),
+            pltpu.SemaphoreType.DMA((3,)),
             pltpu.SemaphoreType.DMA((3,)),
         ],
         compiler_params=pltpu.CompilerParams(vmem_limit_bytes=56 << 20),

time: 32.7 us -> 31.5 us (0.963)
  Pallas kernels: 9.5 us -> 8.26 us
    pallas_call x1, Pallas kernels: 7.48 us -> 6.24 us  [channelise(): pl.pallas_call(filter_kernel, out_shape=jax.ShapeDtypeStruct((CH_DEV, LAN...]
where the time goes in v5:
time: 31.5 us; the launch traced here: 31.4 us
  starting transfers between devices  13.6 us (43%)
  waiting for transfers between devices  9.49 us (30%)
  Pallas kernels  8.26 us (26%)
    ppermute x16, starting transfers between devices, swap(): return lax.ppermute(block, 'row', [(i, i ^ d) for i in range(ROWS)])  12 us
    ppermute x16, waiting for transfers between devices, swap(): return lax.ppermute(block, 'row', [(i, i ^ d) for i in range(ROWS)])  9.49 us
    pallas_call x1, Pallas kernels, channelise(): pl.pallas_call(filter_kernel, out_shape=jax.ShapeDtypeStruct((CH_DEV, LAN...  6.24 us
    pallas_call x1, Pallas kernels, correlate(): pl.pallas_call(correlate_kernel, out_shape=jax.ShapeDtypeStruct((CH_DEV,...  2.02 us
    ppermute x1, starting transfers between devices, gather(): other = lax.ppermute(late, 'col', [(0, 1), (1, 0)])  1.58 us
  transfers between devices with their start and end apart: 17, of which 10 were waited for; matrix products, arithmetic and copies ran while one was open for 0% of the time, Pallas kernels for 0%

profile of v5, /device:TPU:0, one launch (start us, length us, event | category | flops | bytes accessed | tf_op | source)
XLA Modules:
  0.0 31.4 jit_solution(10026199524453012080)
XLA Ops:
  0.0 6.2 %channelise.1 = bf16[16,32,128]{2,1,0:T(8,128)(2,1)} custom-call(bf16[8,67,8,8,128]{4,3,2,1,0:T(8,128)(2,1)} %bitcast.8, bf16[1024,256]{1,0:T(8,128)(2,1)} %constant.2.clone.table, s32[1,32]{1,0:T(1,128)} %bitcast.10, s32[4,8]{1,0:T(4,128)} %bitcast.9), custom_call_target="tpu_custom_call" | custom-call | tf_op jit(solution)/shard_map/channelise/pallas_call | solution.py:216
  6.2 4.1 %collective-permute-start.8 = (bf16[16,32,128]{2,1,0:T(8,128)(2,1)}, bf16[16,32,128]{2,1,0:T(8,128)(2,1)S(1)}, u32[]{:S(2)}, u32[]{:S(2)}) collective-permute-start(bf16[16,32,128]{2,1,0:T(8,128)(2,1)} %channelise.1), channel_id=1, source_target_pairs={{0,16},{2,18},{4,20},{6,22},{8,24},{10,26},{12,28},{14,30},{16,0},... | collective-permute-start | bytes 393224 | tf_op jit(solution)/shard_map/ppermute | solution.py:245
  10.4 2.5 %collective-permute-start.6 = (bf16[16,32,128]{2,1,0:T(8,128)(2,1)}, bf16[16,32,128]{2,1,0:T(8,128)(2,1)S(1)}, u32[]{:S(2)}, u32[]{:S(2)}) collective-permute-start(bf16[16,32,128]{2,1,0:T(8,128)(2,1)} %channelise.1), channel_id=1, source_target_pairs={{0,12},{2,14},{4,8},{6,10},{8,4},{10,6},{12,0},{14,2},{16,28},{18,... | collective-permute-start | bytes 393224 | tf_op jit(solution)/shard_map/ppermute | solution.py:245
  12.9 0.4 %collective-permute-start.4 = (bf16[16,32,128]{2,1,0:T(8,128)(2,1)}, bf16[16,32,128]{2,1,0:T(8,128)(2,1)S(1)}, u32[]{:S(2)}, u32[]{:S(2)}) collective-permute-start(bf16[16,32,128]{2,1,0:T(8,128)(2,1)} %channelise.1), channel_id=1, source_target_pairs={{0,8},{2,10},{4,12},{6,14},{8,0},{10,2},{12,4},{14,6},{16,24},{18,... | collective-permute-start | bytes 393224 | tf_op jit(solution)/shard_map/ppermute | solution.py:245
  13.3 0.5 %collective-permute-start.2 = (bf16[16,32,128]{2,1,0:T(8,128)(2,1)}, bf16[16,32,128]{2,1,0:T(8,128)(2,1)S(1)}, u32[]{:S(2)}, u32[]{:S(2)}) collective-permute-start(bf16[16,32,128]{2,1,0:T(8,128)(2,1)} %channelise.1), channel_id=1, source_target_pairs={{0,4},{2,6},{4,0},{6,2},{8,12},{10,14},{12,8},{14,10},{16,20},{18,... | collective-permute-start | bytes 393224 | tf_op jit(solution)/shard_map/ppermute | solution.py:245
  13.8 0.0 collective-permute-start
  13.8 3.1 %collective-permute-done.8.refs_8_ = bf16[16,32,128]{2,1,0:T(8,128)(2,1)S(1)} collective-permute-done((bf16[16,32,128]{2,1,0:T(8,128)(2,1)}, bf16[16,32,128]{2,1,0:T(8,128)(2,1)S(1)}, u32[]{:S(2)}, u32[]{:S(2)}) %collective-permute-start.8) | collective-permute-done | bytes 131104 | tf_op jit(solution)/shard_map/ppermute | solution.py:245
  17.0 1.6 %collective-permute-start.16 = (bf16[16,32,128]{2,1,0:T(8,128)(2,1)}, bf16[16,32,128]{2,1,0:T(8,128)(2,1)S(1)}, u32[]{:S(2)}, u32[]{:S(2)}) collective-permute-start(bf16[16,32,128]{2,1,0:T(8,128)(2,1)} %channelise.1), channel_id=1, source_target_pairs={{0,1},{1,0},{2,3},{3,2},{4,5},{5,4},{6,7},{7,6},{8,9},{9,8},{10,11... | collective-permute-start | bytes 393224 | tf_op jit(solution)/shard_map/ppermute | solution.py:255
  18.6 1.0 %collective-permute-done.6.refs_6_ = bf16[16,32,128]{2,1,0:T(8,128)(2,1)S(1)} collective-permute-done((bf16[16,32,128]{2,1,0:T(8,128)(2,1)}, bf16[16,32,128]{2,1,0:T(8,128)(2,1)S(1)}, u32[]{:S(2)}, u32[]{:S(2)}) %collective-permute-start.6) | collective-permute-done | bytes 131104 | tf_op jit(solution)/shard_map/ppermute | solution.py:245
  19.5 0.9 %collective-permute-start.14 = (bf16[16,32,128]{2,1,0:T(8,128)(2,1)S(1)}, bf16[16,32,128]{2,1,0:T(8,128)(2,1)S(1)}, u32[]{:S(2)}, u32[]{:S(2)}) collective-permute-start(bf16[16,32,128]{2,1,0:T(8,128)(2,1)S(1)} %collective-permute-done.8.refs_8_), channel_id=1, source_target_pairs={{0,12},{2,14},{4,8},{6,10},{8,4},{10,6},{12,0},{14,2},{16,28},{18,... | collective-permute-start | bytes 393224 | tf_op jit(solution)/shard_map/ppermute | solution.py:245
  20.4 0.6 %collective-permute-done.4.refs_4_ = bf16[16,32,128]{2,1,0:T(8,128)(2,1)S(1)} collective-permute-done((bf16[16,32,128]{2,1,0:T(8,128)(2,1)}, bf16[16,32,128]{2,1,0:T(8,128)(2,1)S(1)}, u32[]{:S(2)}, u32[]{:S(2)}) %collective-permute-start.4) | collective-permute-done | bytes 131104 | tf_op jit(solution)/shard_map/ppermute | solution.py:245
  21.1 1.0 %collective-permute-start.12 = (bf16[16,32,128]{2,1,0:T(8,128)(2,1)S(1)}, bf16[16,32,128]{2,1,0:T(8,128)(2,1)S(1)}, u32[]{:S(2)}, u32[]{:S(2)}) collective-permute-start(bf16[16,32,128]{2,1,0:T(8,128)(2,1)S(1)} %collective-permute-done.8.refs_8_), channel_id=1, source_target_pairs={{0,8},{2,10},{4,12},{6,14},{8,0},{10,2},{12,4},{14,6},{16,24},{18,... | collective-permute-start | bytes 393224 | tf_op jit(solution)/shard_map/ppermute | solution.py:245
  22.0 0.0 collective-permute-done.2.refs_2_
  22.0 1.0 %collective-permute-start.10 = (bf16[16,32,128]{2,1,0:T(8,128)(2,1)S(1)}, bf16[16,32,128]{2,1,0:T(8,128)(2,1)S(1)}, u32[]{:S(2)}, u32[]{:S(2)}) collective-permute-start(bf16[16,32,128]{2,1,0:T(8,128)(2,1)S(1)} %collective-permute-done.8.refs_8_), channel_id=1, source_target_pairs={{0,4},{2,6},{4,0},{6,2},{8,12},{10,14},{12,8},{14,10},{16,20},{18,... | collective-permute-start | bytes 393224 | tf_op jit(solution)/shard_map/ppermute | solution.py:245
  23.0 0.0 collective-permute-done.refs_1_
  23.0 0.0 collective-permute-start.9
  23.0 0.0 collective-permute-done.16.refs_16_
  23.0 0.5 %collective-permute-start.7 = (bf16[16,32,128]{2,1,0:T(8,128)(2,1)S(1)}, bf16[16,32,128]{2,1,0:T(8,128)(2,1)S(1)}, u32[]{:S(2)}, u32[]{:S(2)}) collective-permute-start(bf16[16,32,128]{2,1,0:T(8,128)(2,1)S(1)} %collective-permute-done.6.refs_6_), channel_id=1, source_target_pairs={{0,2},{2,0},{4,6},{6,4},{8,10},{10,8},{12,14},{14,12},{16,18},{18,... | collective-permute-start | bytes 393224 | tf_op jit(solution)/shard_map/ppermute | solution.py:245
  23.5 2.0 %collective-permute-done.14.refs_14_ = bf16[16,32,128]{2,1,0:T(8,128)(2,1)S(1)} collective-permute-done((bf16[16,32,128]{2,1,0:T(8,128)(2,1)S(1)}, bf16[16,32,128]{2,1,0:T(8,128)(2,1)S(1)}, u32[]{:S(2)}, u32[]{:S(2)}) %collective-permute-start.14) | collective-permute-done | bytes 131104 | tf_op jit(solution)/shard_map/ppermute | solution.py:245
  25.5 0.0 collective-permute-start.5
  25.5 1.3 %collective-permute-done.12.refs_12_ = bf16[16,32,128]{2,1,0:T(8,128)(2,1)S(1)} collective-permute-done((bf16[16,32,128]{2,1,0:T(8,128)(2,1)S(1)}, bf16[16,32,128]{2,1,0:T(8,128)(2,1)S(1)}, u32[]{:S(2)}, u32[]{:S(2)}) %collective-permute-start.12) | collective-permute-done | bytes 131104 | tf_op jit(solution)/shard_map/ppermute | solution.py:245
  26.8 0.0 collective-permute-start.3
  26.8 0.5 %collective-permute-done.10.refs_10_ = bf16[16,32,128]{2,1,0:T(8,128)(2,1)S(1)} collective-permute-done((bf16[16,32,128]{2,1,0:T(8,128)(2,1)S(1)}, bf16[16,32,128]{2,1,0:T(8,128)(2,1)S(1)}, u32[]{:S(2)}, u32[]{:S(2)}) %collective-permute-start.10) | collective-permute-done | bytes 131104 | tf_op jit(solution)/shard_map/ppermute | solution.py:245
  27.3 0.0 collective-permute-start.1
  27.3 0.0 collective-permute-done.9.refs_9_
  27.3 0.5 %collective-permute-start.15 = (bf16[16,32,128]{2,1,0:T(8,128)(2,1)S(1)}, bf16[16,32,128]{2,1,0:T(8,128)(2,1)S(1)}, u32[]{:S(2)}, u32[]{:S(2)}) collective-permute-start(bf16[16,32,128]{2,1,0:T(8,128)(2,1)S(1)} %collective-permute-done.14.refs_14_), channel_id=1, source_target_pairs={{0,2},{2,0},{4,6},{6,4},{8,10},{10,8},{12,14},{14,12},{16,18},{18,... | collective-permute-start | bytes 393224 | tf_op jit(solution)/shard_map/ppermute | solution.py:245
  27.8 0.0 collective-permute-done.7.refs_7_
  27.8 0.1 collective-permute-start.13
  27.9 0.0 collective-permute-done.5.refs_5_
  27.9 0.4 %collective-permute-start.11 = (bf16[16,32,128]{2,1,0:T(8,128)(2,1)S(1)}, bf16[16,32,128]{2,1,0:T(8,128)(2,1)S(1)}, u32[]{:S(2)}, u32[]{:S(2)}) collective-permute-start(bf16[16,32,128]{2,1,0:T(8,128)(2,1)S(1)} %collective-permute-done.10.refs_10_), channel_id=1, source_target_pairs={{0,2},{2,0},{4,6},{6,4},{8,10},{10,8},{12,14},{14,12},{16,18},{18,... | collective-permute-start | bytes 393224 | tf_op jit(solution)/shard_map/ppermute | solution.py:245
  28.3 0.0 collective-permute-done.3.refs_3_
  28.3 0.3 collective-permute-done.1.refs_0_
  28.6 0.2 collective-permute-done.15.refs_15_
  28.8 0.3 %collective-permute-done.13.refs_13_ = bf16[16,32,128]{2,1,0:T(8,128)(2,1)S(1)} collective-permute-done((bf16[16,32,128]{2,1,0:T(8,128)(2,1)S(1)}, bf16[16,32,128]{2,1,0:T(8,128)(2,1)S(1)}, u32[]{:S(2)}, u32[]{:S(2)}) %collective-permute-start.13) | collective-permute-done | bytes 131104 | tf_op jit(solution)/shard_map/ppermute | solution.py:245
  29.2 0.2 collective-permute-done.11.refs_11_
  29.3 2.0 %correlate.1 = bf16[16,2,256,128]{3,2,1,0:T(8,128)(2,1)} custom-call(bf16[16,32,128]{2,1,0:T(8,128)(2,1)S(1)} %collective-permute-done.1.refs_0_, bf16[16,32,128]{2,1,0:T(8,128)(2,1)S(1)} %collective-permute-done.refs_1_, bf16[16,32,128]{2,1,0:T(8,128)(2,1)S(1)} %collective-permute-done.2.refs_2_, bf16[16,32,128]{2,1,0:T(8,128)(2,1)S(1)} %collective-permute-done.3.refs_3_, ...), custom_call_target="tpu_custom_call" | custom-call | tf_op jit(solution)/shard_map/correlate/pallas_call | solution.py:307
Async XLA Ops:
  6.2 10.7 %collective-permute-start.8 = (bf16[16,32,128]{2,1,0:T(8,128)(2,1)}, bf16[16,32,128]{2,1,0:T(8,128)(2,1)S(1)}, u32[]{:S(2)}, u32[]{:S(2)}) collective-permute-start(bf16[16,32,128]{2,1,0:T(8,128)(2,1)} %channelise.1), channel_id=1, source_target_pairs={{0,16},{2,18},{4,20},{6,22},{8,24},{10,26},{12,28},{14,30},{16,0},... | collective-permute-start | bytes 393224 | tf_op jit(solution)/shard_map/ppermute | solution.py:245
  10.4 9.1 %collective-permute-start.6 = (bf16[16,32,128]{2,1,0:T(8,128)(2,1)}, bf16[16,32,128]{2,1,0:T(8,128)(2,1)S(1)}, u32[]{:S(2)}, u32[]{:S(2)}) collective-permute-start(bf16[16,32,128]{2,1,0:T(8,128)(2,1)} %channelise.1), channel_id=1, source_target_pairs={{0,12},{2,14},{4,8},{6,10},{8,4},{10,6},{12,0},{14,2},{16,28},{18,... | collective-permute-start | bytes 393224 | tf_op jit(solution)/shard_map/ppermute | solution.py:245
  12.9 8.2 %collective-permute-start.4 = (bf16[16,32,128]{2,1,0:T(8,128)(2,1)}, bf16[16,32,128]{2,1,0:T(8,128)(2,1)S(1)}, u32[]{:S(2)}, u32[]{:S(2)}) collective-permute-start(bf16[16,32,128]{2,1,0:T(8,128)(2,1)} %channelise.1), channel_id=1, source_target_pairs={{0,8},{2,10},{4,12},{6,14},{8,0},{10,2},{12,4},{14,6},{16,24},{18,... | collective-permute-start | bytes 393224 | tf_op jit(solution)/shard_map/ppermute | solution.py:245
  13.3 8.7 %collective-permute-start.2 = (bf16[16,32,128]{2,1,0:T(8,128)(2,1)}, bf16[16,32,128]{2,1,0:T(8,128)(2,1)S(1)}, u32[]{:S(2)}, u32[]{:S(2)}) collective-permute-start(bf16[16,32,128]{2,1,0:T(8,128)(2,1)} %channelise.1), channel_id=1, source_target_pairs={{0,4},{2,6},{4,0},{6,2},{8,12},{10,14},{12,8},{14,10},{16,20},{18,... | collective-permute-start | bytes 393224 | tf_op jit(solution)/shard_map/ppermute | solution.py:245
  13.8 9.2 %collective-permute-start = (bf16[16,32,128]{2,1,0:T(8,128)(2,1)}, bf16[16,32,128]{2,1,0:T(8,128)(2,1)S(1)}, u32[]{:S(2)}, u32[]{:S(2)}) collective-permute-start(bf16[16,32,128]{2,1,0:T(8,128)(2,1)} %channelise.1), channel_id=1, source_target_pairs={{0,2},{2,0},{4,6},{6,4},{8,10},{10,8},{12,14},{14,12},{16,18},{18,... | collective-permute-start | bytes 393224 | tf_op jit(solution)/shard_map/ppermute | solution.py:245
  17.0 6.0 %collective-permute-start.16 = (bf16[16,32,128]{2,1,0:T(8,128)(2,1)}, bf16[16,32,128]{2,1,0:T(8,128)(2,1)S(1)}, u32[]{:S(2)}, u32[]{:S(2)}) collective-permute-start(bf16[16,32,128]{2,1,0:T(8,128)(2,1)} %channelise.1), channel_id=1, source_target_pairs={{0,1},{1,0},{2,3},{3,2},{4,5},{5,4},{6,7},{7,6},{8,9},{9,8},{10,11... | collective-permute-start | bytes 393224 | tf_op jit(solution)/shard_map/ppermute | solution.py:255
  19.5 6.0 %collective-permute-start.14 = (bf16[16,32,128]{2,1,0:T(8,128)(2,1)S(1)}, bf16[16,32,128]{2,1,0:T(8,128)(2,1)S(1)}, u32[]{:S(2)}, u32[]{:S(2)}) collective-permute-start(bf16[16,32,128]{2,1,0:T(8,128)(2,1)S(1)} %collective-permute-done.8.refs_8_), channel_id=1, source_target_pairs={{0,12},{2,14},{4,8},{6,10},{8,4},{10,6},{12,0},{14,2},{16,28},{18,... | collective-permute-start | bytes 393224 | tf_op jit(solution)/shard_map/ppermute | solution.py:245
  21.1 5.7 %collective-permute-start.12 = (bf16[16,32,128]{2,1,0:T(8,128)(2,1)S(1)}, bf16[16,32,128]{2,1,0:T(8,128)(2,1)S(1)}, u32[]{:S(2)}, u32[]{:S(2)}) collective-permute-start(bf16[16,32,128]{2,1,0:T(8,128)(2,1)S(1)} %collective-permute-done.8.refs_8_), channel_id=1, source_target_pairs={{0,8},{2,10},{4,12},{6,14},{8,0},{10,2},{12,4},{14,6},{16,24},{18,... | collective-permute-start | bytes 393224 | tf_op jit(solution)/shard_map/ppermute | solution.py:245
  22.0 5.2 %collective-permute-start.10 = (bf16[16,32,128]{2,1,0:T(8,128)(2,1)S(1)}, bf16[16,32,128]{2,1,0:T(8,128)(2,1)S(1)}, u32[]{:S(2)}, u32[]{:S(2)}) collective-permute-start(bf16[16,32,128]{2,1,0:T(8,128)(2,1)S(1)} %collective-permute-done.8.refs_8_), channel_id=1, source_target_pairs={{0,4},{2,6},{4,0},{6,2},{8,12},{10,14},{12,8},{14,10},{16,20},{18,... | collective-permute-start | bytes 393224 | tf_op jit(solution)/shard_map/ppermute | solution.py:245
  23.0 4.3 %collective-permute-start.9 = (bf16[16,32,128]{2,1,0:T(8,128)(2,1)S(1)}, bf16[16,32,128]{2,1,0:T(8,128)(2,1)S(1)}, u32[]{:S(2)}, u32[]{:S(2)}) collective-permute-start(bf16[16,32,128]{2,1,0:T(8,128)(2,1)S(1)} %collective-permute-done.8.refs_8_), channel_id=1, source_target_pairs={{0,2},{2,0},{4,6},{6,4},{8,10},{10,8},{12,14},{14,12},{16,18},{18,... | collective-permute-start | bytes 393224 | tf_op jit(solution)/shard_map/ppermute | solution.py:245
  23.0 4.8 %collective-permute-start.7 = (bf16[16,32,128]{2,1,0:T(8,128)(2,1)S(1)}, bf16[16,32,128]{2,1,0:T(8,128)(2,1)S(1)}, u32[]{:S(2)}, u32[]{:S(2)}) collective-permute-start(bf16[16,32,128]{2,1,0:T(8,128)(2,1)S(1)} %collective-permute-done.6.refs_6_), channel_id=1, source_target_pairs={{0,2},{2,0},{4,6},{6,4},{8,10},{10,8},{12,14},{14,12},{16,18},{18,... | collective-permute-start | bytes 393224 | tf_op jit(solution)/shard_map/ppermute | solution.py:245
  25.5 2.4 %collective-permute-start.5 = (bf16[16,32,128]{2,1,0:T(8,128)(2,1)S(1)}, bf16[16,32,128]{2,1,0:T(8,128)(2,1)S(1)}, u32[]{:S(2)}, u32[]{:S(2)}) collective-permute-start(bf16[16,32,128]{2,1,0:T(8,128)(2,1)S(1)} %collective-permute-done.4.refs_4_), channel_id=1, source_target_pairs={{0,2},{2,0},{4,6},{6,4},{8,10},{10,8},{12,14},{14,12},{16,18},{18,... | collective-permute-start | bytes 393224 | tf_op jit(solution)/shard_map/ppermute | solution.py:245
  26.8 1.5 %collective-permute-start.3 = (bf16[16,32,128]{2,1,0:T(8,128)(2,1)S(1)}, bf16[16,32,128]{2,1,0:T(8,128)(2,1)S(1)}, u32[]{:S(2)}, u32[]{:S(2)}) collective-permute-start(bf16[16,32,128]{2,1,0:T(8,128)(2,1)S(1)} %collective-permute-done.2.refs_2_), channel_id=1, source_target_pairs={{0,2},{2,0},{4,6},{6,4},{8,10},{10,8},{12,14},{14,12},{16,18},{18,... | collective-permute-start | bytes 393224 | tf_op jit(solution)/shard_map/ppermute | solution.py:245
  27.3 1.3 %collective-permute-start.1 = (bf16[16,32,128]{2,1,0:T(8,128)(2,1)S(1)}, bf16[16,32,128]{2,1,0:T(8,128)(2,1)S(1)}, u32[]{:S(2)}, u32[]{:S(2)}) collective-permute-start(bf16[16,32,128]{2,1,0:T(8,128)(2,1)S(1)} %collective-permute-done.refs_1_), channel_id=1, source_target_pairs={{0,2},{2,0},{4,6},{6,4},{8,10},{10,8},{12,14},{14,12},{16,18},{18,... | collective-permute-start | bytes 393224 | tf_op jit(solution)/shard_map/ppermute | solution.py:245
  27.3 1.5 %collective-permute-start.15 = (bf16[16,32,128]{2,1,0:T(8,128)(2,1)S(1)}, bf16[16,32,128]{2,1,0:T(8,128)(2,1)S(1)}, u32[]{:S(2)}, u32[]{:S(2)}) collective-permute-start(bf16[16,32,128]{2,1,0:T(8,128)(2,1)S(1)} %collective-permute-done.14.refs_14_), channel_id=1, source_target_pairs={{0,2},{2,0},{4,6},{6,4},{8,10},{10,8},{12,14},{14,12},{16,18},{18,... | collective-permute-start | bytes 393224 | tf_op jit(solution)/shard_map/ppermute | solution.py:245
  27.8 1.3 %collective-permute-start.13 = (bf16[16,32,128]{2,1,0:T(8,128)(2,1)S(1)}, bf16[16,32,128]{2,1,0:T(8,128)(2,1)S(1)}, u32[]{:S(2)}, u32[]{:S(2)}) collective-permute-start(bf16[16,32,128]{2,1,0:T(8,128)(2,1)S(1)} %collective-permute-done.12.refs_12_), channel_id=1, source_target_pairs={{0,2},{2,0},{4,6},{6,4},{8,10},{10,8},{12,14},{14,12},{16,18},{18,... | collective-permute-start | bytes 393224 | tf_op jit(solution)/shard_map/ppermute | solution.py:245
  27.9 1.5 %collective-permute-start.11 = (bf16[16,32,128]{2,1,0:T(8,128)(2,1)S(1)}, bf16[16,32,128]{2,1,0:T(8,128)(2,1)S(1)}, u32[]{:S(2)}, u32[]{:S(2)}) collective-permute-start(bf16[16,32,128]{2,1,0:T(8,128)(2,1)S(1)} %collective-permute-done.10.refs_10_), channel_id=1, source_target_pairs={{0,2},{2,0},{4,6},{6,4},{8,10},{10,8},{12,14},{14,12},{16,18},{18,... | collective-permute-start | bytes 393224 | tf_op jit(solution)/shard_map/ppermute | solution.py:245

commit v6 on v5

--- a/solution.py
+++ b/solution.py
@@ -253,7 +253,8 @@
         blocks[d + 1] = swap(blocks[d], 1)
     late, _ = lax.optimization_barrier((own, blocks[8]))
     other = lax.ppermute(late, "col", [(0, 1), (1, 0)])
-    blocks[0] = swap(blocks[1], 1)
+    back, _ = lax.optimization_barrier((blocks[1], blocks[6]))
+    blocks[0] = swap(back, 1)
     return [blocks[d] for d in range(ROWS)], other
 
 

time: 31.5 us -> 31.3 us (level)
  waiting for transfers between devices: 9.49 us -> 8.71 us
  starting transfers between devices: 13.6 us -> 14.1 us
    ppermute x16, waiting for transfers between devices: 9.49 us -> 8.62 us  [swap(): return lax.ppermute(block, 'row', [(i, i ^ d) for i in range(ROWS)])]
    ppermute x16, starting transfers between devices: 12 us -> 12.5 us  [swap(): return lax.ppermute(block, 'row', [(i, i ^ d) for i in range(ROWS)])]
  transfers between devices with their start and end apart: 17 -> 17, of which waited for: 10 -> 9; matrix products, arithmetic and copies ran while one was open for 0% -> 0% of each run, Pallas kernels for 0% -> 0%
where the time goes in v6:
time: 31.3 us; the launch traced here: 31.1 us
  starting transfers between devices  14.1 us (45%)
  waiting for transfers between devices  8.71 us (28%)
  Pallas kernels  8.26 us (26%)
    ppermute x16, starting transfers between devices, swap(): return lax.ppermute(block, 'row', [(i, i ^ d) for i in range(ROWS)])  12.5 us
    ppermute x16, waiting for transfers between devices, swap(): return lax.ppermute(block, 'row', [(i, i ^ d) for i in range(ROWS)])  8.62 us
    pallas_call x1, Pallas kernels, channelise(): pl.pallas_call(filter_kernel, out_shape=jax.ShapeDtypeStruct((CH_DEV, LAN...  6.24 us
    pallas_call x1, Pallas kernels, correlate(): pl.pallas_call(correlate_kernel, out_shape=jax.ShapeDtypeStruct((CH_DEV,...  2.02 us
    ppermute x1, starting transfers between devices, gather(): other = lax.ppermute(late, 'col', [(0, 1), (1, 0)])  1.58 us
  transfers between devices with their start and end apart: 17, of which 9 were waited for; matrix products, arithmetic and copies ran while one was open for 0% of the time, Pallas kernels for 0%

profile of v6, /device:TPU:0, one launch (start us, length us, event | category | flops | bytes accessed | tf_op | source)
XLA Modules:
  0.0 31.1 jit_solution(6531176599229307301)
XLA Ops:
  0.0 6.2 %channelise.1 = bf16[16,32,128]{2,1,0:T(8,128)(2,1)} custom-call(bf16[8,67,8,8,128]{4,3,2,1,0:T(8,128)(2,1)} %bitcast.8, bf16[1024,256]{1,0:T(8,128)(2,1)} %constant.2.clone.table, s32[1,32]{1,0:T(1,128)} %bitcast.10, s32[4,8]{1,0:T(4,128)} %bitcast.9), custom_call_target="tpu_custom_call" | custom-call | tf_op jit(solution)/shard_map/channelise/pallas_call | solution.py:216
  6.2 4.1 %collective-permute-start.8 = (bf16[16,32,128]{2,1,0:T(8,128)(2,1)}, bf16[16,32,128]{2,1,0:T(8,128)(2,1)S(1)}, u32[]{:S(2)}, u32[]{:S(2)}) collective-permute-start(bf16[16,32,128]{2,1,0:T(8,128)(2,1)} %channelise.1), channel_id=1, source_target_pairs={{0,16},{2,18},{4,20},{6,22},{8,24},{10,26},{12,28},{14,30},{16,0},... | collective-permute-start | bytes 393224 | tf_op jit(solution)/shard_map/ppermute | solution.py:245
  10.4 1.6 %collective-permute-start.5 = (bf16[16,32,128]{2,1,0:T(8,128)(2,1)}, bf16[16,32,128]{2,1,0:T(8,128)(2,1)S(1)}, u32[]{:S(2)}, u32[]{:S(2)}) collective-permute-start(bf16[16,32,128]{2,1,0:T(8,128)(2,1)} %channelise.1), channel_id=1, source_target_pairs={{0,8},{2,10},{4,12},{6,14},{8,0},{10,2},{12,4},{14,6},{16,24},{18,... | collective-permute-start | bytes 393224 | tf_op jit(solution)/shard_map/ppermute | solution.py:245
  11.9 1.5 %collective-permute-start.3 = (bf16[16,32,128]{2,1,0:T(8,128)(2,1)}, bf16[16,32,128]{2,1,0:T(8,128)(2,1)S(1)}, u32[]{:S(2)}, u32[]{:S(2)}) collective-permute-start(bf16[16,32,128]{2,1,0:T(8,128)(2,1)} %channelise.1), channel_id=1, source_target_pairs={{0,4},{2,6},{4,0},{6,2},{8,12},{10,14},{12,8},{14,10},{16,20},{18,... | collective-permute-start | bytes 393224 | tf_op jit(solution)/shard_map/ppermute | solution.py:245
  13.4 0.4 %collective-permute-start.1 = (bf16[16,32,128]{2,1,0:T(8,128)(2,1)}, bf16[16,32,128]{2,1,0:T(8,128)(2,1)S(1)}, u32[]{:S(2)}, u32[]{:S(2)}) collective-permute-start(bf16[16,32,128]{2,1,0:T(8,128)(2,1)} %channelise.1), channel_id=1, source_target_pairs={{0,12},{2,14},{4,8},{6,10},{8,4},{10,6},{12,0},{14,2},{16,28},{18,... | collective-permute-start | bytes 393224 | tf_op jit(solution)/shard_map/ppermute | solution.py:245
  13.8 0.0 collective-permute-start
  13.8 3.1 %collective-permute-done.8.refs_8_ = bf16[16,32,128]{2,1,0:T(8,128)(2,1)S(1)} collective-permute-done((bf16[16,32,128]{2,1,0:T(8,128)(2,1)}, bf16[16,32,128]{2,1,0:T(8,128)(2,1)S(1)}, u32[]{:S(2)}, u32[]{:S(2)}) %collective-permute-start.8) | collective-permute-done | bytes 131104 | tf_op jit(solution)/shard_map/ppermute | solution.py:245
  17.0 1.6 %collective-permute-start.16 = (bf16[16,32,128]{2,1,0:T(8,128)(2,1)}, bf16[16,32,128]{2,1,0:T(8,128)(2,1)S(1)}, u32[]{:S(2)}, u32[]{:S(2)}) collective-permute-start(bf16[16,32,128]{2,1,0:T(8,128)(2,1)} %channelise.1), channel_id=1, source_target_pairs={{0,1},{1,0},{2,3},{3,2},{4,5},{5,4},{6,7},{7,6},{8,9},{9,8},{10,11... | collective-permute-start | bytes 393224 | tf_op jit(solution)/shard_map/ppermute | solution.py:255
  18.5 0.0 collective-permute-done.5.refs_4_
  18.6 2.1 %collective-permute-start.14 = (bf16[16,32,128]{2,1,0:T(8,128)(2,1)S(1)}, bf16[16,32,128]{2,1,0:T(8,128)(2,1)S(1)}, u32[]{:S(2)}, u32[]{:S(2)}) collective-permute-start(bf16[16,32,128]{2,1,0:T(8,128)(2,1)S(1)} %collective-permute-done.8.refs_8_), channel_id=1, source_target_pairs={{0,12},{2,14},{4,8},{6,10},{8,4},{10,6},{12,0},{14,2},{16,28},{18,... | collective-permute-start | bytes 393224 | tf_op jit(solution)/shard_map/ppermute | solution.py:245
  20.7 0.0 collective-permute-done.3.refs_2_
  20.7 0.8 %collective-permute-start.12 = (bf16[16,32,128]{2,1,0:T(8,128)(2,1)S(1)}, bf16[16,32,128]{2,1,0:T(8,128)(2,1)S(1)}, u32[]{:S(2)}, u32[]{:S(2)}) collective-permute-start(bf16[16,32,128]{2,1,0:T(8,128)(2,1)S(1)} %collective-permute-done.8.refs_8_), channel_id=1, source_target_pairs={{0,8},{2,10},{4,12},{6,14},{8,0},{10,2},{12,4},{14,6},{16,24},{18,... | collective-permute-start | bytes 393224 | tf_op jit(solution)/shard_map/ppermute | solution.py:245
  21.5 0.0 collective-permute-done.1.refs_6_
  21.5 0.6 %collective-permute-start.10 = (bf16[16,32,128]{2,1,0:T(8,128)(2,1)S(1)}, bf16[16,32,128]{2,1,0:T(8,128)(2,1)S(1)}, u32[]{:S(2)}, u32[]{:S(2)}) collective-permute-start(bf16[16,32,128]{2,1,0:T(8,128)(2,1)S(1)} %collective-permute-done.8.refs_8_), channel_id=1, source_target_pairs={{0,4},{2,6},{4,0},{6,2},{8,12},{10,14},{12,8},{14,10},{16,20},{18,... | collective-permute-start | bytes 393224 | tf_op jit(solution)/shard_map/ppermute | solution.py:245
  22.1 0.0 collective-permute-done.refs_1_
  22.1 0.0 collective-permute-start.9
  22.1 0.1 collective-permute-done.16.refs_16_
  22.1 0.4 %collective-permute-start.6 = (bf16[16,32,128]{2,1,0:T(8,128)(2,1)S(1)}, bf16[16,32,128]{2,1,0:T(8,128)(2,1)S(1)}, u32[]{:S(2)}, u32[]{:S(2)}) collective-permute-start(bf16[16,32,128]{2,1,0:T(8,128)(2,1)S(1)} %collective-permute-done.5.refs_4_), channel_id=1, source_target_pairs={{0,2},{2,0},{4,6},{6,4},{8,10},{10,8},{12,14},{14,12},{16,18},{18,... | collective-permute-start | bytes 393224 | tf_op jit(solution)/shard_map/ppermute | solution.py:245
  22.6 2.7 %collective-permute-done.14.refs_14_ = bf16[16,32,128]{2,1,0:T(8,128)(2,1)S(1)} collective-permute-done((bf16[16,32,128]{2,1,0:T(8,128)(2,1)S(1)}, bf16[16,32,128]{2,1,0:T(8,128)(2,1)S(1)}, u32[]{:S(2)}, u32[]{:S(2)}) %collective-permute-start.14) | collective-permute-done | bytes 131104 | tf_op jit(solution)/shard_map/ppermute | solution.py:245
  25.3 0.0 collective-permute-start.4
  25.3 1.2 %collective-permute-done.12.refs_12_ = bf16[16,32,128]{2,1,0:T(8,128)(2,1)S(1)} collective-permute-done((bf16[16,32,128]{2,1,0:T(8,128)(2,1)S(1)}, bf16[16,32,128]{2,1,0:T(8,128)(2,1)S(1)}, u32[]{:S(2)}, u32[]{:S(2)}) %collective-permute-start.12) | collective-permute-done | bytes 131104 | tf_op jit(solution)/shard_map/ppermute | solution.py:245
  26.5 0.0 collective-permute-start.2
  26.5 0.6 %collective-permute-done.10.refs_10_ = bf16[16,32,128]{2,1,0:T(8,128)(2,1)S(1)} collective-permute-done((bf16[16,32,128]{2,1,0:T(8,128)(2,1)S(1)}, bf16[16,32,128]{2,1,0:T(8,128)(2,1)S(1)}, u32[]{:S(2)}, u32[]{:S(2)}) %collective-permute-start.10) | collective-permute-done | bytes 131104 | tf_op jit(solution)/shard_map/ppermute | solution.py:245
  27.0 0.0 collective-permute-start.7
  27.0 0.0 collective-permute-done.9.refs_9_
  27.0 0.5 %collective-permute-start.15 = (bf16[16,32,128]{2,1,0:T(8,128)(2,1)S(1)}, bf16[16,32,128]{2,1,0:T(8,128)(2,1)S(1)}, u32[]{:S(2)}, u32[]{:S(2)}) collective-permute-start(bf16[16,32,128]{2,1,0:T(8,128)(2,1)S(1)} %collective-permute-done.14.refs_14_), channel_id=1, source_target_pairs={{0,2},{2,0},{4,6},{6,4},{8,10},{10,8},{12,14},{14,12},{16,18},{18,... | collective-permute-start | bytes 393224 | tf_op jit(solution)/shard_map/ppermute | solution.py:245
  27.6 0.0 collective-permute-done.6.refs_5_
  27.6 0.1 collective-permute-start.13
  27.6 0.0 collective-permute-done.4.refs_3_
  27.6 0.4 %collective-permute-start.11 = (bf16[16,32,128]{2,1,0:T(8,128)(2,1)S(1)}, bf16[16,32,128]{2,1,0:T(8,128)(2,1)S(1)}, u32[]{:S(2)}, u32[]{:S(2)}) collective-permute-start(bf16[16,32,128]{2,1,0:T(8,128)(2,1)S(1)} %collective-permute-done.10.refs_10_), channel_id=1, source_target_pairs={{0,2},{2,0},{4,6},{6,4},{8,10},{10,8},{12,14},{14,12},{16,18},{18,... | collective-permute-start | bytes 393224 | tf_op jit(solution)/shard_map/ppermute | solution.py:245
  28.1 0.3 %collective-permute-done.7.refs_7_ = bf16[16,32,128]{2,1,0:T(8,128)(2,1)S(1)} collective-permute-done((bf16[16,32,128]{2,1,0:T(8,128)(2,1)S(1)}, bf16[16,32,128]{2,1,0:T(8,128)(2,1)S(1)}, u32[]{:S(2)}, u32[]{:S(2)}) %collective-permute-start.7) | collective-permute-done | bytes 131104 | tf_op jit(solution)/shard_map/ppermute | solution.py:245
  28.4 0.0 collective-permute-done.2.refs_0_
  28.4 0.2 collective-permute-done.15.refs_15_
  28.6 0.3 %collective-permute-done.13.refs_13_ = bf16[16,32,128]{2,1,0:T(8,128)(2,1)S(1)} collective-permute-done((bf16[16,32,128]{2,1,0:T(8,128)(2,1)S(1)}, bf16[16,32,128]{2,1,0:T(8,128)(2,1)S(1)}, u32[]{:S(2)}, u32[]{:S(2)}) %collective-permute-start.13) | collective-permute-done | bytes 131104 | tf_op jit(solution)/shard_map/ppermute | solution.py:245
  28.9 0.2 collective-permute-done.11.refs_11_
  29.1 2.0 %correlate.1 = bf16[16,2,256,128]{3,2,1,0:T(8,128)(2,1)} custom-call(bf16[16,32,128]{2,1,0:T(8,128)(2,1)S(1)} %collective-permute-done.2.refs_0_, bf16[16,32,128]{2,1,0:T(8,128)(2,1)S(1)} %collective-permute-done.refs_1_, bf16[16,32,128]{2,1,0:T(8,128)(2,1)S(1)} %collective-permute-done.3.refs_2_, bf16[16,32,128]{2,1,0:T(8,128)(2,1)S(1)} %collective-permute-done.4.refs_3_, ...), custom_call_target="tpu_custom_call" | custom-call | tf_op jit(solution)/shard_map/correlate/pallas_call | solution.py:308
Async XLA Ops:
  6.2 10.7 %collective-permute-start.8 = (bf16[16,32,128]{2,1,0:T(8,128)(2,1)}, bf16[16,32,128]{2,1,0:T(8,128)(2,1)S(1)}, u32[]{:S(2)}, u32[]{:S(2)}) collective-permute-start(bf16[16,32,128]{2,1,0:T(8,128)(2,1)} %channelise.1), channel_id=1, source_target_pairs={{0,16},{2,18},{4,20},{6,22},{8,24},{10,26},{12,28},{14,30},{16,0},... | collective-permute-start | bytes 393224 | tf_op jit(solution)/shard_map/ppermute | solution.py:245
  10.4 8.2 %collective-permute-start.5 = (bf16[16,32,128]{2,1,0:T(8,128)(2,1)}, bf16[16,32,128]{2,1,0:T(8,128)(2,1)S(1)}, u32[]{:S(2)}, u32[]{:S(2)}) collective-permute-start(bf16[16,32,128]{2,1,0:T(8,128)(2,1)} %channelise.1), channel_id=1, source_target_pairs={{0,8},{2,10},{4,12},{6,14},{8,0},{10,2},{12,4},{14,6},{16,24},{18,... | collective-permute-start | bytes 393224 | tf_op jit(solution)/shard_map/ppermute | solution.py:245
  11.9 8.8 %collective-permute-start.3 = (bf16[16,32,128]{2,1,0:T(8,128)(2,1)}, bf16[16,32,128]{2,1,0:T(8,128)(2,1)S(1)}, u32[]{:S(2)}, u32[]{:S(2)}) collective-permute-start(bf16[16,32,128]{2,1,0:T(8,128)(2,1)} %channelise.1), channel_id=1, source_target_pairs={{0,4},{2,6},{4,0},{6,2},{8,12},{10,14},{12,8},{14,10},{16,20},{18,... | collective-permute-start | bytes 393224 | tf_op jit(solution)/shard_map/ppermute | solution.py:245
  13.4 8.1 %collective-permute-start.1 = (bf16[16,32,128]{2,1,0:T(8,128)(2,1)}, bf16[16,32,128]{2,1,0:T(8,128)(2,1)S(1)}, u32[]{:S(2)}, u32[]{:S(2)}) collective-permute-start(bf16[16,32,128]{2,1,0:T(8,128)(2,1)} %channelise.1), channel_id=1, source_target_pairs={{0,12},{2,14},{4,8},{6,10},{8,4},{10,6},{12,0},{14,2},{16,28},{18,... | collective-permute-start | bytes 393224 | tf_op jit(solution)/shard_map/ppermute | solution.py:245
  13.8 8.2 %collective-permute-start = (bf16[16,32,128]{2,1,0:T(8,128)(2,1)}, bf16[16,32,128]{2,1,0:T(8,128)(2,1)S(1)}, u32[]{:S(2)}, u32[]{:S(2)}) collective-permute-start(bf16[16,32,128]{2,1,0:T(8,128)(2,1)} %channelise.1), channel_id=1, source_target_pairs={{0,2},{2,0},{4,6},{6,4},{8,10},{10,8},{12,14},{14,12},{16,18},{18,... | collective-permute-start | bytes 393224 | tf_op jit(solution)/shard_map/ppermute | solution.py:245
  17.0 5.2 %collective-permute-start.16 = (bf16[16,32,128]{2,1,0:T(8,128)(2,1)}, bf16[16,32,128]{2,1,0:T(8,128)(2,1)S(1)}, u32[]{:S(2)}, u32[]{:S(2)}) collective-permute-start(bf16[16,32,128]{2,1,0:T(8,128)(2,1)} %channelise.1), channel_id=1, source_target_pairs={{0,1},{1,0},{2,3},{3,2},{4,5},{5,4},{6,7},{7,6},{8,9},{9,8},{10,11... | collective-permute-start | bytes 393224 | tf_op jit(solution)/shard_map/ppermute | solution.py:255
  18.6 6.7 %collective-permute-start.14 = (bf16[16,32,128]{2,1,0:T(8,128)(2,1)S(1)}, bf16[16,32,128]{2,1,0:T(8,128)(2,1)S(1)}, u32[]{:S(2)}, u32[]{:S(2)}) collective-permute-start(bf16[16,32,128]{2,1,0:T(8,128)(2,1)S(1)} %collective-permute-done.8.refs_8_), channel_id=1, source_target_pairs={{0,12},{2,14},{4,8},{6,10},{8,4},{10,6},{12,0},{14,2},{16,28},{18,... | collective-permute-start | bytes 393224 | tf_op jit(solution)/shard_map/ppermute | solution.py:245
  20.7 5.8 %collective-permute-start.12 = (bf16[16,32,128]{2,1,0:T(8,128)(2,1)S(1)}, bf16[16,32,128]{2,1,0:T(8,128)(2,1)S(1)}, u32[]{:S(2)}, u32[]{:S(2)}) collective-permute-start(bf16[16,32,128]{2,1,0:T(8,128)(2,1)S(1)} %collective-permute-done.8.refs_8_), channel_id=1, source_target_pairs={{0,8},{2,10},{4,12},{6,14},{8,0},{10,2},{12,4},{14,6},{16,24},{18,... | collective-permute-start | bytes 393224 | tf_op jit(solution)/shard_map/ppermute | solution.py:245
  21.5 5.5 %collective-permute-start.10 = (bf16[16,32,128]{2,1,0:T(8,128)(2,1)S(1)}, bf16[16,32,128]{2,1,0:T(8,128)(2,1)S(1)}, u32[]{:S(2)}, u32[]{:S(2)}) collective-permute-start(bf16[16,32,128]{2,1,0:T(8,128)(2,1)S(1)} %collective-permute-done.8.refs_8_), channel_id=1, source_target_pairs={{0,4},{2,6},{4,0},{6,2},{8,12},{10,14},{12,8},{14,10},{16,20},{18,... | collective-permute-start | bytes 393224 | tf_op jit(solution)/shard_map/ppermute | solution.py:245
  22.1 5.0 %collective-permute-start.9 = (bf16[16,32,128]{2,1,0:T(8,128)(2,1)S(1)}, bf16[16,32,128]{2,1,0:T(8,128)(2,1)S(1)}, u32[]{:S(2)}, u32[]{:S(2)}) collective-permute-start(bf16[16,32,128]{2,1,0:T(8,128)(2,1)S(1)} %collective-permute-done.8.refs_8_), channel_id=1, source_target_pairs={{0,2},{2,0},{4,6},{6,4},{8,10},{10,8},{12,14},{14,12},{16,18},{18,... | collective-permute-start | bytes 393224 | tf_op jit(solution)/shard_map/ppermute | solution.py:245
  22.1 5.4 %collective-permute-start.6 = (bf16[16,32,128]{2,1,0:T(8,128)(2,1)S(1)}, bf16[16,32,128]{2,1,0:T(8,128)(2,1)S(1)}, u32[]{:S(2)}, u32[]{:S(2)}) collective-permute-start(bf16[16,32,128]{2,1,0:T(8,128)(2,1)S(1)} %collective-permute-done.5.refs_4_), channel_id=1, source_target_pairs={{0,2},{2,0},{4,6},{6,4},{8,10},{10,8},{12,14},{14,12},{16,18},{18,... | collective-permute-start | bytes 393224 | tf_op jit(solution)/shard_map/ppermute | solution.py:245
  25.3 2.4 %collective-permute-start.4 = (bf16[16,32,128]{2,1,0:T(8,128)(2,1)S(1)}, bf16[16,32,128]{2,1,0:T(8,128)(2,1)S(1)}, u32[]{:S(2)}, u32[]{:S(2)}) collective-permute-start(bf16[16,32,128]{2,1,0:T(8,128)(2,1)S(1)} %collective-permute-done.3.refs_2_), channel_id=1, source_target_pairs={{0,2},{2,0},{4,6},{6,4},{8,10},{10,8},{12,14},{14,12},{16,18},{18,... | collective-permute-start | bytes 393224 | tf_op jit(solution)/shard_map/ppermute | solution.py:245
  26.5 1.9 %collective-permute-start.2 = (bf16[16,32,128]{2,1,0:T(8,128)(2,1)S(1)}, bf16[16,32,128]{2,1,0:T(8,128)(2,1)S(1)}, u32[]{:S(2)}, u32[]{:S(2)}) collective-permute-start(bf16[16,32,128]{2,1,0:T(8,128)(2,1)S(1)} %collective-permute-done.refs_1_), channel_id=1, source_target_pairs={{0,2},{2,0},{4,6},{6,4},{8,10},{10,8},{12,14},{14,12},{16,18},{18,... | collective-permute-start | bytes 393224 | tf_op jit(solution)/shard_map/ppermute | solution.py:245
  27.0 1.3 %collective-permute-start.7 = (bf16[16,32,128]{2,1,0:T(8,128)(2,1)S(1)}, bf16[16,32,128]{2,1,0:T(8,128)(2,1)S(1)}, u32[]{:S(2)}, u32[]{:S(2)}) collective-permute-start(bf16[16,32,128]{2,1,0:T(8,128)(2,1)S(1)} %collective-permute-done.1.refs_6_), channel_id=1, source_target_pairs={{0,2},{2,0},{4,6},{6,4},{8,10},{10,8},{12,14},{14,12},{16,18},{18,... | collective-permute-start | bytes 393224 | tf_op jit(solution)/shard_map/ppermute | solution.py:245
  27.0 1.5 %collective-permute-start.15 = (bf16[16,32,128]{2,1,0:T(8,128)(2,1)S(1)}, bf16[16,32,128]{2,1,0:T(8,128)(2,1)S(1)}, u32[]{:S(2)}, u32[]{:S(2)}) collective-permute-start(bf16[16,32,128]{2,1,0:T(8,128)(2,1)S(1)} %collective-permute-done.14.refs_14_), channel_id=1, source_target_pairs={{0,2},{2,0},{4,6},{6,4},{8,10},{10,8},{12,14},{14,12},{16,18},{18,... | collective-permute-start | bytes 393224 | tf_op jit(solution)/shard_map/ppermute | solution.py:245
  27.6 1.3 %collective-permute-start.13 = (bf16[16,32,128]{2,1,0:T(8,128)(2,1)S(1)}, bf16[16,32,128]{2,1,0:T(8,128)(2,1)S(1)}, u32[]{:S(2)}, u32[]{:S(2)}) collective-permute-start(bf16[16,32,128]{2,1,0:T(8,128)(2,1)S(1)} %collective-permute-done.12.refs_12_), channel_id=1, source_target_pairs={{0,2},{2,0},{4,6},{6,4},{8,10},{10,8},{12,14},{14,12},{16,18},{18,... | collective-permute-start | bytes 393224 | tf_op jit(solution)/shard_map/ppermute | solution.py:245
  27.6 1.5 %collective-permute-start.11 = (bf16[16,32,128]{2,1,0:T(8,128)(2,1)S(1)}, bf16[16,32,128]{2,1,0:T(8,128)(2,1)S(1)}, u32[]{:S(2)}, u32[]{:S(2)}) collective-permute-start(bf16[16,32,128]{2,1,0:T(8,128)(2,1)S(1)} %collective-permute-done.10.refs_10_), channel_id=1, source_target_pairs={{0,2},{2,0},{4,6},{6,4},{8,10},{10,8},{12,14},{14,12},{16,18},{18,... | collective-permute-start | bytes 393224 | tf_op jit(solution)/shard_map/ppermute | solution.py:245

commit v7 on v6

--- a/solution.py
+++ b/solution.py
@@ -122,9 +122,9 @@
             get_map.start()
             get_flags.start()
 
-    first_half = lax.broadcasted_iota(jnp.int32, (8, 8, CHUNK), 1) < Q_DEV
+    first_half = lax.broadcasted_iota(jnp.int32, (16, 8, CHUNK), 1) < Q_DEV
     real_lanes = lax.broadcasted_iota(jnp.int32, (CH_DEV, 2 * SPECTRA), 1) < SPECTRA
-    lane_group = lax.broadcasted_iota(jnp.int32, (64, CHUNK), 1) // 32
+    lane_group = lax.broadcasted_iota(jnp.int32, (128, CHUNK), 1) // 32
 
     def pair(low, high):
         upper = first_half[: low.shape[0]]
@@ -133,7 +133,7 @@
         return straight + pltpu.roll(crossed, 4, 1)
 
     def frames_of(p, i, kept):
-        spans = [(64 * i, 64), (256 + 64 * i, 64 if i < 3 else 96)]
+        spans = [(128 * i, 128), (256 + 128 * i, 128 if i < 1 else 160)]
         block = jnp.concatenate(
             [
                 jnp.concatenate([held.at[p, j].reshape(68 * 8, CHUNK)[at : at + size] for at, size in spans], axis=0)
@@ -143,23 +143,23 @@
         )
         both = jnp.dot(block, table_v[...], preferred_element_type=jnp.float32)
         both = both.reshape(-1, 8, 2 * CHUNK)
-        frames[p % 2, 8 * i : 8 * i + 8] = pair(both[:8], both[8:16])
+        frames[p % 2, 16 * i : 16 * i + 16] = pair(both[:16], both[16:32])
         if i == 0:
-            return both[8:11]
-        if i == 3:
-            frames[p % 2, 32:35] = pair(kept, both[16:19])
+            kept = both[16:19]
+        if i == 1:
+            frames[p % 2, 32:35] = pair(kept, both[32:35])
         return kept
 
     def taps_of(p, i):
         total = None
         for tap in range(TAPS):
-            term = frames[p % 2, 8 * i + tap : 8 * i + tap + 8]
+            term = frames[p % 2, 16 * i + tap : 16 * i + tap + 16]
             turn = 32 * (p % 4 - tap) % CHUNK
             if turn:
                 term = pltpu.roll(term, turn, 2)
             total = term if total is None else total + term
-        total = total.reshape(64, CHUNK)
-        at = slice(64 * i, 64 * i + 64)
+        total = total.reshape(128, CHUNK)
+        at = slice(128 * i, 128 * i + 128)
         sums[p // 4, at] = total if p % 4 == 0 else jnp.where(lane_group == p % 4, total, sums[p // 4, at])
 
     def finish(first):
@@ -191,13 +191,13 @@
             get_map.wait()
             get_flags.wait()
         kept = None
-        for i in range(4):
+        for i in range(2):
             kept = frames_of(p, i, kept)
             if p > 0:
                 taps_of(p - 1, i)
         if p == 5:
             finish(0)
-    for i in range(4):
+    for i in range(2):
         taps_of(P_DEV - 1, i)
     finish(4)
     for p in range(P_DEV):

time: 31.3 us -> 31.1 us (level)
  no operation moved by 1% of the time
where the time goes in v7:
time: 31.1 us; the launch traced here: 30.9 us
  starting transfers between devices  14.1 us (45%)
  waiting for transfers between devices  8.74 us (28%)
  Pallas kernels  8.08 us (26%)
    ppermute x16, starting transfers between devices, swap(): return lax.ppermute(block, 'row', [(i, i ^ d) for i in range(ROWS)])  12.5 us
    ppermute x16, waiting for transfers between devices, swap(): return lax.ppermute(block, 'row', [(i, i ^ d) for i in range(ROWS)])  8.63 us
    pallas_call x1, Pallas kernels, channelise(): pl.pallas_call(filter_kernel, out_shape=jax.ShapeDtypeStruct((CH_DEV, LAN...  6.06 us
    pallas_call x1, Pallas kernels, correlate(): pl.pallas_call(correlate_kernel, out_shape=jax.ShapeDtypeStruct((CH_DEV,...  2.02 us
    ppermute x1, starting transfers between devices, gather(): other = lax.ppermute(late, 'col', [(0, 1), (1, 0)])  1.57 us
  transfers between devices with their start and end apart: 17, of which 9 were waited for; matrix products, arithmetic and copies ran while one was open for 0% of the time, Pallas kernels for 0%

profile of v7, /device:TPU:0, one launch (start us, length us, event | category | flops | bytes accessed | tf_op | source)
XLA Modules:
  0.0 30.9 jit_solution(11299917603827802354)
XLA Ops:
  0.0 6.1 %channelise.1 = bf16[16,32,128]{2,1,0:T(8,128)(2,1)} custom-call(bf16[8,67,8,8,128]{4,3,2,1,0:T(8,128)(2,1)} %bitcast.8, bf16[1024,256]{1,0:T(8,128)(2,1)} %constant.2.clone.table, s32[1,32]{1,0:T(1,128)} %bitcast.10, s32[4,8]{1,0:T(4,128)} %bitcast.9), custom_call_target="tpu_custom_call" | custom-call | tf_op jit(solution)/shard_map/channelise/pallas_call | solution.py:216
  6.1 4.1 %collective-permute-start.8 = (bf16[16,32,128]{2,1,0:T(8,128)(2,1)}, bf16[16,32,128]{2,1,0:T(8,128)(2,1)S(1)}, u32[]{:S(2)}, u32[]{:S(2)}) collective-permute-start(bf16[16,32,128]{2,1,0:T(8,128)(2,1)} %channelise.1), channel_id=1, source_target_pairs={{0,16},{2,18},{4,20},{6,22},{8,24},{10,26},{12,28},{14,30},{16,0},... | collective-permute-start | bytes 393224 | tf_op jit(solution)/shard_map/ppermute | solution.py:245
  10.2 1.6 %collective-permute-start.5 = (bf16[16,32,128]{2,1,0:T(8,128)(2,1)}, bf16[16,32,128]{2,1,0:T(8,128)(2,1)S(1)}, u32[]{:S(2)}, u32[]{:S(2)}) collective-permute-start(bf16[16,32,128]{2,1,0:T(8,128)(2,1)} %channelise.1), channel_id=1, source_target_pairs={{0,8},{2,10},{4,12},{6,14},{8,0},{10,2},{12,4},{14,6},{16,24},{18,... | collective-permute-start | bytes 393224 | tf_op jit(solution)/shard_map/ppermute | solution.py:245
  11.8 1.5 %collective-permute-start.3 = (bf16[16,32,128]{2,1,0:T(8,128)(2,1)}, bf16[16,32,128]{2,1,0:T(8,128)(2,1)S(1)}, u32[]{:S(2)}, u32[]{:S(2)}) collective-permute-start(bf16[16,32,128]{2,1,0:T(8,128)(2,1)} %channelise.1), channel_id=1, source_target_pairs={{0,4},{2,6},{4,0},{6,2},{8,12},{10,14},{12,8},{14,10},{16,20},{18,... | collective-permute-start | bytes 393224 | tf_op jit(solution)/shard_map/ppermute | solution.py:245
  13.2 0.4 %collective-permute-start.1 = (bf16[16,32,128]{2,1,0:T(8,128)(2,1)}, bf16[16,32,128]{2,1,0:T(8,128)(2,1)S(1)}, u32[]{:S(2)}, u32[]{:S(2)}) collective-permute-start(bf16[16,32,128]{2,1,0:T(8,128)(2,1)} %channelise.1), channel_id=1, source_target_pairs={{0,12},{2,14},{4,8},{6,10},{8,4},{10,6},{12,0},{14,2},{16,28},{18,... | collective-permute-start | bytes 393224 | tf_op jit(solution)/shard_map/ppermute | solution.py:245
  13.7 0.0 collective-permute-start
  13.7 3.1 %collective-permute-done.8.refs_8_ = bf16[16,32,128]{2,1,0:T(8,128)(2,1)S(1)} collective-permute-done((bf16[16,32,128]{2,1,0:T(8,128)(2,1)}, bf16[16,32,128]{2,1,0:T(8,128)(2,1)S(1)}, u32[]{:S(2)}, u32[]{:S(2)}) %collective-permute-start.8) | collective-permute-done | bytes 131104 | tf_op jit(solution)/shard_map/ppermute | solution.py:245
  16.8 1.6 %collective-permute-start.16 = (bf16[16,32,128]{2,1,0:T(8,128)(2,1)}, bf16[16,32,128]{2,1,0:T(8,128)(2,1)S(1)}, u32[]{:S(2)}, u32[]{:S(2)}) collective-permute-start(bf16[16,32,128]{2,1,0:T(8,128)(2,1)} %channelise.1), channel_id=1, source_target_pairs={{0,1},{1,0},{2,3},{3,2},{4,5},{5,4},{6,7},{7,6},{8,9},{9,8},{10,11... | collective-permute-start | bytes 393224 | tf_op jit(solution)/shard_map/ppermute | solution.py:255
  18.4 0.0 collective-permute-done.5.refs_4_
  18.4 2.2 %collective-permute-start.14 = (bf16[16,32,128]{2,1,0:T(8,128)(2,1)S(1)}, bf16[16,32,128]{2,1,0:T(8,128)(2,1)S(1)}, u32[]{:S(2)}, u32[]{:S(2)}) collective-permute-start(bf16[16,32,128]{2,1,0:T(8,128)(2,1)S(1)} %collective-permute-done.8.refs_8_), channel_id=1, source_target_pairs={{0,12},{2,14},{4,8},{6,10},{8,4},{10,6},{12,0},{14,2},{16,28},{18,... | collective-permute-start | bytes 393224 | tf_op jit(solution)/shard_map/ppermute | solution.py:245
  20.5 0.0 collective-permute-done.3.refs_2_
  20.5 0.8 %collective-permute-start.12 = (bf16[16,32,128]{2,1,0:T(8,128)(2,1)S(1)}, bf16[16,32,128]{2,1,0:T(8,128)(2,1)S(1)}, u32[]{:S(2)}, u32[]{:S(2)}) collective-permute-start(bf16[16,32,128]{2,1,0:T(8,128)(2,1)S(1)} %collective-permute-done.8.refs_8_), channel_id=1, source_target_pairs={{0,8},{2,10},{4,12},{6,14},{8,0},{10,2},{12,4},{14,6},{16,24},{18,... | collective-permute-start | bytes 393224 | tf_op jit(solution)/shard_map/ppermute | solution.py:245
  21.3 0.0 collective-permute-done.1.refs_6_
  21.3 0.5 %collective-permute-start.10 = (bf16[16,32,128]{2,1,0:T(8,128)(2,1)S(1)}, bf16[16,32,128]{2,1,0:T(8,128)(2,1)S(1)}, u32[]{:S(2)}, u32[]{:S(2)}) collective-permute-start(bf16[16,32,128]{2,1,0:T(8,128)(2,1)S(1)} %collective-permute-done.8.refs_8_), channel_id=1, source_target_pairs={{0,4},{2,6},{4,0},{6,2},{8,12},{10,14},{12,8},{14,10},{16,20},{18,... | collective-permute-start | bytes 393224 | tf_op jit(solution)/shard_map/ppermute | solution.py:245
  21.9 0.0 collective-permute-done.refs_1_
  21.9 0.0 collective-permute-start.9
  21.9 0.1 collective-permute-done.16.refs_16_
  22.0 0.4 %collective-permute-start.6 = (bf16[16,32,128]{2,1,0:T(8,128)(2,1)S(1)}, bf16[16,32,128]{2,1,0:T(8,128)(2,1)S(1)}, u32[]{:S(2)}, u32[]{:S(2)}) collective-permute-start(bf16[16,32,128]{2,1,0:T(8,128)(2,1)S(1)} %collective-permute-done.5.refs_4_), channel_id=1, source_target_pairs={{0,2},{2,0},{4,6},{6,4},{8,10},{10,8},{12,14},{14,12},{16,18},{18,... | collective-permute-start | bytes 393224 | tf_op jit(solution)/shard_map/ppermute | solution.py:245
  22.4 2.7 %collective-permute-done.14.refs_14_ = bf16[16,32,128]{2,1,0:T(8,128)(2,1)S(1)} collective-permute-done((bf16[16,32,128]{2,1,0:T(8,128)(2,1)S(1)}, bf16[16,32,128]{2,1,0:T(8,128)(2,1)S(1)}, u32[]{:S(2)}, u32[]{:S(2)}) %collective-permute-start.14) | collective-permute-done | bytes 131104 | tf_op jit(solution)/shard_map/ppermute | solution.py:245
  25.1 0.0 collective-permute-start.4
  25.1 1.2 %collective-permute-done.12.refs_12_ = bf16[16,32,128]{2,1,0:T(8,128)(2,1)S(1)} collective-permute-done((bf16[16,32,128]{2,1,0:T(8,128)(2,1)S(1)}, bf16[16,32,128]{2,1,0:T(8,128)(2,1)S(1)}, u32[]{:S(2)}, u32[]{:S(2)}) %collective-permute-start.12) | collective-permute-done | bytes 131104 | tf_op jit(solution)/shard_map/ppermute | solution.py:245
  26.3 0.0 collective-permute-start.2
  26.3 0.6 %collective-permute-done.10.refs_10_ = bf16[16,32,128]{2,1,0:T(8,128)(2,1)S(1)} collective-permute-done((bf16[16,32,128]{2,1,0:T(8,128)(2,1)S(1)}, bf16[16,32,128]{2,1,0:T(8,128)(2,1)S(1)}, u32[]{:S(2)}, u32[]{:S(2)}) %collective-permute-start.10) | collective-permute-done | bytes 131104 | tf_op jit(solution)/shard_map/ppermute | solution.py:245
  26.9 0.0 collective-permute-start.7
  26.9 0.0 collective-permute-done.9.refs_9_
  26.9 0.5 %collective-permute-start.15 = (bf16[16,32,128]{2,1,0:T(8,128)(2,1)S(1)}, bf16[16,32,128]{2,1,0:T(8,128)(2,1)S(1)}, u32[]{:S(2)}, u32[]{:S(2)}) collective-permute-start(bf16[16,32,128]{2,1,0:T(8,128)(2,1)S(1)} %collective-permute-done.14.refs_14_), channel_id=1, source_target_pairs={{0,2},{2,0},{4,6},{6,4},{8,10},{10,8},{12,14},{14,12},{16,18},{18,... | collective-permute-start | bytes 393224 | tf_op jit(solution)/shard_map/ppermute | solution.py:245
  27.4 0.0 collective-permute-done.6.refs_5_
  27.4 0.1 collective-permute-start.13
  27.4 0.0 collective-permute-done.4.refs_3_
  27.4 0.4 %collective-permute-start.11 = (bf16[16,32,128]{2,1,0:T(8,128)(2,1)S(1)}, bf16[16,32,128]{2,1,0:T(8,128)(2,1)S(1)}, u32[]{:S(2)}, u32[]{:S(2)}) collective-permute-start(bf16[16,32,128]{2,1,0:T(8,128)(2,1)S(1)} %collective-permute-done.10.refs_10_), channel_id=1, source_target_pairs={{0,2},{2,0},{4,6},{6,4},{8,10},{10,8},{12,14},{14,12},{16,18},{18,... | collective-permute-start | bytes 393224 | tf_op jit(solution)/shard_map/ppermute | solution.py:245
  27.9 0.3 %collective-permute-done.7.refs_7_ = bf16[16,32,128]{2,1,0:T(8,128)(2,1)S(1)} collective-permute-done((bf16[16,32,128]{2,1,0:T(8,128)(2,1)S(1)}, bf16[16,32,128]{2,1,0:T(8,128)(2,1)S(1)}, u32[]{:S(2)}, u32[]{:S(2)}) %collective-permute-start.7) | collective-permute-done | bytes 131104 | tf_op jit(solution)/shard_map/ppermute | solution.py:245
  28.2 0.0 collective-permute-done.2.refs_0_
  28.2 0.2 collective-permute-done.15.refs_15_
  28.4 0.3 %collective-permute-done.13.refs_13_ = bf16[16,32,128]{2,1,0:T(8,128)(2,1)S(1)} collective-permute-done((bf16[16,32,128]{2,1,0:T(8,128)(2,1)S(1)}, bf16[16,32,128]{2,1,0:T(8,128)(2,1)S(1)}, u32[]{:S(2)}, u32[]{:S(2)}) %collective-permute-start.13) | collective-permute-done | bytes 131104 | tf_op jit(solution)/shard_map/ppermute | solution.py:245
  28.7 0.2 collective-permute-done.11.refs_11_
  28.9 2.0 %correlate.1 = bf16[16,2,256,128]{3,2,1,0:T(8,128)(2,1)} custom-call(bf16[16,32,128]{2,1,0:T(8,128)(2,1)S(1)} %collective-permute-done.2.refs_0_, bf16[16,32,128]{2,1,0:T(8,128)(2,1)S(1)} %collective-permute-done.refs_1_, bf16[16,32,128]{2,1,0:T(8,128)(2,1)S(1)} %collective-permute-done.3.refs_2_, bf16[16,32,128]{2,1,0:T(8,128)(2,1)S(1)} %collective-permute-done.4.refs_3_, ...), custom_call_target="tpu_custom_call" | custom-call | tf_op jit(solution)/shard_map/correlate/pallas_call | solution.py:308
Async XLA Ops:
  6.1 10.7 %collective-permute-start.8 = (bf16[16,32,128]{2,1,0:T(8,128)(2,1)}, bf16[16,32,128]{2,1,0:T(8,128)(2,1)S(1)}, u32[]{:S(2)}, u32[]{:S(2)}) collective-permute-start(bf16[16,32,128]{2,1,0:T(8,128)(2,1)} %channelise.1), channel_id=1, source_target_pairs={{0,16},{2,18},{4,20},{6,22},{8,24},{10,26},{12,28},{14,30},{16,0},... | collective-permute-start | bytes 393224 | tf_op jit(solution)/shard_map/ppermute | solution.py:245
  10.2 8.2 %collective-permute-start.5 = (bf16[16,32,128]{2,1,0:T(8,128)(2,1)}, bf16[16,32,128]{2,1,0:T(8,128)(2,1)S(1)}, u32[]{:S(2)}, u32[]{:S(2)}) collective-permute-start(bf16[16,32,128]{2,1,0:T(8,128)(2,1)} %channelise.1), channel_id=1, source_target_pairs={{0,8},{2,10},{4,12},{6,14},{8,0},{10,2},{12,4},{14,6},{16,24},{18,... | collective-permute-start | bytes 393224 | tf_op jit(solution)/shard_map/ppermute | solution.py:245
  11.8 8.8 %collective-permute-start.3 = (bf16[16,32,128]{2,1,0:T(8,128)(2,1)}, bf16[16,32,128]{2,1,0:T(8,128)(2,1)S(1)}, u32[]{:S(2)}, u32[]{:S(2)}) collective-permute-start(bf16[16,32,128]{2,1,0:T(8,128)(2,1)} %channelise.1), channel_id=1, source_target_pairs={{0,4},{2,6},{4,0},{6,2},{8,12},{10,14},{12,8},{14,10},{16,20},{18,... | collective-permute-start | bytes 393224 | tf_op jit(solution)/shard_map/ppermute | solution.py:245
  13.2 8.1 %collective-permute-start.1 = (bf16[16,32,128]{2,1,0:T(8,128)(2,1)}, bf16[16,32,128]{2,1,0:T(8,128)(2,1)S(1)}, u32[]{:S(2)}, u32[]{:S(2)}) collective-permute-start(bf16[16,32,128]{2,1,0:T(8,128)(2,1)} %channelise.1), channel_id=1, source_target_pairs={{0,12},{2,14},{4,8},{6,10},{8,4},{10,6},{12,0},{14,2},{16,28},{18,... | collective-permute-start | bytes 393224 | tf_op jit(solution)/shard_map/ppermute | solution.py:245
  13.7 8.2 %collective-permute-start = (bf16[16,32,128]{2,1,0:T(8,128)(2,1)}, bf16[16,32,128]{2,1,0:T(8,128)(2,1)S(1)}, u32[]{:S(2)}, u32[]{:S(2)}) collective-permute-start(bf16[16,32,128]{2,1,0:T(8,128)(2,1)} %channelise.1), channel_id=1, source_target_pairs={{0,2},{2,0},{4,6},{6,4},{8,10},{10,8},{12,14},{14,12},{16,18},{18,... | collective-permute-start | bytes 393224 | tf_op jit(solution)/shard_map/ppermute | solution.py:245
  16.8 5.2 %collective-permute-start.16 = (bf16[16,32,128]{2,1,0:T(8,128)(2,1)}, bf16[16,32,128]{2,1,0:T(8,128)(2,1)S(1)}, u32[]{:S(2)}, u32[]{:S(2)}) collective-permute-start(bf16[16,32,128]{2,1,0:T(8,128)(2,1)} %channelise.1), channel_id=1, source_target_pairs={{0,1},{1,0},{2,3},{3,2},{4,5},{5,4},{6,7},{7,6},{8,9},{9,8},{10,11... | collective-permute-start | bytes 393224 | tf_op jit(solution)/shard_map/ppermute | solution.py:255
  18.4 6.7 %collective-permute-start.14 = (bf16[16,32,128]{2,1,0:T(8,128)(2,1)S(1)}, bf16[16,32,128]{2,1,0:T(8,128)(2,1)S(1)}, u32[]{:S(2)}, u32[]{:S(2)}) collective-permute-start(bf16[16,32,128]{2,1,0:T(8,128)(2,1)S(1)} %collective-permute-done.8.refs_8_), channel_id=1, source_target_pairs={{0,12},{2,14},{4,8},{6,10},{8,4},{10,6},{12,0},{14,2},{16,28},{18,... | collective-permute-start | bytes 393224 | tf_op jit(solution)/shard_map/ppermute | solution.py:245
  20.5 5.8 %collective-permute-start.12 = (bf16[16,32,128]{2,1,0:T(8,128)(2,1)S(1)}, bf16[16,32,128]{2,1,0:T(8,128)(2,1)S(1)}, u32[]{:S(2)}, u32[]{:S(2)}) collective-permute-start(bf16[16,32,128]{2,1,0:T(8,128)(2,1)S(1)} %collective-permute-done.8.refs_8_), channel_id=1, source_target_pairs={{0,8},{2,10},{4,12},{6,14},{8,0},{10,2},{12,4},{14,6},{16,24},{18,... | collective-permute-start | bytes 393224 | tf_op jit(solution)/shard_map/ppermute | solution.py:245
  21.3 5.5 %collective-permute-start.10 = (bf16[16,32,128]{2,1,0:T(8,128)(2,1)S(1)}, bf16[16,32,128]{2,1,0:T(8,128)(2,1)S(1)}, u32[]{:S(2)}, u32[]{:S(2)}) collective-permute-start(bf16[16,32,128]{2,1,0:T(8,128)(2,1)S(1)} %collective-permute-done.8.refs_8_), channel_id=1, source_target_pairs={{0,4},{2,6},{4,0},{6,2},{8,12},{10,14},{12,8},{14,10},{16,20},{18,... | collective-permute-start | bytes 393224 | tf_op jit(solution)/shard_map/ppermute | solution.py:245
  21.9 5.0 %collective-permute-start.9 = (bf16[16,32,128]{2,1,0:T(8,128)(2,1)S(1)}, bf16[16,32,128]{2,1,0:T(8,128)(2,1)S(1)}, u32[]{:S(2)}, u32[]{:S(2)}) collective-permute-start(bf16[16,32,128]{2,1,0:T(8,128)(2,1)S(1)} %collective-permute-done.8.refs_8_), channel_id=1, source_target_pairs={{0,2},{2,0},{4,6},{6,4},{8,10},{10,8},{12,14},{14,12},{16,18},{18,... | collective-permute-start | bytes 393224 | tf_op jit(solution)/shard_map/ppermute | solution.py:245
  22.0 5.4 %collective-permute-start.6 = (bf16[16,32,128]{2,1,0:T(8,128)(2,1)S(1)}, bf16[16,32,128]{2,1,0:T(8,128)(2,1)S(1)}, u32[]{:S(2)}, u32[]{:S(2)}) collective-permute-start(bf16[16,32,128]{2,1,0:T(8,128)(2,1)S(1)} %collective-permute-done.5.refs_4_), channel_id=1, source_target_pairs={{0,2},{2,0},{4,6},{6,4},{8,10},{10,8},{12,14},{14,12},{16,18},{18,... | collective-permute-start | bytes 393224 | tf_op jit(solution)/shard_map/ppermute | solution.py:245
  25.1 2.3 %collective-permute-start.4 = (bf16[16,32,128]{2,1,0:T(8,128)(2,1)S(1)}, bf16[16,32,128]{2,1,0:T(8,128)(2,1)S(1)}, u32[]{:S(2)}, u32[]{:S(2)}) collective-permute-start(bf16[16,32,128]{2,1,0:T(8,128)(2,1)S(1)} %collective-permute-done.3.refs_2_), channel_id=1, source_target_pairs={{0,2},{2,0},{4,6},{6,4},{8,10},{10,8},{12,14},{14,12},{16,18},{18,... | collective-permute-start | bytes 393224 | tf_op jit(solution)/shard_map/ppermute | solution.py:245
  26.3 1.9 %collective-permute-start.2 = (bf16[16,32,128]{2,1,0:T(8,128)(2,1)S(1)}, bf16[16,32,128]{2,1,0:T(8,128)(2,1)S(1)}, u32[]{:S(2)}, u32[]{:S(2)}) collective-permute-start(bf16[16,32,128]{2,1,0:T(8,128)(2,1)S(1)} %collective-permute-done.refs_1_), channel_id=1, source_target_pairs={{0,2},{2,0},{4,6},{6,4},{8,10},{10,8},{12,14},{14,12},{16,18},{18,... | collective-permute-start | bytes 393224 | tf_op jit(solution)/shard_map/ppermute | solution.py:245
  26.9 1.3 %collective-permute-start.7 = (bf16[16,32,128]{2,1,0:T(8,128)(2,1)S(1)}, bf16[16,32,128]{2,1,0:T(8,128)(2,1)S(1)}, u32[]{:S(2)}, u32[]{:S(2)}) collective-permute-start(bf16[16,32,128]{2,1,0:T(8,128)(2,1)S(1)} %collective-permute-done.1.refs_6_), channel_id=1, source_target_pairs={{0,2},{2,0},{4,6},{6,4},{8,10},{10,8},{12,14},{14,12},{16,18},{18,... | collective-permute-start | bytes 393224 | tf_op jit(solution)/shard_map/ppermute | solution.py:245
  26.9 1.5 %collective-permute-start.15 = (bf16[16,32,128]{2,1,0:T(8,128)(2,1)S(1)}, bf16[16,32,128]{2,1,0:T(8,128)(2,1)S(1)}, u32[]{:S(2)}, u32[]{:S(2)}) collective-permute-start(bf16[16,32,128]{2,1,0:T(8,128)(2,1)S(1)} %collective-permute-done.14.refs_14_), channel_id=1, source_target_pairs={{0,2},{2,0},{4,6},{6,4},{8,10},{10,8},{12,14},{14,12},{16,18},{18,... | collective-permute-start | bytes 393224 | tf_op jit(solution)/shard_map/ppermute | solution.py:245
  27.4 1.3 %collective-permute-start.13 = (bf16[16,32,128]{2,1,0:T(8,128)(2,1)S(1)}, bf16[16,32,128]{2,1,0:T(8,128)(2,1)S(1)}, u32[]{:S(2)}, u32[]{:S(2)}) collective-permute-start(bf16[16,32,128]{2,1,0:T(8,128)(2,1)S(1)} %collective-permute-done.12.refs_12_), channel_id=1, source_target_pairs={{0,2},{2,0},{4,6},{6,4},{8,10},{10,8},{12,14},{14,12},{16,18},{18,... | collective-permute-start | bytes 393224 | tf_op jit(solution)/shard_map/ppermute | solution.py:245
  27.4 1.5 %collective-permute-start.11 = (bf16[16,32,128]{2,1,0:T(8,128)(2,1)S(1)}, bf16[16,32,128]{2,1,0:T(8,128)(2,1)S(1)}, u32[]{:S(2)}, u32[]{:S(2)}) collective-permute-start(bf16[16,32,128]{2,1,0:T(8,128)(2,1)S(1)} %collective-permute-done.10.refs_10_), channel_id=1, source_target_pairs={{0,2},{2,0},{4,6},{6,4},{8,10},{10,8},{12,14},{14,12},{16,18},{18,... | collective-permute-start | bytes 393224 | tf_op jit(solution)/shard_map/ppermute | solution.py:245
